TPU v7x, 32 devices: a whole 2x2x4 slice. The times are simulated.
32 devices in a mesh: fsdp: 8 (over z, core), ctx: 4 (over y, x).
Axes of the slice: x: 2, y: 2, z: 4, core: 2. Of those that a mesh axis runs over, the one named last changes fastest.
Arguments:
- tokens: bfloat16 [8192, 2048], P(('fsdp', 'ctx')), may hold values from -6 to 6
- positions: int32 [8192], P(('fsdp', 'ctx')), may hold values from 0 to 1023, as said below
- gain_attn: bfloat16 [2048], P('fsdp'), may hold values from 0.25 to 1.75
- gain_mlp: bfloat16 [2048], P('fsdp'), may hold values from 0.25 to 1.75
- w_query: bfloat16 [2048, 2048], P('fsdp'), may hold values from -0.25 to 0.25
- w_key: bfloat16 [2048, 256], P('fsdp'), may hold values from -0.25 to 0.25
- w_value: bfloat16 [2048, 256], P('fsdp'), may hold values from -0.125 to 0.125
- w_out: bfloat16 [2048, 2048], P('fsdp'), may hold values from -1 to 1
- w_gate: bfloat16 [2048, 5632], P('fsdp'), may hold values from -0.125 to 0.125
- w_up: bfloat16 [2048, 5632], P('fsdp'), may hold values from -0.125 to 0.125
- w_down: bfloat16 [5632, 2048], P('fsdp'), may hold values from -0.15625 to 0.15625
- cotangent: bfloat16 [8192, 2048], P(('fsdp', 'ctx')), may hold values from -6 to 6
Outputs:
- output: bfloat16 [8192, 2048], P(('fsdp', 'ctx'))
- grad_tokens: float32 [8192, 2048], P(('fsdp', 'ctx'))
- grad_gain_attn: float32 [2048], P('fsdp')
- grad_gain_mlp: float32 [2048], P('fsdp')
- grad_query: float32 [2048, 2048], P('fsdp')
- grad_key: float32 [2048, 256], P('fsdp')
- grad_value: float32 [2048, 256], P('fsdp')
- grad_out: float32 [2048, 2048], P('fsdp')
- grad_gate: float32 [2048, 5632], P('fsdp')
- grad_up: float32 [2048, 5632], P('fsdp')
- grad_down: float32 [5632, 2048], P('fsdp')
Inputs may be any that keep to these rules, and one draw needn't show every extreme that they name: positions count from 0 at a document's first token and rise by one per token within it; the first token of every sequence of 1024 has position 0; one sequence, drawn from the seed, is a single document of all 1024 tokens.
All inputs are finite; a program needn't handle non-finite values.
Results may differ from a plain program's by a relative error of at most 0.024.
Values may be sent and summed in bfloat16 or wider, within the bound.
A program may use at most 384 MiB of HBM per device.

v0:
```python
import math

import jax
import jax.numpy as jnp
from jax import lax
from jax.sharding import PartitionSpec as P

HEADS = 32
KV_HEADS = 4
HEAD_DIM = 64


eps_norm = 1e-05
theta_base = 10000.0
neg_large = -1e30


def rms_forward(values_in, gain_row):
    inverse = lax.rsqrt(jnp.mean(values_in * values_in, axis=-1, keepdims=True) + eps_norm)
    return (values_in * inverse * gain_row, inverse)


def rms_backward(values_in, inverse, gain_row, incoming):
    gain_term = jnp.sum(incoming * values_in * inverse, axis=0)
    inner_mean = jnp.mean(incoming * gain_row * values_in, axis=-1, keepdims=True)
    grad_values = (
        gain_row * inverse * incoming - values_in * inverse * inverse * inverse * inner_mean
    )
    return (grad_values, gain_term)


def rope_tables(positions):
    half_width = HEAD_DIM // 2
    frequency = theta_base ** (-(jnp.arange(half_width, dtype=jnp.float32) * 2.0) / HEAD_DIM)
    angles = positions.astype(jnp.float32)[:, None] * frequency[None, :]
    return (jnp.cos(angles)[:, None, :], jnp.sin(angles)[:, None, :])


def rotate(field, cosine, sine_table, direction):
    half_width = field.shape[-1] // 2
    first_half = field[..., :half_width]
    second_half = field[..., half_width:]
    return jnp.concatenate(
        [
            first_half * cosine - direction * second_half * sine_table,
            second_half * cosine + direction * first_half * sine_table,
        ],
        axis=-1,
    )


def per_device(
    tokens,
    positions,
    gain_attn,
    gain_mlp,
    w_query,
    w_key,
    w_value,
    w_out,
    w_gate,
    w_up,
    w_down,
    cotangent,
):
    tok_rows = tokens.shape[0]
    query_width = HEADS * HEAD_DIM
    key_width = KV_HEADS * HEAD_DIM
    group_size = HEADS // KV_HEADS
    score_scale = HEAD_DIM ** (-0.5)
    seq_length = tok_rows * lax.axis_size("ctx")
    query_index = lax.axis_index("ctx") * tok_rows + jnp.arange(tok_rows, dtype=jnp.int32)
    doc_begin = query_index - positions
    cosine, sine_table = rope_tables(positions)
    inputs = tokens.astype(jnp.float32)

    def visible(key_start, key_rows):
        key_index = key_start + jnp.arange(key_rows, dtype=jnp.int32)
        return (key_index[None, :] <= query_index[:, None]) & (
            key_index[None, :] >= doc_begin[:, None]
        )

    gathered = (
        lax.all_gather(gain_attn, "fsdp", axis=0, tiled=True),
        lax.all_gather(gain_mlp, "fsdp", axis=0, tiled=True),
        lax.all_gather(w_query, "fsdp", axis=0, tiled=True),
        lax.all_gather(w_key, "fsdp", axis=0, tiled=True),
        lax.all_gather(w_value, "fsdp", axis=0, tiled=True),
        lax.all_gather(w_out, "fsdp", axis=0, tiled=True),
    )
    gain_one = gathered[0].astype(jnp.float32)
    gain_two = gathered[1].astype(jnp.float32)
    query_full, key_full, value_full, out_full = (
        gathered[2],
        gathered[3],
        gathered[4],
        gathered[5],
    )
    normed_one, inverse_one = rms_forward(inputs, gain_one)
    normed_low = normed_one.astype(jnp.bfloat16)
    pre_query = jnp.dot(normed_low, query_full, preferred_element_type=jnp.float32)
    pre_key = jnp.dot(normed_low, key_full, preferred_element_type=jnp.float32)
    values_low = jnp.dot(normed_low, value_full, preferred_element_type=jnp.float32).astype(
        jnp.bfloat16
    )
    values_low = values_low.reshape(tok_rows, KV_HEADS, HEAD_DIM)
    queries = rotate(pre_query.reshape(tok_rows, HEADS, HEAD_DIM), cosine, sine_table, 1.0).astype(
        jnp.bfloat16
    )
    keys_low = rotate(
        pre_key.reshape(tok_rows, KV_HEADS, HEAD_DIM), cosine, sine_table, 1.0
    ).astype(jnp.bfloat16)
    query_groups = queries.reshape(tok_rows, KV_HEADS, group_size, HEAD_DIM)

    def attend_block(running, key_block, value_block, block_start):
        top_run, total_run, sum_run = running
        allowed = visible(block_start, key_block.shape[0])[:, None, None, :]
        scores = (
            jnp.einsum(
                "qkgd,lkd->qkgl", query_groups, key_block, preferred_element_type=jnp.float32
            )
            * score_scale
        )
        scores = jnp.where(allowed, scores, neg_large)
        top_new = jnp.maximum(top_run, jnp.max(scores, axis=-1))
        weights = jnp.where(allowed, jnp.exp(scores - top_new[..., None]), 0.0)
        factor = jnp.exp(top_run - top_new)
        total_new = total_run * factor + jnp.sum(weights, axis=-1)
        sum_new = sum_run * factor[..., None] + jnp.einsum(
            "qkgl,lkd->qkgd",
            weights.astype(jnp.bfloat16),
            value_block,
            preferred_element_type=jnp.float32,
        )
        return (top_new, total_new, sum_new)

    start_state = (
        jnp.full((tok_rows, KV_HEADS, group_size), neg_large, jnp.float32),
        jnp.zeros((tok_rows, KV_HEADS, group_size), jnp.float32),
        jnp.zeros((tok_rows, KV_HEADS, group_size, HEAD_DIM), jnp.float32),
    )
    key_piece = lax.all_gather(keys_low, "ctx", axis=0, tiled=True)
    value_piece = lax.all_gather(values_low, "ctx", axis=0, tiled=True)
    piece_rows = key_piece.shape[0]
    sub_rows = math.gcd(piece_rows, 512)
    blocks = piece_rows // sub_rows
    key_blocks = key_piece.reshape(blocks, sub_rows, KV_HEADS, HEAD_DIM)
    value_blocks = value_piece.reshape(blocks, sub_rows, KV_HEADS, HEAD_DIM)
    offsets = jnp.arange(blocks, dtype=jnp.int32) * sub_rows

    def scan_step(inner_carry, block_items):
        return (attend_block(inner_carry, block_items[0], block_items[1], block_items[2]), None)

    result, unused_out = lax.scan(scan_step, start_state, (key_blocks, value_blocks, offsets))
    top_final, total_final, sum_final = result
    attended = sum_final / total_final[..., None]
    log_total = top_final + jnp.log(total_final)
    attended_low = attended.reshape(tok_rows, query_width).astype(jnp.bfloat16)
    middle = inputs + jnp.dot(attended_low, out_full, preferred_element_type=jnp.float32)
    normed_two, inverse_two = rms_forward(middle, gain_two)
    normed_two_low = normed_two.astype(jnp.bfloat16)
    columns = normed_two_low
    gate_pre = jnp.dot(
        columns,
        lax.all_gather(w_gate, "fsdp", axis=0, tiled=True),
        preferred_element_type=jnp.float32,
    )
    up_pre = jnp.dot(
        columns,
        lax.all_gather(w_up, "fsdp", axis=0, tiled=True),
        preferred_element_type=jnp.float32,
    )
    hidden_low = (jax.nn.silu(gate_pre) * up_pre).astype(jnp.bfloat16)
    columns = hidden_low
    mlp_branch = jnp.dot(
        columns,
        lax.all_gather(w_down, "fsdp", axis=0, tiled=True),
        preferred_element_type=jnp.float32,
    )
    output = (middle + mlp_branch).astype(jnp.bfloat16)
    gate_full, up_full, down_full = (
        lax.all_gather(w_gate, "fsdp", axis=0, tiled=True),
        lax.all_gather(w_up, "fsdp", axis=0, tiled=True),
        lax.all_gather(w_down, "fsdp", axis=0, tiled=True),
    )
    query_full, key_full, value_full, out_full = (
        lax.all_gather(w_query, "fsdp", axis=0, tiled=True),
        lax.all_gather(w_key, "fsdp", axis=0, tiled=True),
        lax.all_gather(w_value, "fsdp", axis=0, tiled=True),
        lax.all_gather(w_out, "fsdp", axis=0, tiled=True),
    )
    grad_hidden = jnp.einsum("td,fd->tf", cotangent, down_full, preferred_element_type=jnp.float32)
    sigmoid_gate = jax.nn.sigmoid(gate_pre)
    grad_gate_low = (
        grad_hidden * up_pre * sigmoid_gate * (1.0 + gate_pre * (1.0 - sigmoid_gate))
    ).astype(jnp.bfloat16)
    grad_up_low = (grad_hidden * gate_pre * sigmoid_gate).astype(jnp.bfloat16)
    grad_normed_two = jnp.einsum(
        "tf,df->td", grad_gate_low, gate_full, preferred_element_type=jnp.float32
    ) + jnp.einsum("tf,df->td", grad_up_low, up_full, preferred_element_type=jnp.float32)
    grad_from_two, gain_two_term = rms_backward(middle, inverse_two, gain_two, grad_normed_two)
    grad_middle = cotangent.astype(jnp.float32) + grad_from_two
    grad_middle_low = grad_middle.astype(jnp.bfloat16)
    grad_attended_low = jnp.einsum(
        "td,qd->tq", grad_middle_low, out_full, preferred_element_type=jnp.float32
    ).astype(jnp.bfloat16)
    grad_att_groups = grad_attended_low.reshape(tok_rows, KV_HEADS, group_size, HEAD_DIM)
    delta_rows = jnp.sum(grad_att_groups.astype(jnp.float32) * attended, axis=-1)
    keys_all, values_all = (
        lax.all_gather(keys_low, "ctx", axis=0, tiled=True),
        lax.all_gather(values_low, "ctx", axis=0, tiled=True),
    )
    key_step = min(512, seq_length)
    key_count = seq_length // key_step
    key_blocks = keys_all.reshape(key_count, key_step, KV_HEADS, HEAD_DIM)
    value_blocks = values_all.reshape(key_count, key_step, KV_HEADS, HEAD_DIM)
    block_starts = jnp.arange(key_count, dtype=jnp.int32) * key_step

    def back_step(grad_query_run, block_items):
        key_block, value_block, block_start = block_items
        allowed = visible(block_start, key_step)[:, None, None, :]
        scores = (
            jnp.einsum(
                "qkgd,lkd->qkgl", query_groups, key_block, preferred_element_type=jnp.float32
            )
            * score_scale
        )
        probs = jnp.exp(jnp.where(allowed, scores - log_total[..., None], neg_large))
        grad_probs = jnp.einsum(
            "qkgd,lkd->qkgl", grad_att_groups, value_block, preferred_element_type=jnp.float32
        )
        grad_scores_low = (probs * (grad_probs - delta_rows[..., None])).astype(jnp.bfloat16)
        grad_query_run = grad_query_run + jnp.einsum(
            "qkgl,lkd->qkgd", grad_scores_low, key_block, preferred_element_type=jnp.float32
        )
        grad_key_block = (
            jnp.einsum(
                "qkgl,qkgd->lkd", grad_scores_low, query_groups, preferred_element_type=jnp.float32
            )
            * score_scale
        )
        grad_value_block = jnp.einsum(
            "qkgl,qkgd->lkd",
            probs.astype(jnp.bfloat16),
            grad_att_groups,
            preferred_element_type=jnp.float32,
        )
        return (grad_query_run, (grad_key_block, grad_value_block))

    grad_query_acc, key_terms = lax.scan(
        back_step,
        jnp.zeros((tok_rows, KV_HEADS, group_size, HEAD_DIM), jnp.float32),
        (key_blocks, value_blocks, block_starts),
    )
    grad_key_terms = key_terms[0].reshape(seq_length, KV_HEADS, HEAD_DIM)
    grad_value_terms = key_terms[1].reshape(seq_length, KV_HEADS, HEAD_DIM)
    grad_key_mine, grad_value_mine = (
        lax.psum_scatter(
            grad_key_terms.astype(jnp.bfloat16), "ctx", scatter_dimension=0, tiled=True
        ).astype(jnp.float32),
        lax.psum_scatter(
            grad_value_terms.astype(jnp.bfloat16), "ctx", scatter_dimension=0, tiled=True
        ).astype(jnp.float32),
    )
    grad_query_heads = (grad_query_acc * score_scale).reshape(tok_rows, HEADS, HEAD_DIM)
    grad_pre_query = (
        rotate(grad_query_heads, cosine, sine_table, -1.0)
        .reshape(tok_rows, query_width)
        .astype(jnp.bfloat16)
    )
    grad_pre_key = (
        rotate(grad_key_mine, cosine, sine_table, -1.0)
        .reshape(tok_rows, key_width)
        .astype(jnp.bfloat16)
    )
    grad_values_low = grad_value_mine.reshape(tok_rows, key_width).astype(jnp.bfloat16)
    grad_normed_one = (
        jnp.einsum("tq,dq->td", grad_pre_query, query_full, preferred_element_type=jnp.float32)
        + jnp.einsum("tq,dq->td", grad_pre_key, key_full, preferred_element_type=jnp.float32)
        + jnp.einsum("tq,dq->td", grad_values_low, value_full, preferred_element_type=jnp.float32)
    )
    grad_from_one, gain_one_term = rms_backward(inputs, inverse_one, gain_one, grad_normed_one)
    grad_tokens = grad_middle + grad_from_one
    attn_terms = (
        gain_one_term,
        gain_two_term,
        jnp.einsum("td,tq->dq", normed_low, grad_pre_query, preferred_element_type=jnp.float32),
        jnp.einsum("td,tq->dq", normed_low, grad_pre_key, preferred_element_type=jnp.float32),
        jnp.einsum("td,tq->dq", normed_low, grad_values_low, preferred_element_type=jnp.float32),
        jnp.einsum("tq,td->qd", attended_low, grad_middle_low, preferred_element_type=jnp.float32),
    )
    scattered = (
        lax.psum_scatter(
            attn_terms[0].astype(jnp.bfloat16), "fsdp", scatter_dimension=0, tiled=True
        ).astype(jnp.float32),
        lax.psum_scatter(
            attn_terms[1].astype(jnp.bfloat16), "fsdp", scatter_dimension=0, tiled=True
        ).astype(jnp.float32),
        lax.psum_scatter(
            attn_terms[2].astype(jnp.bfloat16), "fsdp", scatter_dimension=0, tiled=True
        ).astype(jnp.float32),
        lax.psum_scatter(
            attn_terms[3].astype(jnp.bfloat16), "fsdp", scatter_dimension=0, tiled=True
        ).astype(jnp.float32),
        lax.psum_scatter(
            attn_terms[4].astype(jnp.bfloat16), "fsdp", scatter_dimension=0, tiled=True
        ).astype(jnp.float32),
        lax.psum_scatter(
            attn_terms[5].astype(jnp.bfloat16), "fsdp", scatter_dimension=0, tiled=True
        ).astype(jnp.float32),
    )
    gate_up_low = jnp.concatenate([grad_gate_low, grad_up_low], axis=1)
    columns = normed_two_low
    gate_up_sum = lax.psum_scatter(
        jnp.einsum("tc,tf->cf", columns, gate_up_low, preferred_element_type=jnp.float32).astype(
            jnp.bfloat16
        ),
        "fsdp",
        scatter_dimension=0,
        tiled=True,
    )
    columns = hidden_low
    down_sum = lax.psum_scatter(
        jnp.einsum("tc,td->cd", columns, cotangent, preferred_element_type=jnp.float32).astype(
            jnp.bfloat16
        ),
        "fsdp",
        scatter_dimension=0,
        tiled=True,
    )
    totals = (
        lax.psum(scattered[0].astype(jnp.bfloat16), "ctx").astype(jnp.float32),
        lax.psum(scattered[1].astype(jnp.bfloat16), "ctx").astype(jnp.float32),
        lax.psum(scattered[2].astype(jnp.bfloat16), "ctx").astype(jnp.float32),
        lax.psum(scattered[3].astype(jnp.bfloat16), "ctx").astype(jnp.float32),
        lax.psum(scattered[4].astype(jnp.bfloat16), "ctx").astype(jnp.float32),
        lax.psum(scattered[5].astype(jnp.bfloat16), "ctx").astype(jnp.float32),
        lax.psum(gate_up_sum, "ctx").astype(jnp.float32),
        lax.psum(down_sum, "ctx").astype(jnp.float32),
    )
    gate_up_part = totals[6]
    down_part = totals[7]
    ff_width = w_gate.shape[1]
    return (
        output,
        grad_tokens,
        totals[0],
        totals[1],
        totals[2],
        totals[3],
        totals[4],
        totals[5],
        gate_up_part[:, :ff_width],
        gate_up_part[:, ff_width:],
        down_part,
    )


def solution(mesh):
    return jax.shard_map(
        per_device,
        mesh=mesh,
        in_specs=(
            P(("fsdp", "ctx"), None),
            P(("fsdp", "ctx")),
            P("fsdp"),
            P("fsdp"),
            P("fsdp", None),
            P("fsdp", None),
            P("fsdp", None),
            P("fsdp", None),
            P("fsdp", None),
            P("fsdp", None),
            P("fsdp", None),
            P(("fsdp", "ctx"), None),
        ),
        out_specs=(
            P(("fsdp", "ctx"), None),
            P(("fsdp", "ctx"), None),
            P("fsdp"),
            P("fsdp"),
            P("fsdp", None),
            P("fsdp", None),
            P("fsdp", None),
            P("fsdp", None),
            P("fsdp", None),
            P("fsdp", None),
            P("fsdp", None),
        ),
        check_vma=False,
    )
```

profile of v0, /device:TPU:8, one launch (start us, length us, event | category | flops | bytes accessed | tf_op | source)
XLA Modules:
  0.0 2184.6 jit_solution(17897738325891800169)
XLA Ops:
  12.1 9.1 all-gather
  21.2 11.9 all-gather.1
  36.2 14.5 all_gather.44
  58.3 14.4 all_gather.47
  73.5 63.4 %all-gather.12.cloned.1.call-done = bf16[2048,2048]{1,0:T(8,128)(2,1)} async-done(((bf16[256,2048]{1,0:T(8,128)(2,1)}), bf16[2048,2048]{1,0:T(8,128)(2,1)}) %all-gather.12.cloned.1.call-update) | async-done | bytes 8388624 | tf_op jit(solution)/shard_map/all_gather | solution.py:86
  144.2 51.5 %while.30 = (s32[]{:T(128)}, f32[256,4,8]{0,2,1:T(8,128)S(1)}, f32[256,4,8]{0,2,1:T(8,128)S(1)}, f32[256,4,8,64]{0,3,2,1:T(8,128)}, s32[2]{0:T(128)S(1)}, /*inde...) while((s32[]{:T(128)}, f32[256,4,8]{0,2,1:T(8,128)S(1)}, ...), condition=%wide.region_4.5_spmd.clone, body=%wide.region_1.4_spmd.clone.sunk | while | flops 1130275584 | bytes 126360792 | solution.py:154
  178.4 8.6 fusion.150
  198.5 20.5 all-gather.16.cloned.1.call-done
  226.7 194.6 %all-gather.18.cloned.1.call-done = bf16[2048,5632]{1,0:T(8,128)(2,1)} async-done(((bf16[256,5632]{1,0:T(8,128)(2,1)}), bf16[2048,5632]{1,0:T(8,128)(2,1)}) %all-gather.18.cloned.1.call-update) | async-done | bytes 23068688 | tf_op jit(solution)/shard_map/all_gather | solution.py:165
  421.4 13.7 fusion.81
  435.1 188.7 %all-gather.20.cloned.1.call-done = bf16[2048,5632]{1,0:T(8,128)(2,1)} async-done(((bf16[256,5632]{1,0:T(8,128)(2,1)}), bf16[2048,5632]{1,0:T(8,128)(2,1)}) %all-gather.20.cloned.1.call-update) | async-done | bytes 23068688 | tf_op jit(solution)/shard_map/all_gather | solution.py:170
  623.8 12.6 fusion.82
  636.3 190.0 %all-gather.22.cloned.1.call-done = bf16[5632,2048]{1,0:T(8,128)(2,1)} async-done(((bf16[704,2048]{1,0:T(8,128)(2,1)}), bf16[5632,2048]{1,0:T(8,128)(2,1)}) %all-gather.22.cloned.1.call-update) | async-done | bytes 23068688 | tf_op jit(solution)/shard_map/all_gather | solution.py:177
  826.3 26.2 %multiply_convert_fusion = (bf16[256,5632]{1,0:T(8,128)(2,1)}, bf16[256,5632]{1,0:T(8,128)(2,1)}, bf16[256,5632]{1,0:T(8,128)(2,1)}) fusion(f32[256,5632]{1,0:T(8,128)} %fusion.81, f32[256,5632]{1,0:T(8,128)} %fusion.82, bf16[256,2048]{1,0:T(8,128)(2,1)S(1)} %copy-done.12, bf16[5632,2048]{1,0:T(8,128)(2,1)} %all-gather.22.cloned.1.call-done), kind=kOutput, calls=%fused_computation.66 | convolution fusion | flops 5928648704 | bytes 44302336 | tf_op jit(solution)/shard_map/td,fd->tf/dot_general | solution.py:192
  852.4 12.5 fusion.83
  865.0 14.5 multiply_reduce_fusion
  894.7 69.2 %while.31 = (s32[]{:T(128)}, f32[256,4,8,64]{0,3,2,1:T(8,128)}, bf16[2,512,4,64]{1,3,2,0:T(8,128)(2,1)}, bf16[2,512,4,64]{1,3,2,0:T(8,128)(2,1)}, bf16[2,512,4,6...) while((s32[]{:T(128)}, f32[256,4,8,64]{0,3,2,1:T(8,128)}, ...), condition=%wide.region_9.10_spmd.clone, body=%wide.region_8.9_spmd.clone.sunk | while | flops 2727871232 | bytes 191733136 | solution.py:250
  920.5 8.6 fusion.165
  955.3 8.6 fusion.165
  968.0 24.1 %reduce-scatter.11.cloned.1.call-done = bf16[256,4,64]{0,2,1:T(8,128)(2,1)} async-done(((bf16[1024,4,64]{0,2,1:T(8,128)(2,1)}), bf16[256,4,64]{0,2,1:T(8,128)(2,1)}) %reduce-scatter.11.cloned.1.call-update) | async-done | bytes 131088 | tf_op jit(solution)/shard_map/reduce_scatter | solution.py:258
  994.7 25.7 %reduce-scatter.13.cloned.1.call-done = bf16[256,4,64]{0,2,1:T(8,128)(2,1)} async-done(((bf16[1024,4,64]{0,2,1:T(8,128)(2,1)}), bf16[256,4,64]{0,2,1:T(8,128)(2,1)}) %reduce-scatter.13.cloned.1.call-update) | async-done | bytes 131088 | tf_op jit(solution)/shard_map/reduce_scatter | solution.py:261
  1039.1 12.6 convolution_convert_fusion.1
  1051.8 21.1 convolution_convert_fusion
  1073.3 11.9 reduce-scatter.19.cloned.1.call-done
  1085.3 91.1 %reduce-scatter.15.cloned.1.call-done = bf16[256,2048]{1,0:T(8,128)(2,1)} async-done(((bf16[2048,2048]{1,0:T(8,128)(2,1)}), bf16[256,2048]{1,0:T(8,128)(2,1)}) %reduce-scatter.15.cloned.1.call-update) | async-done | bytes 1048592 | tf_op jit(solution)/shard_map/reduce_scatter | solution.py:299
  1176.3 90.3 %reduce-scatter.21.cloned.1.call-done = bf16[256,2048]{1,0:T(8,128)(2,1)} async-done(((bf16[2048,2048]{1,0:T(8,128)(2,1)}), bf16[256,2048]{1,0:T(8,128)(2,1)}) %reduce-scatter.21.cloned.1.call-update) | async-done | bytes 1048592 | tf_op jit(solution)/shard_map/reduce_scatter | solution.py:308
  1266.6 228.0 %reduce-scatter.23.cloned.1.call-done = bf16[704,2048]{1,0:T(8,128)(2,1)} async-done(((bf16[5632,2048]{1,0:T(8,128)(2,1)}), bf16[704,2048]{1,0:T(8,128)(2,1)}) %reduce-scatter.23.cloned.1.call-update) | async-done | bytes 2883600 | tf_op jit(solution)/shard_map/reduce_scatter | solution.py:323
  1494.7 444.3 %reduce-scatter.25.cloned.1.call-done = bf16[256,11264]{1,0:T(8,128)(2,1)} async-done(((bf16[2048,11264]{1,0:T(8,128)(2,1)}), bf16[256,11264]{1,0:T(8,128)(2,1)}) %reduce-scatter.25.cloned.1.call-update) | async-done | bytes 5767184
  1947.2 13.3 fusion.55
  1963.9 13.1 all-reduce.3
  1977.3 10.5 all-reduce.4
  1992.7 169.8 %all-reduce.8.cloned.1.call-done = (bf16[256,2048]{1,0:T(8,128)(2,1)}, bf16[256,256]{1,0:T(8,128)(2,1)}, bf16[256,256]{1,0:T(8,128)(2,1)}, bf16[256,2048]{1,0:T(...) async-done(((bf16[256,2048]{1,0:T(8,128)(2,1)}, bf16[256,256]{1,0:T(8,128)(2,1)}, bf16[256,256]{1,0:T(8,128)(2,1)}, bf16[256,2048]{1,0:T(8,128)(2,1)}, ...) | async-done | bytes 11010064 | tf_op jit(solution)/shard_map/psum | solution.py:334
  (227 shorter events, 200.3 us)
Async XLA Ops:
  7.2 27.1 %all-gather.10.cloned.1.call-start = ((), (), s32[]{:S(2)}) async-start(), calls=%async_computation.8 | async-start | bytes 1179648 | tf_op jit(solution)/shard_map/all_gather | solution.py:87
  7.9 48.5 %all-gather.14.cloned.1.call-start = ((), (), s32[]{:S(2)}) async-start(), calls=%async_computation.10 | async-start | bytes 1179648 | tf_op jit(solution)/shard_map/all_gather | solution.py:88
  8.7 128.2 %all-gather.12.cloned.1.call-start = ((), (), s32[]{:S(2)}) async-start(), calls=%async_computation.9 | async-start | bytes 9437184 | tf_op jit(solution)/shard_map/all_gather | solution.py:86
  9.4 209.6 %all-gather.16.cloned.1.call-start = ((), (), s32[]{:S(2)}) async-start(), calls=%async_computation.11 | async-start | bytes 9437184 | tf_op jit(solution)/shard_map/all_gather | solution.py:89
  10.0 411.4 %all-gather.18.cloned.1.call-start = ((), (), s32[]{:S(2)}) async-start(), calls=%async_computation.12 | async-start | bytes 25952256 | tf_op jit(solution)/shard_map/all_gather | solution.py:165
  10.6 22.5 %copy-start.4 = (bf16[256,2048]{1,0:T(8,128)(2,1)S(1)}, bf16[256,2048]{1,0:T(8,128)(2,1)}, u32[]{:S(2)}) copy-start(bf16[256,2048]{1,0:T(8,128)(2,1)} %param.16) | copy-start | bytes 3145732
  10.6 22.8 %copy-start.35 = (s32[256]{0:T(256)S(1)}, s32[256]{0:T(256)}, u32[]{:S(2)}) copy-start(s32[256]{0:T(256)} %param.17) | copy-start | bytes 3076
  10.6 613.1 %all-gather.20.cloned.1.call-start = ((), (), s32[]{:S(2)}) async-start(), calls=%async_computation.13 | async-start | bytes 25952256 | tf_op jit(solution)/shard_map/all_gather | solution.py:170
  11.2 815.1 %all-gather.22.cloned.1.call-start = ((), (), s32[]{:S(2)}) async-start(), calls=%async_computation.14 | async-start | bytes 25952256 | tf_op jit(solution)/shard_map/all_gather | solution.py:177
  11.9 980.1 %reduce-scatter.11.cloned.1.call-start = ((), (), s32[]{:S(2)}) async-start(), calls=%async_computation.15 | async-start | bytes 655360 | tf_op jit(solution)/shard_map/reduce_scatter | solution.py:258
  21.1 115.8 %copy-start.26 = (f32[8,1,256]{2,1,0:T(1,128)}, f32[8,1,256]{2,1,0:T(1,128)S(1)}, u32[]{:S(2)}) copy-start(f32[8,1,256]{2,1,0:T(1,128)S(1)} %convert_element_type.192) | copy-start | bytes 24580
  33.4 103.5 %copy-start.32 = (f32[256]{0:T(256)}, f32[256]{0:T(256)S(1)}, u32[]{:S(2)}) copy-start(f32[256]{0:T(256)S(1)} %add_rsqrt_fusion.1) | copy-start | bytes 3076
  34.3 109.5 %copy-start.20 = (f32[256,32]{0,1:T(8,128)}, f32[256,32]{0,1:T(8,128)S(1)}, u32[]{:S(2)}) copy-start(f32[256,32]{0,1:T(8,128)S(1)} %get-tuple-element.359) | copy-start | bytes 98308
  145.9 16.1 copy-start.22
  171.0 15.9 copy-start.22
  226.7 194.6 %copy-start.13 = (bf16[256,2048]{1,0:T(8,128)(2,1)}, bf16[256,2048]{1,0:T(8,128)(2,1)S(1)}, u32[]{:S(2)}) copy-start(bf16[256,2048]{1,0:T(8,128)(2,1)S(1)} %multiply_convert_fusion.3) | copy-start | bytes 3145732
  435.1 391.2 %copy-start.12 = (bf16[256,2048]{1,0:T(8,128)(2,1)S(1)}, bf16[256,2048]{1,0:T(8,128)(2,1)}, u32[]{:S(2)}) copy-start(bf16[256,2048]{1,0:T(8,128)(2,1)} %param.27) | copy-start | bytes 3145732
  963.9 29.1 %copy-start.21 = (f32[256,32]{0,1:T(8,128)S(1)}, f32[256,32]{0,1:T(8,128)}, u32[]{:S(2)}) copy-start(f32[256,32]{0,1:T(8,128)} %copy-done.20) | copy-start | bytes 98308
  963.9 29.1 %copy-start.25 = (f32[256,32]{0,1:T(8,128)S(1)}, f32[256,32]{0,1:T(8,128)}, u32[]{:S(2)}) copy-start(f32[256,32]{0,1:T(8,128)} %get-tuple-element.357) | copy-start | bytes 98308
  963.9 29.2 %copy-start.5 = (bf16[256,2048]{1,0:T(8,128)(2,1)S(1)}, bf16[256,2048]{1,0:T(8,128)(2,1)}, u32[]{:S(2)}) copy-start(bf16[256,2048]{1,0:T(8,128)(2,1)} %param.16) | copy-start | bytes 3145732
  963.9 29.2 %copy-start.27 = (f32[8,1,256]{2,1,0:T(1,128)S(1)}, f32[8,1,256]{2,1,0:T(1,128)}, u32[]{:S(2)}) copy-start(f32[8,1,256]{2,1,0:T(1,128)} %copy-done.26) | copy-start | bytes 24580
  963.9 29.2 %copy-start.33 = (f32[256]{0:T(256)S(1)}, f32[256]{0:T(256)}, u32[]{:S(2)}) copy-start(f32[256]{0:T(256)} %copy-done.32) | copy-start | bytes 3076
  965.9 54.5 %reduce-scatter.13.cloned.1.call-start = ((), (), s32[]{:S(2)}) async-start(), calls=%async_computation.16 | async-start | bytes 655360 | tf_op jit(solution)/shard_map/reduce_scatter | solution.py:261
  967.9 105.4 %reduce-scatter.17.cloned.1.call-start = ((), (), s32[]{:S(2)}) async-start(), calls=%async_computation.18 | async-start | bytes 1179648 | tf_op jit(solution)/shard_map/reduce_scatter | solution.py:302
  994.7 28.6 %copy-start.3 = (f32[256,4,8,64]{0,3,2,1:T(8,128)S(1)}, f32[256,4,8,64]{0,3,2,1:T(8,128)}, u32[]{:S(2)}) copy-start(f32[256,4,8,64]{0,3,2,1:T(8,128)} %get-tuple-element.137) | copy-start | bytes 6291460
  994.7 90.6 %reduce-scatter.19.cloned.1.call-start = ((), (), s32[]{:S(2)}) async-start(), calls=%async_computation.19 | async-start | bytes 1179648 | tf_op jit(solution)/shard_map/reduce_scatter | solution.py:305
  1023.0 153.3 %reduce-scatter.15.cloned.1.call-start = ((), (), s32[]{:S(2)}) async-start(), calls=%async_computation.17 | async-start | bytes 9437184 | tf_op jit(solution)/shard_map/reduce_scatter | solution.py:299
  1030.7 235.9 %reduce-scatter.21.cloned.1.call-start = ((), (), s32[]{:S(2)}) async-start(), calls=%async_computation.20 | async-start | bytes 9437184 | tf_op jit(solution)/shard_map/reduce_scatter | solution.py:308
  1039.1 455.6 %reduce-scatter.23.cloned.1.call-start = ((), (), s32[]{:S(2)}) async-start(), calls=%async_computation.21 | async-start | bytes 25952256 | tf_op jit(solution)/shard_map/reduce_scatter | solution.py:323
  1051.8 887.2 %reduce-scatter.25.cloned.1.call-start = ((), (), s32[]{:S(2)}) async-start(), calls=%async_computation.22 | async-start | bytes 51904512
  1073.0 1089.4 %all-reduce.8.cloned.1.call-start = ((), (), s32[]{:S(2)}) async-start(), calls=%async_computation.23 | async-start | bytes 22020096 | tf_op jit(solution)/shard_map/psum | solution.py:334
  1947.2 13.3 copy-start.18
  (31 other events, 146.2 us)
Sparse Core Ops, SparseCore 0:
  9.6 23.4 all-gather.9
  34.7 21.5 all-gather.13
  58.0 78.8 all-gather.11
  138.3 80.5 all-gather.15
  220.5 200.8 all-gather.17
  422.9 200.8 all-gather.19
  625.4 200.8 all-gather.21
  966.1 25.9 reduce-scatter.10
  995.7 24.7 reduce-scatter.12
  1023.2 28.5 reduce-scatter.16
  1054.6 30.5 reduce-scatter.18
  1087.4 88.8 reduce-scatter.14
  1178.6 87.9 reduce-scatter.20
  1268.8 225.7 reduce-scatter.22
  1496.9 442.0 reduce-scatter.24
  1944.0 218.3 all-reduce.7
where the time goes:
time: 2190 us; the launch traced here: 2180 us
  waiting for transfers between devices  1750 us (80%)
  matrix products  259 us (12%)
  blocking collectives  73.5 us (3%)
  other arithmetic  49.7 us (2%)
  local copies, waits for them, and re-layouts  32.2 us (1%)
    unnamed x17, waiting for transfers between devices  449 us
    reduce_scatter x1, waiting for transfers between devices, per_device(): lax.psum_scatter(jnp.einsum('tc,td->cd', columns, cotangent, preferred_el...  228 us
    all_gather x1, waiting for transfers between devices, per_device(): lax.all_gather(w_gate, 'fsdp', axis=0, tiled=True)  195 us
    all_gather x1, waiting for transfers between devices, per_device(): lax.all_gather(w_down, 'fsdp', axis=0, tiled=True)  190 us
    all_gather x1, waiting for transfers between devices, per_device(): lax.all_gather(w_up, 'fsdp', axis=0, tiled=True)  189 us
    psum x1, waiting for transfers between devices, per_device(): lax.psum(scattered[2].astype(jnp.bfloat16), 'ctx').astype(jnp.float32)  170 us
    reduce_scatter x1, waiting for transfers between devices, per_device(): lax.psum_scatter(attn_terms[2].astype(jnp.bfloat16), 'fsdp', scatter_dime...  91.1 us
    reduce_scatter x1, waiting for transfers between devices, per_device(): lax.psum_scatter(attn_terms[5].astype(jnp.bfloat16), 'fsdp', scatter_dime...  90.3 us
  transfers between devices with their start and end apart: 16, of which 14 were waited for; matrix products, arithmetic and copies ran while one was open for 8% of the time, Pallas kernels for 0%

commit v1 on v0

v1 whole, which is shorter than its diff:
```python
import jax
import jax.numpy as jnp
from jax import lax
from jax.sharding import PartitionSpec as P

HEADS = 32
KV_HEADS = 4
HEAD_DIM = 64

eps_norm = 1e-05
theta_base = 10000.0
neg_large = -1e30
bf16 = jnp.bfloat16
f32 = jnp.float32


def dot(a, b):
    return jnp.dot(a, b, preferred_element_type=f32)


def dot_nt(a, b):
    return lax.dot_general(a, b, (((1,), (1,)), ((), ())), preferred_element_type=f32)


def dot_tn(a, b):
    return lax.dot_general(a, b, (((0,), (0,)), ((), ())), preferred_element_type=f32)


def rope_tables(positions):
    half_width = HEAD_DIM // 2
    frequency = theta_base ** (-(jnp.arange(half_width, dtype=f32) * 2.0) / HEAD_DIM)
    angles = positions.astype(f32)[:, None] * frequency[None, :]
    return (jnp.cos(angles)[:, None, :], jnp.sin(angles)[:, None, :])


def rotate(field, cosine, sine_table, direction):
    half_width = field.shape[-1] // 2
    first_half = field[..., :half_width]
    second_half = field[..., half_width:]
    return jnp.concatenate(
        [
            first_half * cosine - direction * second_half * sine_table,
            second_half * cosine + direction * first_half * sine_table,
        ],
        axis=-1,
    )


def gather(x, axis_name, axis=0):
    return lax.all_gather(x, axis_name, axis=axis, tiled=True)


def scatter(x, axis_name, axis=0):
    return lax.psum_scatter(x.astype(bf16), axis_name, scatter_dimension=axis, tiled=True)


def per_device(
    tokens,
    positions,
    gain_attn,
    gain_mlp,
    w_query,
    w_key,
    w_value,
    w_out,
    w_gate,
    w_up,
    w_down,
    cotangent,
):
    n_ctx = lax.axis_size("ctx")
    n_fsdp = lax.axis_size("fsdp")
    c = lax.axis_index("ctx")
    rows = tokens.shape[0]
    width = tokens.shape[1]
    seq = rows * n_ctx
    own_rows = w_query.shape[0]
    my_heads = HEADS // n_ctx
    q_width = my_heads * HEAD_DIM
    kv_heads = max(1, KV_HEADS // n_ctx)
    copies = max(1, n_ctx // KV_HEADS)
    kv_width = kv_heads * HEAD_DIM
    per_kv = my_heads // kv_heads
    col_width = width // n_ctx
    ff_width = w_gate.shape[1]
    unit = ff_width // (n_fsdp * n_ctx)
    scale = HEAD_DIM ** (-0.5)

    def columns(w, start, count):
        return lax.dynamic_slice_in_dim(w, start, count, axis=1)

    gain_one = gain_attn.astype(f32)[:, None]
    gain_two = gain_mlp.astype(f32)[:, None]

    qkv_own = jnp.concatenate(
        [
            columns(w_query, c * q_width, q_width),
            columns(w_key, (c // copies) * kv_width, kv_width),
            columns(w_value, (c // copies) * kv_width, kv_width),
        ],
        axis=1,
    )
    qkv_own = (gain_one * qkv_own).astype(bf16)
    out_own = columns(w_out, c * col_width, col_width)

    def units(w):
        parts = w.reshape(own_rows, n_fsdp, n_ctx, unit)
        return lax.dynamic_index_in_dim(parts, c, axis=2, keepdims=False).reshape(
            own_rows, n_fsdp * unit
        )

    gate_own = (gain_two * units(w_gate)).astype(bf16)
    up_own = (gain_two * units(w_up)).astype(bf16)
    down_own = lax.dynamic_slice_in_dim(w_down, c * unit, unit, axis=0)

    x_all = gather(tokens, "ctx")
    pos_all = gather(positions, "ctx")
    qkv_w = gather(qkv_own, "fsdp")
    out_w = gather(out_own, "fsdp")
    gate_w = gather(gate_own, "fsdp")
    up_w = gather(up_own, "fsdp")
    down_w = gather(down_own, "fsdp")
    cot_all = gather(cotangent, "ctx")

    x_f = x_all.astype(f32)
    r_one = lax.rsqrt(jnp.mean(x_f * x_f, axis=-1, keepdims=True) + eps_norm)
    pre = dot(x_all, qkv_w) * r_one
    cosine, sine = rope_tables(pos_all)
    index = jnp.arange(seq, dtype=jnp.int32)
    begin = index - pos_all
    allowed = (index[None, :] <= index[:, None]) & (index[None, :] >= begin[:, None])

    q = rotate(pre[:, :q_width].reshape(seq, my_heads, HEAD_DIM), cosine, sine, 1.0).astype(bf16)
    k = rotate(
        pre[:, q_width : q_width + kv_width].reshape(seq, kv_heads, HEAD_DIM), cosine, sine, 1.0
    ).astype(bf16)
    v = pre[:, q_width + kv_width :].astype(bf16).reshape(seq, kv_heads, HEAD_DIM)
    q = q.reshape(seq, kv_heads, per_kv, HEAD_DIM)

    scores = jnp.einsum("qkgd,lkd->kgql", q, k, preferred_element_type=f32) * scale
    scores = jnp.where(allowed[None, None], scores, neg_large)
    top = jnp.max(scores, axis=-1, keepdims=True)
    weights = jnp.where(allowed[None, None], jnp.exp(scores - top), 0.0)
    probs = weights / jnp.sum(weights, axis=-1, keepdims=True)
    probs_low = probs.astype(bf16)
    attended = jnp.einsum("kgql,lkd->qkgd", probs_low, v, preferred_element_type=f32)
    att_own = attended.astype(bf16).reshape(seq, q_width)
    att_all = gather(att_own, "ctx", axis=1)

    mid_own = columns(x_all, c * col_width, col_width).astype(f32) + dot(att_all, out_w)
    mid_all = gather(mid_own.astype(bf16), "ctx", axis=1)
    mid_f = mid_all.astype(f32)
    r_two = lax.rsqrt(jnp.mean(mid_f * mid_f, axis=-1, keepdims=True) + eps_norm)
    gate = dot(mid_all, gate_w) * r_two
    up = dot(mid_all, up_w) * r_two
    sig = jax.nn.sigmoid(gate)
    hidden = (gate * sig * up).astype(bf16)
    mlp = scatter(dot(hidden, down_w), "ctx").astype(f32)
    mid_rows = lax.dynamic_slice_in_dim(mid_all, c * rows, rows, axis=0).astype(f32)
    output = (mid_rows + mlp).astype(bf16)

    grad_hidden = dot_nt(cot_all, down_w)
    grad_down_raw = scatter(dot_tn(hidden, cot_all), "fsdp")
    d_gate = grad_hidden * up * sig * (1.0 + gate * (1.0 - sig))
    d_up = grad_hidden * gate * sig
    stat_two = jnp.sum(d_gate * gate + d_up * up, axis=-1, keepdims=True)
    d_gate = (d_gate * r_two).astype(bf16)
    d_up = (d_up * r_two).astype(bf16)
    grad_gate_raw = scatter(dot_tn(mid_all, d_gate), "fsdp")
    grad_up_raw = scatter(dot_tn(mid_all, d_up), "fsdp")
    back_two = dot_nt(d_gate, gate_w) + dot_nt(d_up, up_w)
    back_two = back_two - mid_f * (r_two * r_two * stat_two * (1.0 / width))
    back_own = scatter(back_two, "ctx", axis=1).astype(f32)
    gm_own = columns(cot_all, c * col_width, col_width).astype(f32) + back_own
    gm_low = gm_own.astype(bf16)

    grad_out_raw = scatter(dot_tn(att_all, gm_low), "fsdp")
    d_att = scatter(dot_nt(gm_low, out_w), "ctx", axis=1).reshape(seq, kv_heads, per_kv, HEAD_DIM)
    d_probs = jnp.einsum("qkgd,lkd->kgql", d_att, v, preferred_element_type=f32)
    delta = jnp.sum(probs * d_probs, axis=-1, keepdims=True)
    d_scores = (probs * (d_probs - delta)).astype(bf16)
    d_q = jnp.einsum("kgql,lkd->qkgd", d_scores, k, preferred_element_type=f32) * scale
    d_k = jnp.einsum("kgql,qkgd->lkd", d_scores, q, preferred_element_type=f32) * scale
    d_v = jnp.einsum("kgql,qkgd->lkd", probs_low, d_att, preferred_element_type=f32)
    d_pre = jnp.concatenate(
        [
            rotate(d_q.reshape(seq, my_heads, HEAD_DIM), cosine, sine, -1.0).reshape(seq, q_width),
            rotate(d_k, cosine, sine, -1.0).reshape(seq, kv_width),
            d_v.reshape(seq, kv_width),
        ],
        axis=1,
    )
    stat_one = jnp.sum(d_pre * pre, axis=-1, keepdims=True)
    d_pre = (d_pre * r_one).astype(bf16)
    grad_qkv_raw = scatter(dot_tn(x_all, d_pre), "fsdp")
    back_one = dot_nt(d_pre, qkv_w) - x_f * (r_one * r_one * stat_one * (1.0 / width))
    at = (jnp.arange(width, dtype=jnp.int32) // col_width == c)[None, :]
    back_one = back_one + jnp.where(at, jnp.tile(gm_own, (1, n_ctx)), 0.0)
    grad_tokens = scatter(back_one, "ctx").astype(f32)

    qkv_grad = gather(grad_qkv_raw[None], "ctx").astype(f32)

    def joined(part):
        return jnp.moveaxis(part, 0, 1).reshape(own_rows, -1)

    raw_query = joined(qkv_grad[:, :, :q_width])

    def kv(part):
        part = part.reshape(n_ctx // copies, copies, own_rows, kv_width).sum(axis=1)
        return joined(part)

    raw_key = kv(qkv_grad[:, :, q_width : q_width + kv_width])
    raw_value = kv(qkv_grad[:, :, q_width + kv_width :])
    grad_out = gather(grad_out_raw, "ctx", axis=1).astype(f32)

    def spread(part):
        full = gather(part[None], "ctx").reshape(n_ctx, own_rows, n_fsdp, unit)
        return full.transpose(1, 2, 0, 3).reshape(own_rows, ff_width).astype(f32)

    raw_gate = spread(grad_gate_raw)
    raw_up = spread(grad_up_raw)
    grad_down = gather(grad_down_raw, "ctx").astype(f32)

    def gain_term(raw, w):
        return jnp.sum(raw * w.astype(f32), axis=1)

    grad_gain_one = (
        gain_term(raw_query, w_query) + gain_term(raw_key, w_key) + gain_term(raw_value, w_value)
    )
    grad_gain_two = gain_term(raw_gate, w_gate) + gain_term(raw_up, w_up)
    return (
        output,
        grad_tokens,
        grad_gain_one,
        grad_gain_two,
        gain_one * raw_query,
        gain_one * raw_key,
        gain_one * raw_value,
        grad_out,
        gain_two * raw_gate,
        gain_two * raw_up,
        grad_down,
    )


def solution(mesh):
    both = P(("fsdp", "ctx"), None)
    first = P("fsdp", None)
    return jax.shard_map(
        per_device,
        mesh=mesh,
        in_specs=(both, P(("fsdp", "ctx")), P("fsdp"), P("fsdp")) + (first,) * 7 + (both,),
        out_specs=(both, both, P("fsdp"), P("fsdp")) + (first,) * 7,
        check_vma=False,
    )
```

time: 2190 us -> 1250 us (0.57)
  waiting for transfers between devices: 1750 us -> 781 us
  local copies, waits for them, and re-layouts: 32.2 us -> 98.7 us
  blocking collectives: 73.5 us -> 8.19 us
  other arithmetic: 49.7 us -> 88 us
    unnamed x17 -> x23, waiting for transfers between devices: 449 us -> 3.15 us
    reduce_scatter x7 -> x9, waiting for transfers between devices: 471 us -> 286 us  [scatter(): lax.psum_scatter(x.astype(bf16), axis_name, scatter_dimension=axis, tiled...]
    all_gather x7 -> x14, waiting for transfers between devices: 663 us -> 492 us  [gather(): return lax.all_gather(x, axis_name, axis=axis, tiled=True)]
    psum x1 -> x0, waiting for transfers between devices: 170 us -> none  [per_device(): lax.psum(scattered[2].astype(jnp.bfloat16), 'ctx').astype(jnp.float32)]
    all_gather x4 -> x1, blocking collectives: 49.8 us -> 8.19 us  [gather(): return lax.all_gather(x, axis_name, axis=axis, tiled=True)]
    convert_element_type x3 -> x7, local copies, waits for them, and re-layouts: 5.36 us -> 38.9 us  [the longest x6 36 us: spread(): return full.transpose(1, 2, 0, 3).reshape(own_rows, ff_width).astype(f32)]
    unnamed x67 -> x98, local copies, waits for them, and re-layouts: 6.61 us -> 39 us
    another operation x6 -> x2, other arithmetic: 0.76 us -> 30.4 us
  transfers between devices with their start and end apart: 16 -> 23, of which waited for: 14 -> 20; matrix products, arithmetic and copies ran while one was open for 8% -> 30% of each run, Pallas kernels for 0% -> 0%
where the time goes in v1:
time: 1250 us; the launch traced here: 1240 us
  waiting for transfers between devices  781 us (62%)
  matrix products  250 us (20%)
  local copies, waits for them, and re-layouts  98.7 us (8%)
  other arithmetic  88 us (7%)
  between operations  15.1 us (1%)
    all_gather x14, waiting for transfers between devices, gather(): return lax.all_gather(x, axis_name, axis=axis, tiled=True)  492 us
    reduce_scatter x9, waiting for transfers between devices, scatter(): lax.psum_scatter(x.astype(bf16), axis_name, scatter_dimension=axis, tiled...  286 us
    dot_general x5, matrix products, dot_nt(): lax.dot_general(a, b, (((1,), (1,)), ((), ())), preferred_element_type=f32)  54.6 us
    dot_general x5, matrix products, dot(): return jnp.dot(a, b, preferred_element_type=f32)  51.5 us
    dot_general x5, matrix products, dot_tn(): lax.dot_general(a, b, (((0,), (0,)), ((), ())), preferred_element_type=f32)  51.4 us
    unnamed x98, local copies, waits for them, and re-layouts  39 us
    convert_element_type x6, local copies, waits for them, and re-layouts, spread(): return full.transpose(1, 2, 0, 3).reshape(own_rows, ff_width).astype(f32)  36 us
    another operation x2, other arithmetic  30.4 us
  transfers between devices with their start and end apart: 23, of which 20 were waited for; matrix products, arithmetic and copies ran while one was open for 30% of the time, Pallas kernels for 0%

profile of v1, /device:TPU:8, one launch (start us, length us, event | category | flops | bytes accessed | tf_op | source)
XLA Modules:
  0.0 1241.6 jit_solution(4867924627730754356)
XLA Ops:
  24.3 39.4 %all-gather.19.cloned.1.call-done = bf16[1024,2048]{1,0:T(8,128)(2,1)} async-done(((bf16[256,2048]{1,0:T(8,128)(2,1)}), bf16[1024,2048]{1,0:T(8,128)(2,1)}) %all-gather.19.cloned.1.call-update) | async-done | bytes 4194320 | tf_op jit(solution)/shard_map/all_gather | solution.py:50
  67.4 31.8 %all-gather.21.cloned.1.call-done = bf16[2048,640]{1,0:T(8,128)(2,1)} async-done(((bf16[256,640]{1,0:T(8,128)(2,1)}), bf16[2048,640]{1,0:T(8,128)(2,1)}) %all-gather.21.cloned.1.call-update) | async-done | bytes 2621456 | tf_op jit(solution)/shard_map/all_gather | solution.py:50
  106.8 13.7 %fusion.3 = (f32[8,1024]{1,0:T(8,128)S(1)}, f32[1024,1024,8]{1,0,2:T(8,128)}) fusion(pred[1024,1024]{0,1:T(8,128)(4,1)S(1)} %copy-done.7, bf16[1024,8,32]{0,2,1:T(8,128)(2,1)S(1)} %get-tuple-element.45, bf16[1024,8,32]{0,2,1:T(8,128)(2,1)S(1)} %get-tuple-element.44, bf16[1024,32]{0,1:T(8,128)(2,1)S(1)} %get-tuple-element.51, ...), kind=kOutput, calls=%fused_computation.7 | convolution fusion | flops 1101258752 | bytes 35815424 | tf_op jit(solution)/shard_map/qkgd,lkd->kgql/dot_general | solution.py:140
  120.5 14.8 %fusion.5 = f32[8,1024]{1,0:T(8,128)S(1)} fusion(f32[1024,1024,8]{1,0,2:T(8,128)} %get-tuple-element.66, f32[8,1024]{1,0:T(8,128)S(1)} %get-tuple-element.65, pred[1024,1024]{0,1:T(8,128)(4,1)S(1)} %copy-done.7), kind=kLoop, calls=%fused_computation.9 | loop fusion | flops 41934848 | bytes 34668544 | tf_op jit(solution)/shard_map/reduce_sum | solution.py:144
  135.4 16.3 %fusion.26 = bf16[64,8,1024]{2,0,1:T(8,128)(2,1)} fusion(f32[1024,640]{0,1:T(8,128)S(1)} %multiply_bitcast_fusion, f32[8,1024]{1,0:T(8,128)S(1)} %fusion.5, f32[8,1024]{1,0:T(8,128)S(1)} %get-tuple-element.65, f32[1024,1024,8]{1,0,2:T(8,128)} %get-tuple-element.66, pred[1024,1024]{0,1:T(8,128)(4,1)S(1)} %copy-done.7), kind=kOutput, calls=%fused_computation.65 | convolution fusion | flops 1124597760 | bytes 35848192 | tf_op jit(solution)/shard_map/kgql,lkd->qkgd/dot_general | solution.py:146
  153.4 50.8 %all-gather.23.cloned.1.call-done = bf16[1024,2048]{0,1:T(8,128)(2,1)} async-done(((bf16[1024,512]{0,1:T(8,128)(2,1)}), bf16[1024,2048]{0,1:T(8,128)(2,1)}) %all-gather.23.cloned.1.call-update) | async-done | bytes 4194320 | tf_op jit(solution)/shard_map/all_gather | solution.py:50
  222.7 35.9 %all-gather.35.cloned.1.call-done = bf16[1024,2048]{1,0:T(8,128)(2,1)} async-done(((bf16[256,2048]{1,0:T(8,128)(2,1)}), bf16[1024,2048]{1,0:T(8,128)(2,1)}) %all-gather.35.cloned.1.call-update) | async-done | bytes 4194320 | tf_op jit(solution)/shard_map/all_gather | solution.py:50
  258.6 60.5 %all-gather.33.cloned.1.call-done = bf16[1408,2048]{1,0:T(8,128)(2,1)} async-done(((bf16[176,2048]{1,0:T(8,128)(2,1)}), bf16[1408,2048]{1,0:T(8,128)(2,1)}) %all-gather.33.cloned.1.call-update) | async-done | bytes 5767184 | tf_op jit(solution)/shard_map/all_gather | solution.py:50
  319.1 11.8 fusion.76
  330.9 43.9 %all-gather.27.cloned.1.call-done = bf16[1024,2048]{1,0:T(8,128)(2,1)} async-done(((bf16[1024,512]{1,0:T(8,128)(2,1)}), bf16[1024,2048]{1,0:T(8,128)(2,1)}) %all-gather.27.cloned.1.call-update) | async-done | bytes 4194320 | tf_op jit(solution)/shard_map/all_gather | solution.py:50
  377.9 57.0 %all-gather.29.cloned.1.call-done = bf16[2048,1408]{0,1:T(8,128)(2,1)} async-done(((bf16[256,1408]{0,1:T(8,128)(2,1)}), bf16[2048,1408]{0,1:T(8,128)(2,1)}) %all-gather.29.cloned.1.call-update) | async-done | bytes 5767184 | tf_op jit(solution)/shard_map/all_gather | solution.py:50
  434.9 11.8 fusion.75
  446.6 49.5 %all-gather.31.cloned.1.call-done = bf16[2048,1408]{0,1:T(8,128)(2,1)} async-done(((bf16[256,1408]{0,1:T(8,128)(2,1)}), bf16[2048,1408]{0,1:T(8,128)(2,1)}) %all-gather.31.cloned.1.call-update) | async-done | bytes 5767184 | tf_op jit(solution)/shard_map/all_gather | solution.py:50
  496.1 16.9 %add_reduce_fusion = (f32[1024]{0:T(1024)S(1)}, f32[1024,1408]{1,0:T(8,128)}, bf16[1024,1408]{1,0:T(8,128)(2,1)}) fusion(f32[1024,1408]{1,0:T(8,128)} %fusion.75, f32[1024]{0:T(1024)S(1)} %add_rsqrt_fusion, f32[1408,1024]{0,1:T(8,128)} %fusion.76, bf16[1024,2048]{1,0:T(8,128)(2,1)} %all-gather.27.cloned.1.call-done, ...), kind=kOutput, calls=%fused_computation.41 | convolution fusion | flops 5934414848 | bytes 30154752 | tf_op jit(solution)/shard_map/dot_general | solution.py:18
  513.1 11.5 fusion.68
  524.6 15.9 %fusion.18 = bf16[1024,2048]{1,0:T(8,128)(2,1)} fusion(bf16[1024,2048]{1,0:T(8,128)(2,1)S(1)} %copy-done.10, f32[1024,2048]{1,0:T(8,128)} %fusion.68, f32[1024]{0:T(1024)S(1)} %multiply_multiply_fusion.1, bf16[2048,1408]{0,1:T(8,128)(2,1)} %all-gather.31.cloned.1.call-done, f32[1024]{0:T(1024)S(1)} %add_rsqrt_fusion, f32[1408,1024]{0,1:T(8,128)} %fusion.76, ...), kind=kOutput, calls=%fused_computation.26 | convolution fusion | flops 5927600128 | bytes 34086912 | tf_op jit(solution)/shard_map/dot_general | solution.py:22
  540.5 54.0 %reduce-scatter.12.cloned.1.call-done = bf16[1024,512]{1,0:T(8,128)(2,1)} async-done(((bf16[1024,2048]{1,0:T(8,128)(2,1)}), bf16[1024,512]{1,0:T(8,128)(2,1)}) %reduce-scatter.12.cloned.1.call-update) | async-done | bytes 1048592 | tf_op jit(solution)/shard_map/reduce_scatter | solution.py:54
  609.2 15.6 %convolution_convert_fusion.1 = bf16[2048,1408]{1,0:T(8,128)(2,1)} fusion(bf16[1024,2048]{1,0:T(8,128)(2,1)} %all-gather.27.cloned.1.call-done, f32[1024]{0:T(1024)S(1)} %add_rsqrt_fusion, f32[1408,1024]{0,1:T(8,128)} %fusion.76, f32[1024,1408]{1,0:T(8,128)} %fusion.75), kind=kOutput, calls=%fused_computation.28 | convolution fusion | flops 5919997952 | bytes 21499904 | tf_op jit(solution)/shard_map/dot_general | solution.py:26
  624.9 12.1 convolution_convert_fusion.2
  658.6 26.6 %fusion = (f32[8,1024]{1,0:T(8,128)S(1)}, f32[1024,1024,8]{1,0,2:T(8,128)}) fusion(f32[8,1024]{1,0:T(8,128)S(1)} %fusion.5, f32[8,1024]{1,0:T(8,128)S(1)} %get-tuple-element.65, f32[1024,1024,8]{1,0,2:T(8,128)} %get-tuple-element.66, pred[1024,1024]{0,1:T(8,128)(4,1)} %fusion.24, bf16[1024,8,64]{0,2,1:T(8,128)(2,1)} %bitcast.208, f32[1024,640]{0,1:T(8,128)S(1)} %copy-done.6), kind=kOutput, calls=%fused_computation.3 | convolution fusion | flops 1132453888 | bytes 69435392 | tf_op jit(solution)/shard_map/qkgd,lkd->kgql/dot_general | solution.py:179
  685.2 30.1 %fusion.6 = bf16[8,1024,1024]{1,2,0:T(8,128)(2,1)} fusion(f32[1024,1024,8]{1,0,2:T(8,128)} %get-tuple-element.68, f32[8,1024]{1,0:T(8,128)S(1)} %get-tuple-element.67, f32[8,1024]{1,0:T(8,128)S(1)} %fusion.5, f32[8,1024]{1,0:T(8,128)S(1)} %get-tuple-element.65, f32[1024,1024,8]{1,0,2:T(8,128)} %get-tuple-element.66, pred[1024,1024]{0,1:T(8,128)(4,1)} %fusion.24), kind=kLoop, calls=%fused_computation.10 | loop fusion | flops 67108864 | bytes 85032960 | tf_op jit(solution)/shard_map/reshape.17
  715.3 11.4 fusion.35
  738.2 15.3 %fusion.31 = f32[1024,64]{0,1:T(8,128)S(1)} fusion(bf16[1024,8,64]{0,2,1:T(8,128)(2,1)} %bitcast.209, f32[8,1024]{1,0:T(8,128)S(1)} %copy-done.27, f32[8,1024]{1,0:T(8,128)S(1)} %copy-done.25, f32[1024,1024,8]{1,0,2:T(8,128)} %get-tuple-element.66, pred[1024,1024]{0,1:T(8,128)(4,1)} %fusion.24), kind=kOutput, calls=%fused_computation.70 | convolution fusion | flops 1124073472 | bytes 35979264 | tf_op jit(solution)/shard_map/kgql,qkgd->lkd/dot_general | solution.py:184
  773.1 50.4 %reduce-scatter.20.cloned.1.call-done = bf16[256,1408]{1,0:T(8,128)(2,1)} async-done(((bf16[2048,1408]{1,0:T(8,128)(2,1)}), bf16[256,1408]{1,0:T(8,128)(2,1)}) %reduce-scatter.20.cloned.1.call-update) | async-done | bytes 720912 | tf_op jit(solution)/shard_map/reduce_scatter | solution.py:54
  823.6 65.9 %reduce-scatter.26.cloned.1.call-done = bf16[176,2048]{1,0:T(8,128)(2,1)} async-done(((bf16[1408,2048]{1,0:T(8,128)(2,1)}), bf16[176,2048]{1,0:T(8,128)(2,1)}) %reduce-scatter.26.cloned.1.call-update) | async-done | bytes 720912 | tf_op jit(solution)/shard_map/reduce_scatter | solution.py:54
  889.6 36.9 %reduce-scatter.18.cloned.1.call-done = bf16[256,640]{0,1:T(8,128)(2,1)} async-done(((bf16[2048,640]{0,1:T(8,128)(2,1)}), bf16[256,640]{0,1:T(8,128)(2,1)}) %reduce-scatter.18.cloned.1.call-update) | async-done | bytes 327696 | tf_op jit(solution)/shard_map/reduce_scatter | solution.py:54
  951.0 34.6 %reduce-scatter.10.cloned.1.call-done = bf16[256,2048]{1,0:T(8,128)(2,1)} async-done(((bf16[1024,2048]{1,0:T(8,128)(2,1)}), bf16[256,2048]{1,0:T(8,128)(2,1)}) %reduce-scatter.10.cloned.1.call-update) | async-done | bytes 1048592 | tf_op jit(solution)/shard_map/reduce_scatter | solution.py:54
  988.5 25.4 %all-gather.37.cloned.1.call-done = bf16[256,2048]{1,0:T(8,128)(2,1)} async-done(((bf16[256,512]{1,0:T(8,128)(2,1)}), bf16[256,2048]{1,0:T(8,128)(2,1)}) %all-gather.37.cloned.1.call-update) | async-done | bytes 1048592 | tf_op jit(solution)/shard_map/all_gather | solution.py:50
  1016.7 41.0 %all-gather.45.cloned.1.call-done = bf16[1024,1408]{1,0:T(8,128)(2,1)} async-done(((bf16[256,1408]{1,0:T(8,128)(2,1)}), bf16[1024,1408]{1,0:T(8,128)(2,1)}) %all-gather.45.cloned.1.call-update) | async-done | bytes 2883600 | tf_op jit(solution)/shard_map/all_gather | solution.py:50
  1076.9 24.5 %all-gather.43.cloned.1.call-done = bf16[1024,1408]{1,0:T(8,128)(2,1)} async-done(((bf16[256,1408]{1,0:T(8,128)(2,1)}), bf16[1024,1408]{1,0:T(8,128)(2,1)}) %all-gather.43.cloned.1.call-update) | async-done | bytes 2883600 | tf_op jit(solution)/shard_map/all_gather | solution.py:50
  1150.4 25.5 %all-gather.41.cloned.1.call-done = bf16[1024,640]{0,1:T(8,128)(2,1)} async-done(((bf16[256,640]{0,1:T(8,128)(2,1)}), bf16[1024,640]{0,1:T(8,128)(2,1)}) %all-gather.41.cloned.1.call-update) | async-done | bytes 1310736 | tf_op jit(solution)/shard_map/all_gather | solution.py:50
  1194.6 37.3 %reduce-scatter.16.cloned.1.call-done = bf16[256,2048]{1,0:T(8,128)(2,1)} async-done(((bf16[1024,2048]{1,0:T(8,128)(2,1)}), bf16[256,2048]{1,0:T(8,128)(2,1)}) %reduce-scatter.16.cloned.1.call-update) | async-done | bytes 1048592 | tf_op jit(solution)/shard_map/reduce_scatter | solution.py:54
  (211 shorter events, 238.4 us)
Async XLA Ops:
  7.2 145.2 %copy-start = (bf16[704,2048]{1,0:T(8,128)(2,1)S(1)}, bf16[704,2048]{1,0:T(8,128)(2,1)}, u32[]{:S(2)}) copy-start(bf16[704,2048]{1,0:T(8,128)(2,1)} %param.22) | copy-start | bytes 8650756
  7.2 56.6 %all-gather.19.cloned.1.call-start = ((), (), s32[]{:S(2)}) async-start(), calls=%async_computation.9 | async-start | bytes 5242880 | tf_op jit(solution)/shard_map/all_gather | solution.py:50
  7.9 91.3 %all-gather.21.cloned.1.call-start = ((), (), s32[]{:S(2)}) async-start(), calls=%async_computation.10 | async-start | bytes 2949120 | tf_op jit(solution)/shard_map/all_gather | solution.py:50
  11.6 141.8 %all-gather.25.cloned.1.call-start = ((), (), s32[]{:S(2)}) async-start(), calls=%async_computation.12 | async-start | bytes 2359296 | tf_op jit(solution)/shard_map/all_gather | solution.py:50
  13.3 190.9 %all-gather.23.cloned.1.call-start = ((), (), s32[]{:S(2)}) async-start(), calls=%async_computation.11 | async-start | bytes 5242880 | tf_op jit(solution)/shard_map/all_gather | solution.py:50
  13.4 91.7 %copy-start.34 = (f32[32]{0:T(128)}, f32[32]{0:T(128)S(1)}, u32[]{:S(2)}) copy-start(f32[32]{0:T(128)S(1)} %multiply_power_fusion) | copy-start | bytes 388
  21.6 83.5 %copy-start.28 = (f32[1024]{0:T(1024)}, f32[1024]{0:T(1024)S(1)}, u32[]{:S(2)}) copy-start(f32[1024]{0:T(1024)S(1)} %convert_element_type.186) | copy-start | bytes 12292
  24.3 81.3 %copy-start.14 = (f32[1024,32]{0,1:T(8,128)}, f32[1024,32]{0,1:T(8,128)S(1)}, u32[]{:S(2)}) copy-start(f32[1024,32]{0,1:T(8,128)S(1)} %get-tuple-element.58) | copy-start | bytes 393220
  67.4 37.3 %copy-start.38 = (f32[1024]{0:T(1024)}, f32[1024]{0:T(1024)S(1)}, u32[]{:S(2)}) copy-start(f32[1024]{0:T(1024)S(1)} %add_rsqrt_fusion.1) | copy-start | bytes 12292
  120.5 564.7 %copy-start.24 = (f32[8,1024]{1,0:T(8,128)}, f32[8,1024]{1,0:T(8,128)S(1)}, u32[]{:S(2)}) copy-start(f32[8,1024]{1,0:T(8,128)S(1)} %get-tuple-element.65) | copy-start | bytes 98308
  135.3 549.9 %copy-start.26 = (f32[8,1024]{1,0:T(8,128)}, f32[8,1024]{1,0:T(8,128)S(1)}, u32[]{:S(2)}) copy-start(f32[8,1024]{1,0:T(8,128)S(1)} %fusion.5) | copy-start | bytes 98308
  151.7 106.9 %all-gather.35.cloned.1.call-start = ((), (), s32[]{:S(2)}) async-start(), calls=%async_computation.18 | async-start | bytes 5242880 | tf_op jit(solution)/shard_map/all_gather | solution.py:50
  152.3 166.9 %all-gather.33.cloned.1.call-start = ((), (), s32[]{:S(2)}) async-start(), calls=%async_computation.16 | async-start | bytes 6488064 | tf_op jit(solution)/shard_map/all_gather | solution.py:50
  153.3 57.4 %copy-start.41 = (bf16[256]{0:T(256)(128)(2,1)S(1)}, bf16[256]{0:T(256)(128)(2,1)}, u32[]{:S(2)}) copy-start(bf16[256]{0:T(256)(128)(2,1)} %param.15) | copy-start | bytes 1540
  153.3 221.5 %all-gather.27.cloned.1.call-start = ((), (), s32[]{:S(2)}) async-start(), calls=%async_computation.13 | async-start | bytes 5242880 | tf_op jit(solution)/shard_map/all_gather | solution.py:50
  210.6 224.3 %all-gather.29.cloned.1.call-start = ((), (), s32[]{:S(2)}) async-start(), calls=%async_computation.14 | async-start | bytes 6488064 | tf_op jit(solution)/shard_map/all_gather | solution.py:50
  222.0 274.2 %all-gather.31.cloned.1.call-start = ((), (), s32[]{:S(2)}) async-start(), calls=%async_computation.15 | async-start | bytes 6488064 | tf_op jit(solution)/shard_map/all_gather | solution.py:50
  222.7 371.8 %reduce-scatter.12.cloned.1.call-start = ((), (), s32[]{:S(2)}) async-start(), calls=%async_computation.19 | async-start | bytes 5242880 | tf_op jit(solution)/shard_map/reduce_scatter | solution.py:54
  540.5 115.5 %reduce-scatter.14.cloned.1.call-start = ((), (), s32[]{:S(2)}) async-start(), calls=%async_computation.20 | async-start | bytes 5242880 | tf_op jit(solution)/shard_map/reduce_scatter | solution.py:54
  603.2 168.6 %reduce-scatter.24.cloned.1.call-start = ((), (), s32[]{:S(2)}) async-start(), calls=%async_computation.25 | async-start | bytes 2359296 | tf_op jit(solution)/shard_map/reduce_scatter | solution.py:54
  609.1 163.2 %reduce-scatter.22.cloned.1.call-start = ((), (), s32[]{:S(2)}) async-start(), calls=%async_computation.24 | async-start | bytes 6488064 | tf_op jit(solution)/shard_map/reduce_scatter | solution.py:54
  624.8 198.7 %reduce-scatter.20.cloned.1.call-start = ((), (), s32[]{:S(2)}) async-start(), calls=%async_computation.23 | async-start | bytes 6488064 | tf_op jit(solution)/shard_map/reduce_scatter | solution.py:54
  637.0 252.5 %reduce-scatter.26.cloned.1.call-start = ((), (), s32[]{:S(2)}) async-start(), calls=%async_computation.27 | async-start | bytes 6488064 | tf_op jit(solution)/shard_map/reduce_scatter | solution.py:54
  649.4 277.1 %reduce-scatter.18.cloned.1.call-start = ((), (), s32[]{:S(2)}) async-start(), calls=%async_computation.22 | async-start | bytes 2949120 | tf_op jit(solution)/shard_map/reduce_scatter | solution.py:54
  760.8 224.8 %reduce-scatter.10.cloned.1.call-start = ((), (), s32[]{:S(2)}) async-start(), calls=%async_computation.17 | async-start | bytes 5242880 | tf_op jit(solution)/shard_map/reduce_scatter | solution.py:54
  771.7 242.2 %all-gather.37.cloned.1.call-start = ((), (), s32[]{:S(2)}) async-start(), calls=%async_computation.26 | async-start | bytes 1310720 | tf_op jit(solution)/shard_map/all_gather | solution.py:50
  772.3 285.5 %all-gather.45.cloned.1.call-start = ((), (), s32[]{:S(2)}) async-start(), calls=%async_computation.31 | async-start | bytes 3604480 | tf_op jit(solution)/shard_map/all_gather | solution.py:50
  773.0 328.4 %all-gather.43.cloned.1.call-start = ((), (), s32[]{:S(2)}) async-start(), calls=%async_computation.30 | async-start | bytes 3604480 | tf_op jit(solution)/shard_map/all_gather | solution.py:50
  823.5 321.7 %all-gather.39.cloned.1.call-start = ((), (), s32[]{:S(2)}) async-start(), calls=%async_computation.28 | async-start | bytes 3604480 | tf_op jit(solution)/shard_map/all_gather | solution.py:50
  889.5 286.4 %all-gather.41.cloned.1.call-start = ((), (), s32[]{:S(2)}) async-start(), calls=%async_computation.29 | async-start | bytes 1638400 | tf_op jit(solution)/shard_map/all_gather | solution.py:50
  926.5 305.4 %reduce-scatter.16.cloned.1.call-start = ((), (), s32[]{:S(2)}) async-start(), calls=%async_computation.21 | async-start | bytes 5242880 | tf_op jit(solution)/shard_map/reduce_scatter | solution.py:54
  1188.6 46.1 %copy-start.1 = (bf16[704,2048]{1,0:T(8,128)(2,1)S(1)}, bf16[704,2048]{1,0:T(8,128)(2,1)}, u32[]{:S(2)}) copy-start(bf16[704,2048]{1,0:T(8,128)(2,1)} %param.22) | copy-start | bytes 8650756
  (34 other events, 341.2 us)
Sparse Core Ops, SparseCore 0:
  9.9 53.8 all-gather.18
  66.0 33.1 all-gather.20
  101.4 28.7 all-gather.24
  151.8 52.3 all-gather.22
  205.9 52.6 all-gather.34
  260.7 58.3 all-gather.32
  321.5 53.2 all-gather.26
  377.0 57.8 all-gather.28
  437.1 59.0 all-gather.30
  540.6 53.8 reduce-scatter.11
  603.3 52.6 reduce-scatter.13
  658.7 32.1 reduce-scatter.23
  693.2 64.2 reduce-scatter.21
  760.3 63.2 reduce-scatter.19
  826.2 63.2 reduce-scatter.25
  891.7 34.8 reduce-scatter.17
  929.9 55.6 reduce-scatter.9
  987.4 26.4 all-gather.36
  1015.9 41.8 all-gather.44
  1059.6 41.7 all-gather.42
  1103.4 41.7 all-gather.38
  1147.2 28.6 all-gather.40
  1179.2 52.6 reduce-scatter.15

commit v2 on v1

v2 whole, which is shorter than its diff:
```python
import jax
import jax.numpy as jnp
from jax import lax
from jax.experimental import pallas as pl
from jax.experimental.pallas import tpu as pltpu
from jax.sharding import PartitionSpec as P

HEADS = 32
KV_HEADS = 4
HEAD_DIM = 64

eps_norm = 1e-05
theta_base = 10000.0
neg_large = -1e30
bf16 = jnp.bfloat16
f32 = jnp.float32
MESH_IDS = pl.DeviceIdType.MESH


def dot(a, b):
    return jnp.dot(a, b, preferred_element_type=f32)


def dot_nt(a, b):
    return lax.dot_general(a, b, (((1,), (1,)), ((), ())), preferred_element_type=f32)


def dot_tn(a, b):
    return lax.dot_general(a, b, (((0,), (0,)), ((), ())), preferred_element_type=f32)


class Place:
    def __init__(self):
        self.f = lax.axis_index("fsdp")
        self.c = lax.axis_index("ctx")
        self.depth = lax.axis_size("fsdp") // 2
        self.z = self.f // 2
        self.core = self.f % 2
        self.other = 1 - self.core
        self.cx = self.c + 1 - 2 * (self.c % 2)
        self.cy = self.c + 2 - 4 * (self.c // 2)
        self.cd = 3 - self.c
        self.sibling = {"fsdp": self.f + 1 - 2 * self.core}
        self.up = {"fsdp": self.f + 2}
        self.down = {"fsdp": self.f - 2}
        self.x = {"ctx": self.cx}
        self.y = {"ctx": self.cy}

    def has_up(self):
        return self.z < self.depth - 1

    def has_down(self):
        return self.z > 0

    def barrier(self):
        sem = pltpu.get_barrier_semaphore()

        def greet(device):
            pl.semaphore_signal(sem, inc=1, device_id=device, device_id_type=MESH_IDS)

        greet(self.sibling)
        greet(self.x)
        greet(self.y)

        @pl.when(self.has_up())
        def _():
            greet(self.up)

        @pl.when(self.has_down())
        def _():
            greet(self.down)

        last = self.depth - 1
        pl.semaphore_wait(sem, 4 - self.z // last + (self.z + last - 1) // last)


def remote(src, dst, send_sem, recv_sem, device):
    return pltpu.make_async_remote_copy(
        src_ref=src,
        dst_ref=dst,
        send_sem=send_sem,
        recv_sem=recv_sem,
        device_id=device,
        device_id_type=MESH_IDS,
    )


class LineGather:
    SEMS = 21

    def __init__(self, place, own, full, sems):
        self.p, self.own, self.full, self.sems = place, own, full, sems
        self.rows = own.shape[0]
        self.n = place.depth

    def view(self, level, core):
        start = pl.multiple_of((2 * level + core) * self.rows, 16)
        return self.full.at[pl.ds(start, self.rows)]

    def to_up(self, hop):
        p = self.p
        level = p.z - (hop - 1)
        src = self.own if hop == 1 else self.view(level, p.core)
        return remote(
            src, self.view(level, p.core), self.sems.at[hop - 1], self.sems.at[6 + hop - 1], p.up
        )

    def to_down(self, hop):
        p = self.p
        level = p.z + (hop - 1)
        src = self.own if hop == 1 else self.view(level, p.core)
        return remote(
            src, self.view(level, p.core), self.sems.at[3 + hop - 1], self.sems.at[9 + hop - 1], p.down
        )

    def to_sibling(self, level, own=False):
        p = self.p
        src = self.own if own else self.view(level, p.core)
        return remote(
            src, self.view(level, p.core), self.sems.at[12 + level], self.sems.at[16 + level], p.sibling
        )

    def local(self):
        p = self.p
        return pltpu.make_async_copy(self.own, self.view(p.z, p.core), self.sems.at[20])

    def start(self):
        p = self.p

        @pl.when(p.has_up())
        def _():
            self.to_up(1).start()

        @pl.when(p.has_down())
        def _():
            self.to_down(1).start()

        self.to_sibling(p.z, True).start()
        self.local().start()

    def arrived(self, level, sem):
        view = self.view(level, self.p.core)
        remote(view, view, self.sems.at[0], sem, self.p.sibling).wait_recv()

    def hop(self, s):
        p = self.p

        @pl.when(p.z >= s)
        def _():
            self.arrived(p.z - s, self.sems.at[6 + s - 1])
            if s < self.n - 1:

                @pl.when(p.has_up())
                def _():
                    self.to_up(s + 1).start()

            self.to_sibling(p.z - s).start()

        @pl.when(p.z + s < self.n)
        def _():
            self.arrived(p.z + s, self.sems.at[9 + s - 1])
            if s < self.n - 1:

                @pl.when(p.has_down())
                def _():
                    self.to_down(s + 1).start()

            self.to_sibling(p.z + s).start()

    def finish(self):
        p = self.p
        self.local().wait()
        for level in range(self.n):
            view = self.view(level, p.other)
            remote(view, view, self.sems.at[0], self.sems.at[16 + level], p.sibling).wait_recv()

    def drain(self):
        p = self.p
        for s in range(1, self.n):

            @pl.when(p.has_up() & (p.z >= s - 1))
            def _():
                self.to_up(s).wait_send()

            @pl.when(p.has_down() & (p.z + s - 1 < self.n))
            def _():
                self.to_down(s).wait_send()

        for level in range(self.n):
            self.to_sibling(level).wait_send()


class PlaneGather:
    SEMS = 8

    def __init__(self, place, view, half, sems, own=None):
        self.p, self.view, self.half, self.sems = place, view, half, sems
        self.own = own

    def src(self):
        return self.view(self.p.c) if self.own is None else self.own

    def to_x(self):
        p = self.p
        return remote(self.src(), self.view(p.c), self.sems.at[0], self.sems.at[2], p.x)

    def to_y(self):
        p = self.p
        return remote(self.src(), self.view(p.c), self.sems.at[1], self.sems.at[3], p.y)

    def on_to_y(self):
        p, h = self.p, self.half(self.p.cx, 0)
        return remote(h, h, self.sems.at[4], self.sems.at[6], p.y)

    def on_to_x(self):
        p, h = self.p, self.half(self.p.cy, 1)
        return remote(h, h, self.sems.at[5], self.sems.at[7], p.x)

    def start(self):
        self.to_x().start()
        self.to_y().start()

    def got(self, ref, sem):
        remote(ref, ref, self.sems.at[0], sem, self.p.x).wait_recv()

    def middle(self):
        p = self.p
        self.got(self.view(p.cx), self.sems.at[2])
        self.on_to_y().start()
        self.got(self.view(p.cy), self.sems.at[3])
        self.on_to_x().start()

    def finish(self):
        p = self.p
        self.got(self.half(p.cd, 0), self.sems.at[6])
        self.got(self.half(p.cd, 1), self.sems.at[7])

    def drain(self):
        self.to_x().wait_send()
        self.to_y().wait_send()
        self.on_to_y().wait_send()
        self.on_to_x().wait_send()


def rows_at(index, count):
    return pl.ds(pl.multiple_of(index * count, count), count)


def any_spec(count):
    return [pl.BlockSpec(memory_space=pl.ANY)] * count


def call(kernel, ins, outs, scratch, collective_id, flops, name):
    return pl.pallas_call(
        kernel,
        out_shape=[jax.ShapeDtypeStruct(s, d) for s, d in outs],
        in_specs=any_spec(len(ins)),
        out_specs=any_spec(len(outs)),
        scratch_shapes=scratch,
        compiler_params=pltpu.CompilerParams(
            collective_id=collective_id, has_side_effects=True, vmem_limit_bytes=60 * 2**20
        ),
        cost_estimate=pl.CostEstimate(flops=flops, bytes_accessed=2**26, transcendentals=2**22),
        name=name,
    )(*ins)


def forward_kernel(
    tok, tab, gains, wqkv_o, wout_o, wgate_o, wup_o, cot,
    x_out, xn_out, qt_out, kt_out, vt_out, lse_out, o_out, m_out,
    wqkv_out, wout_out, wgate, wup, cot_all, tab_out,
    X, XN, QT, KT, VT, K, LSE, O, M, WQ, WO, TAB, G8, GROW, BIAS, OT,
    line_sems, plane_sems, copy_sems,
):
    p = Place()
    n_ctx = 4
    rows = tok.shape[0]
    half = rows // 2
    qw = QT.shape[0]
    heads = qw // HEAD_DIM
    cw = O.shape[1] // n_ctx
    scale = HEAD_DIM ** (-0.5)

    p.barrier()

    gain_line = LineGather(p, gains, G8, line_sems.at[0])
    qkv_line = LineGather(p, wqkv_o, WQ, line_sems.at[1])
    out_line = LineGather(p, wout_o, WO, line_sems.at[2])
    gate_line = LineGather(p, wgate_o, wgate, line_sems.at[3])
    up_line = LineGather(p, wup_o, wup, line_sems.at[4])

    def row_block(ref):
        return (
            lambda c: ref.at[rows_at(c, rows)],
            lambda c, h: ref.at[pl.ds(pl.multiple_of(c * rows + h * half, half), half)],
        )

    tok_plane = PlaneGather(p, *row_block(X), plane_sems.at[0], own=tok)
    cot_plane = PlaneGather(p, *row_block(cot_all), plane_sems.at[1], own=cot)
    tab_rows = tab.shape[0]
    tab_plane = PlaneGather(
        p,
        lambda c: TAB.at[c],
        lambda c, h: TAB.at[c, pl.ds(h * (tab_rows // 2), tab_rows // 2)],
        plane_sems.at[2],
        own=tab,
    )

    def col_block(ref, b):
        def view(c):
            return ref.at[pl.ds(b * rows, rows), rows_at(c, cw)]

        def halves(c, h):
            return ref.at[pl.ds(b * rows + h * half, half), rows_at(c, cw)]

        return view, halves

    o_plane = [PlaneGather(p, *col_block(O, b), plane_sems.at[3 + b]) for b in range(n_ctx)]
    m_plane = [PlaneGather(p, *col_block(M, b), plane_sems.at[7 + b]) for b in range(n_ctx)]

    gain_line.start()
    qkv_line.start()
    tab_plane.start()
    tok_plane.start()
    out_line.start()
    own_tok = pltpu.make_async_copy(tok, X.at[rows_at(p.c, rows)], copy_sems.at[0])
    own_tab = pltpu.make_async_copy(tab, TAB.at[p.c], copy_sems.at[1])
    own_cot = pltpu.make_async_copy(cot, cot_all.at[rows_at(p.c, rows)], copy_sems.at[2])
    own_tok.start()
    own_tab.start()
    own_cot.start()

    gain_line.hop(1)
    tab_plane.middle()
    gain_line.hop(2)
    qkv_line.hop(1)
    gain_line.hop(3)
    gain_line.finish()
    for f in range(2 * p.depth):
        GROW[:, f * gains.shape[1] : (f + 1) * gains.shape[1]] = G8[16 * f : 16 * f + 8, :].astype(f32)

    def norm(c):
        at = rows_at(c, rows)
        x = X[at, :].astype(f32)
        r = lax.rsqrt(jnp.mean(x * x, axis=-1, keepdims=True) + eps_norm)
        XN[at, :] = (x * r * GROW[0:1, :]).astype(bf16)

    own_tok.wait()
    norm(p.c)
    out_line.hop(1)
    qkv_line.hop(2)
    tok_plane.middle()
    out_line.hop(2)
    gate_line.start()
    norm(p.cx)
    norm(p.cy)
    qkv_line.hop(3)
    tok_plane.finish()
    cot_plane.start()
    out_line.hop(3)
    up_line.start()
    norm(p.cd)
    x_copy = pltpu.make_async_copy(X, x_out, copy_sems.at[3])
    xn_copy = pltpu.make_async_copy(XN, xn_out, copy_sems.at[4])
    x_copy.start()
    xn_copy.start()
    own_tab.wait()
    tab_plane.finish()
    qkv_line.finish()

    @pl.loop(0, n_ctx)
    def _(b):
        at = rows_at(b, rows)
        pre = dot(XN[at, :], WQ[...]).T
        cosine = TAB[b, 0:32, :]
        sine = TAB[b, 32:64, :]
        for h in range(heads + 1):
            u = pre[64 * h : 64 * h + 32]
            w = pre[64 * h + 32 : 64 * h + 64]
            first = u * cosine - w * sine
            second = w * cosine + u * sine
            if h < heads:
                QT[64 * h : 64 * h + 32, at] = first.astype(bf16)
                QT[64 * h + 32 : 64 * h + 64, at] = second.astype(bf16)
            else:
                KT[0:32, at] = first.astype(bf16)
                KT[32:64, at] = second.astype(bf16)
                K[at, :] = jnp.concatenate([first, second], axis=0).T.astype(bf16)
        VT[:, at] = pre[qw + 64 :].astype(bf16)

    wq_copy = pltpu.make_async_copy(WQ, wqkv_out, copy_sems.at[5])
    wq_copy.start()
    gate_line.hop(1)

    def attend(b):
        n = (b + 1) * rows
        key = lax.broadcasted_iota(jnp.int32, (n, rows), 0)
        query = lax.broadcasted_iota(jnp.int32, (n, rows), 1) + b * rows
        begin = TAB[b, 64:65, :].astype(jnp.int32)
        BIAS[0:n, :] = jnp.where((key <= query) & (key >= begin), 0.0, neg_large)
        cols = slice(b * rows, (b + 1) * rows)

        @pl.loop(0, heads)
        def _(h):
            head = rows_at(h, HEAD_DIM)
            s = dot(K[0:n, :], QT[head, cols]) * scale + BIAS[0:n, :]
            top = jnp.max(s, axis=0, keepdims=True)
            e = jnp.exp(s - top)
            total = jnp.sum(e, axis=0, keepdims=True)
            probs = (e * (1.0 / total)).astype(bf16)
            OT[head, :] = dot(VT[:, 0:n], probs)
            LSE[rows_at(h, 8), cols] = jnp.broadcast_to(top + jnp.log(total), (8, rows))

        O[pl.ds(b * rows, rows), rows_at(p.c, cw)] = OT[...].T.astype(bf16)
        o_plane[b].start()

    def middle(b):
        at = pl.ds(b * rows, rows)
        mine = rows_at(p.c, cw)
        mid = X[at, mine].astype(f32) + dot(O[at, :], WO[...])
        M[at, mine] = mid.astype(bf16)
        m_plane[b].start()

    attend(0)
    attend(1)
    o_plane[0].middle()
    attend(2)
    o_plane[1].middle()
    attend(3)
    o_plane[2].middle()
    cot_plane.middle()
    out_line.finish()
    o_plane[0].finish()
    middle(0)
    o_plane[3].middle()
    up_line.hop(1)
    o_plane[1].finish()
    middle(1)
    m_plane[0].middle()
    o_plane[2].finish()
    middle(2)
    m_plane[1].middle()
    gate_line.hop(2)
    o_plane[3].finish()
    middle(3)
    m_plane[2].middle()
    up_line.hop(2)
    m_plane[3].middle()
    copies = [x_copy, xn_copy, wq_copy]
    for i, (src, dst) in enumerate(
        ((QT, qt_out), (KT, kt_out), (VT, vt_out), (LSE, lse_out), (O, o_out), (WO, wout_out), (TAB, tab_out))
    ):
        copy = pltpu.make_async_copy(src, dst, copy_sems.at[6 + i])
        copy.start()
        copies.append(copy)
    for b in range(n_ctx):
        m_plane[b].finish()
    m_copy = pltpu.make_async_copy(M, m_out, copy_sems.at[13])
    m_copy.start()
    copies.append(m_copy)
    gate_line.hop(3)
    up_line.hop(3)
    cot_plane.finish()
    gate_line.finish()
    up_line.finish()
    own_cot.wait()
    for copy in copies:
        copy.wait()
    for line in (gain_line, qkv_line, out_line, gate_line, up_line):
        line.drain()
    for plane in [tok_plane, cot_plane, tab_plane] + o_plane + m_plane:
        plane.drain()


def forward_stage(tok, tab, gains, wqkv_o, wout_o, wgate_o, wup_o, cot):
    n_fsdp, n_ctx = lax.axis_size("fsdp"), lax.axis_size("ctx")
    rows, width = tok.shape
    seq = rows * n_ctx
    whole = n_fsdp * wqkv_o.shape[0]
    nq, nw, nu = wqkv_o.shape[1], wout_o.shape[1], wgate_o.shape[1]
    qw = HEADS // n_ctx * HEAD_DIM
    heads = qw // HEAD_DIM
    tab_shape = (n_ctx,) + tab.shape
    outs = [
        ((seq, width), bf16), ((seq, width), bf16), ((qw, seq), bf16), ((64, seq), bf16), ((64, seq), bf16),
        ((8 * heads, seq), f32), ((seq, width), bf16), ((seq, width), bf16), ((whole, nq), bf16),
        ((whole, nw), bf16), ((whole, nu), bf16), ((whole, nu), bf16), ((seq, width), bf16), (tab_shape, f32),
    ]
    scratch = [
        pltpu.VMEM((seq, width), bf16),
        pltpu.VMEM((seq, width), bf16),
        pltpu.VMEM((qw, seq), bf16),
        pltpu.VMEM((64, seq), bf16),
        pltpu.VMEM((64, seq), bf16),
        pltpu.VMEM((seq, 64), bf16),
        pltpu.VMEM((8 * heads, seq), f32),
        pltpu.VMEM((seq, width), bf16),
        pltpu.VMEM((seq, width), bf16),
        pltpu.VMEM((whole, nq), bf16),
        pltpu.VMEM((whole, nw), bf16),
        pltpu.VMEM(tab_shape, f32),
        pltpu.VMEM((16 * n_fsdp, gains.shape[1]), bf16),
        pltpu.VMEM((8, width), f32),
        pltpu.VMEM((seq, rows), f32),
        pltpu.VMEM((qw, rows), f32),
        pltpu.SemaphoreType.DMA((5, LineGather.SEMS)),
        pltpu.SemaphoreType.DMA((11, PlaneGather.SEMS)),
        pltpu.SemaphoreType.DMA((14,)),
    ]
    ins = (tok, tab, gains, wqkv_o, wout_o, wgate_o, wup_o, cot)
    flops = 2 * seq * width * (nq + nw) + 8 * heads * seq * seq * HEAD_DIM
    return call(forward_kernel, ins, outs, scratch, 1, flops, "forward_stage")


middle_stage = None

backward_stage = None

def rotate(field, cosine, sine_table, direction):
    half_width = field.shape[-1] // 2
    first_half = field[..., :half_width]
    second_half = field[..., half_width:]
    return jnp.concatenate(
        [
            first_half * cosine - direction * second_half * sine_table,
            second_half * cosine + direction * first_half * sine_table,
        ],
        axis=-1,
    )


def gather(x, axis_name, axis=0):
    return lax.all_gather(x, axis_name, axis=axis, tiled=True)


def scatter(x, axis_name, axis=0):
    return lax.psum_scatter(x.astype(bf16), axis_name, scatter_dimension=axis, tiled=True)


def columns(w, start, count):
    return lax.dynamic_slice_in_dim(w, start, count, axis=1)


def visible(begin):
    seq = begin.shape[0]
    index = jnp.arange(seq, dtype=jnp.int32)
    return (index[None, :] <= index[:, None]) & (index[None, :] >= begin[:, None])


def forward_plain(tok, tab, gains, wqkv_o, wout_o, wgate_o, wup_o, cot):
    n_ctx = lax.axis_size("ctx")
    c = lax.axis_index("ctx")
    x = gather(tok, "ctx")
    tabs = gather(tab[None], "ctx")
    wqkv = gather(wqkv_o, "fsdp")
    wout = gather(wout_o, "fsdp")
    wgate = gather(wgate_o, "fsdp")
    wup = gather(wup_o, "fsdp")
    cot_all = gather(cot, "ctx")
    gain = gather(gains[0:1], "fsdp", axis=1).astype(f32)
    xf = x.astype(f32)
    r = lax.rsqrt(jnp.mean(xf * xf, axis=-1, keepdims=True) + eps_norm)
    xn = (xf * r * gain).astype(bf16)
    seq, width = x.shape
    heads = HEADS // n_ctx
    qw = heads * HEAD_DIM
    pre = dot(xn, wqkv)
    cosine = tabs[:, 0:32].transpose(0, 2, 1).reshape(seq, 1, 32)
    sine = tabs[:, 32:64].transpose(0, 2, 1).reshape(seq, 1, 32)
    begin = tabs[:, 64].reshape(seq).astype(jnp.int32)
    kvw = (wqkv.shape[1] - qw) // 2
    kv = kvw // HEAD_DIM
    q = rotate(pre[:, :qw].reshape(seq, heads, HEAD_DIM), cosine, sine, 1.0).astype(bf16)
    k = rotate(pre[:, qw : qw + kvw].reshape(seq, kv, HEAD_DIM), cosine, sine, 1.0).astype(bf16)
    v = pre[:, qw + kvw :].astype(bf16).reshape(seq, kv, HEAD_DIM)
    qg = q.reshape(seq, kv, heads // kv, HEAD_DIM)
    scores = jnp.einsum("qkgd,lkd->kgql", qg, k, preferred_element_type=f32) * HEAD_DIM ** (-0.5)
    scores = jnp.where(visible(begin)[None, None], scores, neg_large)
    top = jnp.max(scores, axis=-1, keepdims=True)
    weights = jnp.exp(scores - top)
    total = jnp.sum(weights, axis=-1, keepdims=True)
    probs_low = (weights / total).astype(bf16)
    att = jnp.einsum("kgql,lkd->qkgd", probs_low, v, preferred_element_type=f32)
    o = gather(att.astype(bf16).reshape(seq, qw), "ctx", axis=1)
    lse = (top + jnp.log(total)).reshape(heads, 1, seq)
    lse = jnp.broadcast_to(lse, (heads, 8, seq)).reshape(8 * heads, seq)
    cw = width // n_ctx
    mid = columns(x, c * cw, cw).astype(f32) + dot(o, wout)
    m = gather(mid.astype(bf16), "ctx", axis=1)
    qt = q.reshape(seq, qw).T
    kt = k.reshape(seq, kvw).T
    vt = v.reshape(seq, kvw).T
    return x, xn, qt, kt, vt, lse, o, m, wqkv, wout, wgate, wup, cot_all, tabs


def middle_plain(m, cot_all, wgate, wup, wdown_o):
    n_ctx = lax.axis_size("ctx")
    c = lax.axis_index("ctx")
    seq, width = m.shape
    rows = seq // n_ctx
    cw = width // n_ctx
    wdown = gather(wdown_o, "fsdp")
    mf = m.astype(f32)
    r = lax.rsqrt(jnp.mean(mf * mf, axis=-1, keepdims=True) + eps_norm)
    gate = dot(m, wgate) * r
    up = dot(m, wup) * r
    sig = jax.nn.sigmoid(gate)
    hidden = (gate * sig * up).astype(bf16)
    mlp = scatter(dot(hidden, wdown), "ctx").astype(f32)
    mid_rows = lax.dynamic_slice_in_dim(m, c * rows, rows, axis=0).astype(f32)
    output = (mid_rows + mlp).astype(bf16)
    grad_hidden = dot_nt(cot_all, wdown)
    down_raw = scatter(dot_tn(hidden, cot_all), "fsdp")
    d_gate = grad_hidden * up * sig * (1.0 + gate * (1.0 - sig))
    d_up = grad_hidden * gate * sig
    stat = jnp.sum(d_gate * gate + d_up * up, axis=-1, keepdims=True)
    d_gate = (d_gate * r).astype(bf16)
    d_up = (d_up * r).astype(bf16)
    gate_raw = dot_tn(m, d_gate).astype(bf16)
    up_raw = dot_tn(m, d_up).astype(bf16)
    back = dot_nt(d_gate, wgate) + dot_nt(d_up, wup) - mf * (r * r * stat * (1.0 / width))
    back_own = scatter(back, "ctx", axis=1).astype(f32)
    gm = (columns(cot_all, c * cw, cw).astype(f32) + back_own).astype(bf16)
    return output, down_raw, gate_raw, up_raw, gm


def backward_plain(x, xn, gain, qt, kt, vt, lse, o, gm, wqkv, wout, tabs, gate_raw, up_raw):
    n_ctx = lax.axis_size("ctx")
    c = lax.axis_index("ctx")
    seq, width = x.shape
    heads = HEADS // n_ctx
    qw = heads * HEAD_DIM
    kvw = kt.shape[0]
    kv = kvw // HEAD_DIM
    cw = width // n_ctx
    scale = HEAD_DIM ** (-0.5)
    cosine = tabs[:, 0:32].transpose(0, 2, 1).reshape(seq, 1, 32)
    sine = tabs[:, 32:64].transpose(0, 2, 1).reshape(seq, 1, 32)
    begin = tabs[:, 64].reshape(seq).astype(jnp.int32)
    gate_grad = scatter(gate_raw, "fsdp")
    up_grad = scatter(up_raw, "fsdp")
    out_grad = scatter(dot_tn(o, gm), "fsdp")
    d_att = scatter(dot_nt(gm, wout), "ctx", axis=1).reshape(seq, kv, heads // kv, HEAD_DIM)
    q = qt.T.reshape(seq, kv, heads // kv, HEAD_DIM)
    k = kt.T.reshape(seq, kv, HEAD_DIM)
    v = vt.T.reshape(seq, kv, HEAD_DIM)
    scores = jnp.einsum("qkgd,lkd->kgql", q, k, preferred_element_type=f32) * scale
    scores = jnp.where(visible(begin)[None, None], scores, neg_large)
    lse = lse.reshape(kv, heads // kv, 8, seq)[:, :, 0, :, None]
    probs = jnp.exp(scores - lse)
    d_probs = jnp.einsum("qkgd,lkd->kgql", d_att, v, preferred_element_type=f32)
    delta = jnp.sum(probs * d_probs, axis=-1, keepdims=True)
    d_scores = (probs * (d_probs - delta)).astype(bf16)
    d_q = jnp.einsum("kgql,lkd->qkgd", d_scores, k, preferred_element_type=f32) * scale
    d_k = jnp.einsum("kgql,qkgd->lkd", d_scores, q, preferred_element_type=f32) * scale
    d_v = jnp.einsum("kgql,qkgd->lkd", probs.astype(bf16), d_att, preferred_element_type=f32)
    stat = (
        jnp.sum(d_q * q, axis=(1, 2, 3)) + jnp.sum(d_k * k, axis=(1, 2)) + jnp.sum(d_v * v, axis=(1, 2))
    )[:, None]
    d_q = rotate(d_q.reshape(seq, heads, HEAD_DIM), cosine, sine, -1.0).reshape(seq, qw)
    d_k = rotate(d_k, cosine, sine, -1.0).reshape(seq, kvw)
    d_pre = jnp.concatenate([d_q, d_k, d_v.reshape(seq, kvw)], axis=1).astype(bf16)
    qkv_grad = scatter(dot_tn(xn, d_pre), "fsdp")
    xf = x.astype(f32)
    r = lax.rsqrt(jnp.mean(xf * xf, axis=-1, keepdims=True) + eps_norm)
    back = dot_nt(d_pre, wqkv) * (gain * r) - xf * (r * r * stat * (1.0 / width))
    at = (jnp.arange(width, dtype=jnp.int32) // cw == c)[None, :]
    back = back + jnp.where(at, jnp.tile(gm.astype(f32), (1, n_ctx)), 0.0)
    grad_tokens = scatter(back, "ctx").astype(f32)
    qkv_all = gather(qkv_grad[None], "ctx")
    out_all = gather(out_grad, "ctx", axis=1)
    gate_all = gather(gate_grad[None], "ctx")
    up_all = gather(up_grad[None], "ctx")
    return grad_tokens, qkv_all, out_all, gate_all, up_all


def per_device(
    tokens,
    positions,
    gain_attn,
    gain_mlp,
    w_query,
    w_key,
    w_value,
    w_out,
    w_gate,
    w_up,
    w_down,
    cotangent,
):
    n_ctx = lax.axis_size("ctx")
    n_fsdp = lax.axis_size("fsdp")
    kernels = n_ctx == 4 and n_fsdp == 8
    c = lax.axis_index("ctx")
    rows, width = tokens.shape
    own_rows = w_query.shape[0]
    qw = HEADS // n_ctx * HEAD_DIM
    copies = max(1, n_ctx // KV_HEADS)
    kvw = max(1, KV_HEADS // n_ctx) * HEAD_DIM
    cw = width // n_ctx
    ff_width = w_gate.shape[1]
    unit = ff_width // (n_fsdp * n_ctx)
    gain_one = gain_attn.astype(f32)[:, None]
    gain_two = gain_mlp.astype(f32)[:, None]

    wqkv_o = jnp.concatenate(
        [
            columns(w_query, c * qw, qw),
            columns(w_key, (c // copies) * kvw, kvw),
            columns(w_value, (c // copies) * kvw, kvw),
        ],
        axis=1,
    )
    wout_o = columns(w_out, c * cw, cw)

    def units(w):
        parts = w.reshape(own_rows, n_fsdp, n_ctx, unit)
        mine = lax.dynamic_index_in_dim(parts, c, axis=2, keepdims=False)
        return (gain_two * mine.reshape(own_rows, n_fsdp * unit)).astype(bf16)

    wgate_o, wup_o = units(w_gate), units(w_up)
    wdown_o = lax.dynamic_slice_in_dim(w_down, c * unit, unit, axis=0)
    gains = jnp.broadcast_to(gain_attn[None, :], (16, own_rows))
    frequency = theta_base ** (-(jnp.arange(HEAD_DIM // 2, dtype=f32) * 2.0) / HEAD_DIM)
    angles = frequency[:, None] * positions.astype(f32)[None, :]
    begin = c * rows + jnp.arange(rows, dtype=jnp.int32) - positions
    tab = jnp.concatenate(
        [jnp.cos(angles), jnp.sin(angles), jnp.broadcast_to(begin.astype(f32)[None, :], (16, rows))],
        axis=0,
    )

    forward = forward_stage if kernels else forward_plain
    x, xn, qt, kt, vt, lse, o, m, wqkv, wout, wgate, wup, cot_all, tabs = forward(
        tokens, tab, gains, wqkv_o, wout_o, wgate_o, wup_o, cotangent
    )
    middle = middle_plain
    output, down_raw, gate_raw, up_raw, gm = middle(m, cot_all, wgate, wup, wdown_o)
    gain_row = gather(gain_attn, "fsdp").astype(f32)[None, :]
    backward = backward_plain
    grad_tokens, qkv_all, out_all, gate_all, up_all = backward(
        x, xn, gain_row, qt, kt, vt, lse, o, gm, wqkv, wout, tabs, gate_raw, up_raw
    )

    qkv_all = qkv_all.astype(f32)

    def joined(part):
        return jnp.moveaxis(part, 0, 1).reshape(own_rows, -1)

    def kv_part(part):
        return joined(part.reshape(n_ctx // copies, copies, own_rows, kvw).sum(axis=1))

    grad_query = joined(qkv_all[:, :, :qw])
    grad_key = kv_part(qkv_all[:, :, qw : qw + kvw])
    grad_value = kv_part(qkv_all[:, :, qw + kvw :])
    grad_out = out_all.astype(f32)

    def spread(full):
        full = full.reshape(n_ctx, own_rows, n_fsdp, unit)
        return full.transpose(1, 2, 0, 3).reshape(own_rows, ff_width).astype(f32)

    raw_gate, raw_up = spread(gate_all), spread(up_all)
    grad_down = gather(down_raw, "ctx").astype(f32) if down_raw.shape[0] == unit else down_raw.astype(f32)

    def gain_term(grad, w):
        return jnp.sum(grad * w.astype(f32), axis=1)

    grad_gain_one = (
        gain_term(grad_query, w_query) + gain_term(grad_key, w_key) + gain_term(grad_value, w_value)
    ) / gain_one[:, 0]
    grad_gain_two = gain_term(raw_gate, w_gate) + gain_term(raw_up, w_up)
    return (
        output,
        grad_tokens,
        grad_gain_one,
        grad_gain_two,
        grad_query,
        grad_key,
        grad_value,
        grad_out,
        gain_two * raw_gate,
        gain_two * raw_up,
        grad_down,
    )


def solution(mesh):
    both = P(("fsdp", "ctx"), None)
    first = P("fsdp", None)
    return jax.shard_map(
        per_device,
        mesh=mesh,
        in_specs=(both, P(("fsdp", "ctx")), P("fsdp"), P("fsdp")) + (first,) * 7 + (both,),
        out_specs=(both, both, P("fsdp"), P("fsdp")) + (first,) * 7,
        check_vma=False,
    )
```

time: 1250 us -> 993 us (0.79)
  waiting for transfers between devices: 781 us -> 397 us
  Pallas kernels: 0 us -> 181 us
  matrix products: 250 us -> 211 us
  other arithmetic: 88 us -> 74.5 us
    all_gather x14 -> x6, waiting for transfers between devices: 492 us -> 123 us  [gather(): return lax.all_gather(x, axis_name, axis=axis, tiled=True)]
    pallas_call x0 -> x1, Pallas kernels: none -> 181 us  [call(): pl.pallas_call(kernel, out_shape=[jax.ShapeDtypeStruct(s, d) for s, d in...]
    dot_general x6 -> x5, matrix products: 92.2 us -> 73.6 us  [the longest x1 24.7 us: backward_plain(): d_probs = jnp.einsum('qkgd,lkd->kgql', d_att, v, preferred_element_type=f32)]
    dot_general x5 -> x3, matrix products: 51.5 us -> 37.3 us  [dot(): return jnp.dot(a, b, preferred_element_type=f32)]
    reduce_scatter x9, waiting for transfers between devices: 286 us -> 273 us  [scatter(): lax.psum_scatter(x.astype(bf16), axis_name, scatter_dimension=axis, tiled...]
    reduce_sum x4 -> x5, other arithmetic: 21.7 us -> 9.16 us  [the longest x1 3.18 us: backward_plain(): r = lax.rsqrt(jnp.mean(xf * xf, axis=-1, keepdims=True) + eps_norm)]
    another operation x2 -> x3, other arithmetic: 30.4 us -> 29.5 us
    unnamed x98 -> x79, local copies, waits for them, and re-layouts: 39 us -> 38.7 us
  transfers between devices with their start and end apart: 23 -> 15, of which waited for: 20 -> 11; matrix products, arithmetic and copies ran while one was open for 30% -> 32% of each run, Pallas kernels for 0% -> 18%
where the time goes in v2:
time: 993 us; the launch traced here: 986 us
  waiting for transfers between devices  397 us (40%)
  matrix products  211 us (21%)
  Pallas kernels  181 us (18%)
  local copies, waits for them, and re-layouts  94.4 us (10%)
  other arithmetic  74.5 us (8%)
  between operations  14.7 us (1%)
  blocking collectives  12.8 us (1%)
    reduce_scatter x9, waiting for transfers between devices, scatter(): lax.psum_scatter(x.astype(bf16), axis_name, scatter_dimension=axis, tiled...  273 us
    pallas_call x1, Pallas kernels, call(): pl.pallas_call(kernel, out_shape=[jax.ShapeDtypeStruct(s, d) for s, d in...  181 us
    all_gather x6, waiting for transfers between devices, gather(): return lax.all_gather(x, axis_name, axis=axis, tiled=True)  123 us
    dot_general x5, matrix products, dot_nt(): lax.dot_general(a, b, (((1,), (1,)), ((), ())), preferred_element_type=f32)  50.9 us
    dot_general x5, matrix products, dot_tn(): lax.dot_general(a, b, (((0,), (0,)), ((), ())), preferred_element_type=f32)  49 us
    unnamed x79, local copies, waits for them, and re-layouts  38.7 us
    dot_general x3, matrix products, dot(): return jnp.dot(a, b, preferred_element_type=f32)  37.3 us
    convert_element_type x6, local copies, waits for them, and re-layouts, spread(): return full.transpose(1, 2, 0, 3).reshape(own_rows, ff_width).astype(f32)  36 us
  transfers between devices with their start and end apart: 15, of which 11 were waited for; matrix products, arithmetic and copies ran while one was open for 32% of the time, Pallas kernels for 18%

profile of v2, /device:TPU:8, one launch (start us, length us, event | category | flops | bytes accessed | tf_op | source)
XLA Modules:
  0.0 986.2 jit_solution(2770476862494953950)
XLA Ops:
  35.2 180.8 %forward_stage.1 = (bf16[1024,2048]{1,0:T(8,128)(2,1)}, bf16[1024,2048]{1,0:T(8,128)(2,1)}, bf16[512,1024]{1,0:T(8,128)(2,1)}, bf16[64,1024]{1,0:T(8,128)(2,1)},...) custom-call(bf16[256,2048]{1,0:T(8,128)(2,1)} %tok.1, ...), custom_call_target="tpu_custom_call" | custom-call | flops 9126805504 | bytes 67108864 | tf_op jit(solution)/shard_map/forward_stage/pallas_call | solution.py:254
  219.0 11.7 %fusion.48 = f32[1024,1408]{1,0:T(8,128)} fusion(bf16[1024,2048]{1,0:T(8,128)(2,1)} %get-tuple-element.25, bf16[2048,1408]{1,0:T(8,128)(2,1)} %get-tuple-element.26), kind=kOutput, calls=%fused_computation.121 | convolution fusion | flops 5905580032 | bytes 15728640 | tf_op jit(solution)/shard_map/dot_general | solution.py:21
  230.7 11.9 %fusion.49 = f32[1024,1408]{1,0:T(8,128)} fusion(bf16[1024,2048]{1,0:T(8,128)(2,1)} %get-tuple-element.33, bf16[1408,2048]{1,0:T(8,128)(2,1)} %all-gather.11.cloned.1.call-done), kind=kOutput, calls=%fused_computation.122 | convolution fusion | flops 5905580032 | bytes 15728640 | tf_op jit(solution)/shard_map/dot_general | solution.py:25
  242.6 14.7 %add_reduce_fusion = (f32[1024]{0:T(1024)S(1)}, f32[1024,1408]{1,0:T(8,128)S(1)}, bf16[1024,1408]{1,0:T(8,128)(2,1)}) fusion(f32[1024,1408]{1,0:T(8,128)} %fusion.48, f32[1024]{0:T(1024)S(1)} %add_rsqrt_fusion.1, f32[1024,1408]{1,0:T(8,128)} %fusion.49, bf16[1024,2048]{1,0:T(8,128)(2,1)S(1)} %copy-done.7, bf16[2048,1408]{1,0:T(8,128)(2,1)} %get-tuple-element.27), kind=kOutput, calls=%fused_computation.33 | convolution fusion | flops 5934414848 | bytes 30154752 | tf_op jit(solution)/shard_map/dot_general | solution.py:21
  259.7 9.1 fusion.43
  268.8 16.4 %fusion.13 = bf16[1024,2048]{1,0:T(8,128)(2,1)} fusion(bf16[1024,2048]{1,0:T(8,128)(2,1)} %get-tuple-element.25, f32[1024,2048]{1,0:T(8,128)} %fusion.43, f32[1024]{0:T(1024)S(1)} %multiply_multiply_fusion.2, bf16[2048,1408]{1,0:T(8,128)(2,1)} %get-tuple-element.27, f32[1024]{0:T(1024)S(1)} %add_rsqrt_fusion.1, f32[1024,1408]{1,0:T(8,128)} %fusion.49, ...), kind=kOutput, calls=%fused_computation.19 | convolution fusion | flops 5927600128 | bytes 34086912 | tf_op jit(solution)/shard_map/dot_general | solution.py:25
  285.3 54.2 %reduce-scatter.12.cloned.1.call-done = bf16[1024,512]{1,0:T(8,128)(2,1)} async-done(((bf16[1024,2048]{1,0:T(8,128)(2,1)}), bf16[1024,512]{1,0:T(8,128)(2,1)}) %reduce-scatter.12.cloned.1.call-update) | async-done | bytes 1048592 | tf_op jit(solution)/shard_map/reduce_scatter | solution.py:537
  353.9 15.4 %convolution_convert_fusion.1 = bf16[2048,1408]{1,0:T(8,128)(2,1)} fusion(bf16[1024,2048]{1,0:T(8,128)(2,1)} %get-tuple-element.25, f32[1024]{0:T(1024)S(1)} %add_rsqrt_fusion.1, f32[1024,1408]{1,0:T(8,128)} %fusion.49, f32[1024,1408]{1,0:T(8,128)} %fusion.48), kind=kOutput, calls=%fused_computation.25 | convolution fusion | flops 5919997952 | bytes 21499904 | tf_op jit(solution)/shard_map/dot_general | solution.py:29
  369.4 12.1 %convolution_convert_fusion.2 = bf16[2048,1408]{1,0:T(8,128)(2,1)} fusion(bf16[1024,2048]{1,0:T(8,128)(2,1)} %get-tuple-element.25, f32[1024,1408]{1,0:T(8,128)} %copy-done.29, f32[1024]{0:T(1024)S(1)} %add_rsqrt_fusion.1), kind=kOutput, calls=%fused_computation.26 | convolution fusion | flops 5911347200 | bytes 15732736 | tf_op jit(solution)/shard_map/dot_general | solution.py:29
  383.7 13.4 %fusion.33 = f32[1024,1024,8]{1,0,2:T(8,128)} fusion(bf16[1024,8,64]{0,2,1:T(8,128)(2,1)S(1)} %bitcast.199, bf16[64,1024]{1,0:T(8,128)(2,1)S(1)} %copy-done.13), kind=kOutput, calls=%fused_computation.78 | convolution fusion | flops 1073741824 | bytes 34734080 | tf_op jit(solution)/shard_map/qkgd,lkd->kgql/dot_general | solution.py:647
  397.1 8.0 convolution_convert_fusion
  407.9 24.7 %fusion.2 = (f32[8,1024]{1,0:T(8,128)S(1)}, f32[1024,1024,8]{1,0,2:T(8,128)}) fusion(f32[1024,1024,8]{1,0,2:T(8,128)} %fusion.33, f32[8,1024]{1,0:T(8,128)S(1)} %bitcast.210, pred[1024,1024]{0,1:T(8,128)(4,1)S(1)} %fusion.20, bf16[1024,8,64]{0,2,1:T(8,128)(2,1)} %bitcast.206, bf16[64,1024]{1,0:T(8,128)(2,1)S(1)} %copy-done.21), kind=kOutput, calls=%fused_computation.5 | convolution fusion | flops 1115676672 | bytes 69402624 | tf_op jit(solution)/shard_map/qkgd,lkd->kgql/dot_general | solution.py:651
  432.6 29.2 %fusion.7 = bf16[8,1024,1024]{1,2,0:T(8,128)(2,1)} fusion(f32[1024,1024,8]{1,0,2:T(8,128)} %get-tuple-element.90, f32[1024,1024,8]{1,0,2:T(8,128)} %fusion.33, f32[8,1024]{1,0:T(8,128)S(1)} %get-tuple-element.89, f32[8,1024]{1,0:T(8,128)S(1)} %bitcast.211, pred[1024,1024]{0,1:T(8,128)(4,1)S(1)} %fusion.20), kind=kLoop, calls=%fused_computation.10 | loop fusion | flops 50331648 | bytes 85000192 | tf_op jit(solution)/shard_map/reshape.12
  461.8 11.1 %fusion.28 = (f32[1024]{0:T(1024)S(1)}, f32[1024,1,64]{0,2,1:T(8,128)S(1)}) fusion(bf16[64,1024]{1,0:T(8,128)(2,1)S(1)} %copy-done.13, bf16[1024,8,64]{0,2,1:T(8,128)(2,1)S(1)} %bitcast.200, bf16[8,1024,1024]{1,2,0:T(8,128)(2,1)} %fusion.7), kind=kOutput, calls=%fused_computation.70 | convolution fusion | flops 1074002944 | bytes 18223104 | tf_op jit(solution)/shard_map/kgql,qkgd->lkd/dot_general | solution.py:655
  473.0 9.1 fusion.21
  483.6 15.3 %convert_bitcast_fusion = (bf16[1024,64]{0,1:T(8,128)(2,1)S(1)}, f32[1024]{0:T(1024)S(1)}) fusion(bf16[64,1024]{1,0:T(8,128)(2,1)S(1)} %copy-done.21, bf16[1024,8,64]{0,2,1:T(8,128)(2,1)S(1)} %bitcast.207, f32[1024,1024,8]{1,0,2:T(8,128)} %fusion.33, f32[8,1024]{1,0:T(8,128)S(1)} %bitcast.212, pred[1024,1024]{0,1:T(8,128)(4,1)S(1)} %fusion.20), kind=kOutput, calls=%fused_computation.80 | convolution fusion | flops 1107557376 | bytes 35950592 | tf_op jit(solution)/shard_map/kgql,qkgd->lkd/dot_general | solution.py:656
  499.0 7.6 convolution_convert_fusion.5
  506.6 11.0 %convolution_convert_fusion.4 = bf16[1024,2048]{1,0:T(8,128)(2,1)} fusion(bf16[1024,1408]{1,0:T(8,128)(2,1)} %get-tuple-element.63, bf16[1408,2048]{1,0:T(8,128)(2,1)} %all-gather.11.cloned.1.call-done), kind=kOutput, calls=%fused_computation.44 | convolution fusion | flops 5907677184 | bytes 12845056 | tf_op jit(solution)/shard_map/dot_general | solution.py:21
  519.0 49.4 %reduce-scatter.20.cloned.1.call-done = bf16[256,1408]{1,0:T(8,128)(2,1)} async-done(((bf16[2048,1408]{1,0:T(8,128)(2,1)}), bf16[256,1408]{1,0:T(8,128)(2,1)}) %reduce-scatter.20.cloned.1.call-update) | async-done | bytes 720912 | tf_op jit(solution)/shard_map/reduce_scatter | solution.py:537
  568.5 66.1 %reduce-scatter.26.cloned.1.call-done = bf16[176,2048]{1,0:T(8,128)(2,1)} async-done(((bf16[1408,2048]{1,0:T(8,128)(2,1)}), bf16[176,2048]{1,0:T(8,128)(2,1)}) %reduce-scatter.26.cloned.1.call-update) | async-done | bytes 720912 | tf_op jit(solution)/shard_map/reduce_scatter | solution.py:537
  634.6 37.0 %reduce-scatter.18.cloned.1.call-done = bf16[256,640]{1,0:T(8,128)(2,1)} async-done(((bf16[2048,640]{1,0:T(8,128)(2,1)}), bf16[256,640]{1,0:T(8,128)(2,1)}) %reduce-scatter.18.cloned.1.call-update) | async-done | bytes 327696 | tf_op jit(solution)/shard_map/reduce_scatter | solution.py:537
  671.7 12.8 %all-gather.3 = bf16[8,1,256]{2,1,0:T(2,128)(2,1)S(1)} all-gather(bf16[1,1,256]{2,1,0:T(2,128)(2,1)S(1)} %reshape.302), channel_id=1, replica_groups=mesh['fsdp'=8,'ctx'=4] {'fsdp'}, dimensions={0}, use_global_device_ids=true | all-gather | bytes 4608 | tf_op jit(solution)/shard_map/all_gather | solution.py:533
  692.2 8.0 copy.98
  700.3 7.1 fusion.17
  708.3 22.1 %reduce-scatter.10.cloned.1.call-done = bf16[256,2048]{1,0:T(8,128)(2,1)} async-done(((bf16[1024,2048]{1,0:T(8,128)(2,1)}), bf16[256,2048]{1,0:T(8,128)(2,1)}) %reduce-scatter.10.cloned.1.call-update) | async-done | bytes 1048592 | tf_op jit(solution)/shard_map/reduce_scatter | solution.py:537
  733.4 25.4 %all-gather.13.cloned.1.call-done = bf16[256,2048]{1,0:T(8,128)(2,1)} async-done(((bf16[256,512]{1,0:T(8,128)(2,1)}), bf16[256,2048]{1,0:T(8,128)(2,1)}) %all-gather.13.cloned.1.call-update) | async-done | bytes 1048592 | tf_op jit(solution)/shard_map/all_gather | solution.py:533
  761.6 41.1 %all-gather.21.cloned.1.call-done = bf16[1024,1408]{1,0:T(8,128)(2,1)} async-done(((bf16[256,1408]{1,0:T(8,128)(2,1)}), bf16[1024,1408]{1,0:T(8,128)(2,1)}) %all-gather.21.cloned.1.call-update) | async-done | bytes 2883600 | tf_op jit(solution)/shard_map/all_gather | solution.py:533
  807.8 7.9 reshape.293
  821.8 24.5 %all-gather.19.cloned.1.call-done = bf16[1024,1408]{1,0:T(8,128)(2,1)} async-done(((bf16[256,1408]{1,0:T(8,128)(2,1)}), bf16[1024,1408]{1,0:T(8,128)(2,1)}) %all-gather.19.cloned.1.call-update) | async-done | bytes 2883600 | tf_op jit(solution)/shard_map/all_gather | solution.py:533
  851.5 7.8 reshape.292
  895.3 25.6 %all-gather.17.cloned.1.call-done = bf16[1024,640]{1,0:T(8,128)(2,1)} async-done(((bf16[256,640]{1,0:T(8,128)(2,1)}), bf16[1024,640]{1,0:T(8,128)(2,1)}) %all-gather.17.cloned.1.call-update) | async-done | bytes 1310736 | tf_op jit(solution)/shard_map/all_gather | solution.py:533
  932.9 43.8 %reduce-scatter.16.cloned.1.call-done = bf16[256,2048]{1,0:T(8,128)(2,1)} async-done(((bf16[1024,2048]{1,0:T(8,128)(2,1)}), bf16[256,2048]{1,0:T(8,128)(2,1)}) %reduce-scatter.16.cloned.1.call-update) | async-done | bytes 1048592 | tf_op jit(solution)/shard_map/reduce_scatter | solution.py:537
  (175 shorter events, 137.3 us)
Async XLA Ops:
  7.2 223.5 %all-gather.11.cloned.1.call-start = ((), (), s32[]{:S(2)}) async-start(), calls=%async_computation.9 | async-start | bytes 6488064 | tf_op jit(solution)/shard_map/all_gather | solution.py:533
  10.0 329.5 %reduce-scatter.12.cloned.1.call-start = ((), (), s32[]{:S(2)}) async-start(), calls=%async_computation.11 | async-start | bytes 5242880 | tf_op jit(solution)/shard_map/reduce_scatter | solution.py:537
  10.7 22.5 %copy-start.22 = (f32[256]{0:T(256)}, f32[256]{0:T(256)S(1)}, u32[]{:S(2)}) copy-start(f32[256]{0:T(256)S(1)} %convert_element_type.198) | copy-start | bytes 3076
  13.8 11.5 %copy-start.2 = (bf16[256,5632]{0,1:T(8,128)(2,1)}, bf16[256,5632]{0,1:T(8,128)(2,1)S(1)}, u32[]{:S(2)}) copy-start(bf16[256,5632]{0,1:T(8,128)(2,1)S(1)} %copy.62) | copy-start | bytes 8650756
  21.1 8.5 copy-start.26
  21.1 9.3 copy-start.16
  21.2 9.3 copy-start.18
  25.3 9.2 copy-start.24
  230.7 11.9 %copy-start.7 = (bf16[1024,2048]{1,0:T(8,128)(2,1)S(1)}, bf16[1024,2048]{1,0:T(8,128)(2,1)}, u32[]{:S(2)}) copy-start(bf16[1024,2048]{1,0:T(8,128)(2,1)} %get-tuple-element.25) | copy-start | bytes 12582916
  230.7 29.0 %slice-start = ((s8[5767168]{0:T(1024)(128)(4,1)}), s8[4194304]{0:T(1024)(128)(4,1)S(1)}, s32[]{:S(2)}) async-start(s8[5767168]{0:T(1024)(128)(4,1)} %bitcast.220), calls=%async_computation.24 | async-start | bytes 8388608
  242.6 17.1 %slice-start.1 = ((s8[5767168]{0:T(1024)(128)(4,1)}), s8[1572864]{0:T(1024)(128)(4,1)S(1)}, s32[]{:S(2)}) async-start(s8[5767168]{0:T(1024)(128)(4,1)} %bitcast.220), calls=%async_computation.25 | async-start | bytes 3145728
  285.3 120.4 %reduce-scatter.14.cloned.1.call-start = ((), (), s32[]{:S(2)}) async-start(), calls=%async_computation.12 | async-start | bytes 5242880 | tf_op jit(solution)/shard_map/reduce_scatter | solution.py:537
  347.7 170.0 %reduce-scatter.24.cloned.1.call-start = ((), (), s32[]{:S(2)}) async-start(), calls=%async_computation.17 | async-start | bytes 2359296 | tf_op jit(solution)/shard_map/reduce_scatter | solution.py:537
  353.8 164.5 %reduce-scatter.22.cloned.1.call-start = ((), (), s32[]{:S(2)}) async-start(), calls=%async_computation.16 | async-start | bytes 6488064 | tf_op jit(solution)/shard_map/reduce_scatter | solution.py:537
  369.3 199.1 %reduce-scatter.20.cloned.1.call-start = ((), (), s32[]{:S(2)}) async-start(), calls=%async_computation.15 | async-start | bytes 6488064 | tf_op jit(solution)/shard_map/reduce_scatter | solution.py:537
  381.5 253.1 %reduce-scatter.26.cloned.1.call-start = ((), (), s32[]{:S(2)}) async-start(), calls=%async_computation.19 | async-start | bytes 6488064 | tf_op jit(solution)/shard_map/reduce_scatter | solution.py:537
  383.6 13.4 %copy-start.20 = (bf16[1024,2048]{1,0:T(8,128)(2,1)S(1)}, bf16[1024,2048]{1,0:T(8,128)(2,1)}, u32[]{:S(2)}) copy-start(bf16[1024,2048]{1,0:T(8,128)(2,1)} %get-tuple-element.33) | copy-start | bytes 12582916
  383.7 13.4 %copy-start.27 = (bf16[1024,1408]{1,0:T(8,128)(2,1)S(1)}, bf16[1024,1408]{1,0:T(8,128)(2,1)}, u32[]{:S(2)}) copy-start(bf16[1024,1408]{1,0:T(8,128)(2,1)} %get-tuple-element.63) | copy-start | bytes 8650756
  405.2 266.5 %reduce-scatter.18.cloned.1.call-start = ((), (), s32[]{:S(2)}) async-start(), calls=%async_computation.14 | async-start | bytes 2949120 | tf_op jit(solution)/shard_map/reduce_scatter | solution.py:537
  506.6 223.9 %reduce-scatter.10.cloned.1.call-start = ((), (), s32[]{:S(2)}) async-start(), calls=%async_computation.10 | async-start | bytes 5242880 | tf_op jit(solution)/shard_map/reduce_scatter | solution.py:537
  517.6 154.1 %copy-start.25 = (bf16[256]{0:T(256)(128)(2,1)S(1)}, bf16[256]{0:T(256)(128)(2,1)}, u32[]{:S(2)}) copy-start(bf16[256]{0:T(256)(128)(2,1)} %param.14) | copy-start | bytes 1540
  517.6 170.2 %copy-start.11 = (bf16[1024,512]{1,0:T(8,128)(2,1)S(1)}, bf16[1024,512]{1,0:T(8,128)(2,1)}, u32[]{:S(2)}) copy-start(bf16[1024,512]{1,0:T(8,128)(2,1)} %copy-done.10) | copy-start | bytes 3145732
  517.6 241.2 %all-gather.13.cloned.1.call-start = ((), (), s32[]{:S(2)}) async-start(), calls=%async_computation.18 | async-start | bytes 1310720 | tf_op jit(solution)/shard_map/all_gather | solution.py:533
  518.2 284.4 %all-gather.21.cloned.1.call-start = ((), (), s32[]{:S(2)}) async-start(), calls=%async_computation.23 | async-start | bytes 3604480 | tf_op jit(solution)/shard_map/all_gather | solution.py:533
  519.0 327.4 %all-gather.19.cloned.1.call-start = ((), (), s32[]{:S(2)}) async-start(), calls=%async_computation.22 | async-start | bytes 3604480 | tf_op jit(solution)/shard_map/all_gather | solution.py:533
  568.4 321.7 %all-gather.15.cloned.1.call-start = ((), (), s32[]{:S(2)}) async-start(), calls=%async_computation.20 | async-start | bytes 3604480 | tf_op jit(solution)/shard_map/all_gather | solution.py:533
  634.6 286.2 %all-gather.17.cloned.1.call-start = ((), (), s32[]{:S(2)}) async-start(), calls=%async_computation.21 | async-start | bytes 1638400 | tf_op jit(solution)/shard_map/all_gather | solution.py:533
  671.7 305.0 %reduce-scatter.16.cloned.1.call-start = ((), (), s32[]{:S(2)}) async-start(), calls=%async_computation.13 | async-start | bytes 5242880 | tf_op jit(solution)/shard_map/reduce_scatter | solution.py:537
  692.2 8.0 copy-start.12
  692.2 8.0 copy-start.14
  692.2 8.1 copy-start.28
  927.0 52.4 %copy-start.1 = (bf16[704,2048]{1,0:T(8,128)(2,1)S(1)}, bf16[704,2048]{1,0:T(8,128)(2,1)}, u32[]{:S(2)}) copy-start(bf16[704,2048]{1,0:T(8,128)(2,1)} %param.22) | copy-start | bytes 8650756
  (15 other events, 57.7 us)
Sparse Core Ops, SparseCore 0:
  10.2 72.2 all-gather.10
  285.4 54.0 reduce-scatter.11
  347.8 52.6 reduce-scatter.13
  403.2 32.0 reduce-scatter.23
  438.0 64.3 reduce-scatter.21
  505.2 63.2 reduce-scatter.19
  571.3 63.2 reduce-scatter.25
  636.9 34.7 reduce-scatter.17
  674.6 55.8 reduce-scatter.9
  732.3 26.4 all-gather.12
  760.8 41.8 all-gather.20
  804.5 41.7 all-gather.18
  848.3 41.7 all-gather.14
  892.0 28.8 all-gather.16
  923.9 52.6 reduce-scatter.15

commit v3 on v2

--- a/solution.py
+++ b/solution.py
@@ -263,6 +263,64 @@
         cost_estimate=pl.CostEstimate(flops=flops, bytes_accessed=2**26, transcendentals=2**22),
         name=name,
     )(*ins)
+
+
+class PlaneScatter:
+    SEMS = 8
+
+    def __init__(self, place, part, half, first, second, sems):
+        self.p, self.part, self.half = place, part, half
+        self.first, self.second, self.sems = first, second, sems
+
+    def ref(self):
+        return self.part(self.p.c)
+
+    def far_to_y(self):
+        p = self.p
+        return remote(self.half(p.cd, 0), self.first.at[0], self.sems.at[0], self.sems.at[2], p.y)
+
+    def far_to_x(self):
+        p = self.p
+        return remote(self.half(p.cd, 1), self.first.at[1], self.sems.at[1], self.sems.at[3], p.x)
+
+    def to_x(self):
+        p = self.p
+        return remote(self.part(p.cx), self.second.at[0], self.sems.at[4], self.sems.at[6], p.x)
+
+    def to_y(self):
+        p = self.p
+        return remote(self.part(p.cy), self.second.at[1], self.sems.at[5], self.sems.at[7], p.y)
+
+    def start(self):
+        self.far_to_y().start()
+        self.far_to_x().start()
+
+    def got(self, ref, sem):
+        remote(ref, ref, self.sems.at[0], sem, self.p.x).wait_recv()
+
+    def add(self, ref, other):
+        ref[...] = (ref[...].astype(f32) + other[...].astype(f32)).astype(bf16)
+
+    def middle(self):
+        p = self.p
+        self.got(self.first.at[0], self.sems.at[2])
+        self.add(self.half(p.cx, 0), self.first.at[0])
+        self.to_x().start()
+        self.got(self.first.at[1], self.sems.at[3])
+        self.add(self.half(p.cy, 1), self.first.at[1])
+        self.to_y().start()
+
+    def finish(self):
+        self.got(self.second.at[0], self.sems.at[6])
+        self.got(self.second.at[1], self.sems.at[7])
+        own = self.part(self.p.c)[...].astype(f32)
+        return own + self.second[0].astype(f32) + self.second[1].astype(f32)
+
+    def drain(self):
+        self.far_to_y().wait_send()
+        self.far_to_x().wait_send()
+        self.to_x().wait_send()
+        self.to_y().wait_send()
 
 
 def forward_kernel(
@@ -512,9 +570,216 @@
     return call(forward_kernel, ins, outs, scratch, 1, flops, "forward_stage")
 
 
-middle_stage = None
-
-backward_stage = None
+def tiles_of(total, most):
+    sizes, at = [], 0
+    while at < total:
+        sizes.append((at, min(most, total - at)))
+        at += most
+    return sizes
+
+
+def middle_kernel(
+    m_in, cot_in, wgate_in, wup_in, wdown_o,
+    y_out, down_part, gate_part, up_part, gm_out,
+    M, COT, WG, WU, WD, GATE, UP, HID, R2, PD, PH, D1, D2, H1, H2, GM, Y, STAGE_D, STAGE,
+    line_sems, plane_sems, copy_sems, stage_sems,
+):
+    p = Place()
+    n_ctx = 4
+    seq, width = M.shape
+    rows = seq // n_ctx
+    half = rows // 2
+    cw = width // n_ctx
+    units = GATE.shape[1]
+    loads = []
+    for i, (src, dst) in enumerate(((m_in, M), (wgate_in, WG), (wup_in, WU), (cot_in, COT))):
+        loads.append(pltpu.make_async_copy(src, dst, copy_sems.at[i]))
+        loads[-1].start()
+
+    p.barrier()
+    down_line = LineGather(p, wdown_o, WD, line_sems.at[0])
+    down_line.start()
+
+    loads[0].wait()
+    loads[1].wait()
+    loads[2].wait()
+
+    @pl.loop(0, n_ctx)
+    def _(b):
+        at = rows_at(b, rows)
+        mf = M[at, :].astype(f32)
+        r = lax.rsqrt(jnp.mean(mf * mf, axis=-1, keepdims=True) + eps_norm)
+        gate = dot(M[at, :], WG[...]) * r
+        up = dot(M[at, :], WU[...]) * r
+        R2[at, :] = jnp.broadcast_to(r, (rows, 128))
+        GATE[at, :] = gate.astype(bf16)
+        UP[at, :] = up.astype(bf16)
+        HID[at, :] = (gate * (1.0 / (1.0 + jnp.exp(-gate))) * up).astype(bf16)
+
+    down_line.hop(1)
+    loads[3].wait()
+    stage_copies = {}
+    for i, (at, size) in enumerate(tiles_of(units, STAGE_D.shape[1])):
+        slot = i % 2
+        if i >= 2:
+            stage_copies[i - 2].wait()
+        STAGE_D[slot, 0:size, :] = dot_tn(HID[:, at : at + size], COT[...]).astype(bf16)
+        copy = pltpu.make_async_copy(
+            STAGE_D.at[slot, pl.ds(0, size)], down_part.at[pl.ds(at, size)], stage_sems.at[slot]
+        )
+        copy.start()
+        stage_copies[i] = copy
+    n_down = len(stage_copies)
+    down_line.hop(2)
+    stage_copies[n_down - 2].wait()
+    stage_copies[n_down - 1].wait()
+    down_line.hop(3)
+    down_line.finish()
+
+    y_plane = PlaneScatter(
+        p,
+        lambda c: PD.at[rows_at(c, rows)],
+        lambda c, h: PD.at[pl.ds(pl.multiple_of(c * rows + h * half, half), half)],
+        D1,
+        D2,
+        plane_sems.at[0],
+    )
+
+    def col_scatter(b):
+        return PlaneScatter(
+            p,
+            lambda c: PH.at[pl.ds(b * rows, rows), rows_at(c, cw)],
+            lambda c, h: PH.at[pl.ds(b * rows + h * half, half), rows_at(c, cw)],
+            H1.at[b],
+            H2.at[b],
+            plane_sems.at[1 + b],
+        )
+
+    h_plane = [col_scatter(b) for b in range(n_ctx)]
+
+    def partial_out(c):
+        at = rows_at(c, rows)
+        PD[at, :] = dot(HID[at, :], WD[...]).astype(bf16)
+
+    partial_out(p.cd)
+    y_plane.start()
+    partial_out(p.cx)
+    partial_out(p.cy)
+    y_plane.middle()
+    partial_out(p.c)
+
+    def back(b):
+        at = pl.ds(b * rows, rows)
+        r = R2[at, 0:1]
+        grad_hidden = dot_nt(COT[at, :], WD[...])
+        gate = GATE[at, :].astype(f32)
+        up = UP[at, :].astype(f32)
+        sig = 1.0 / (1.0 + jnp.exp(-gate))
+        d_up = grad_hidden * gate * sig
+        d_gate = grad_hidden * up * sig * (1.0 + gate * (1.0 - sig))
+        stat = jnp.sum(d_gate * gate + d_up * up, axis=-1, keepdims=True)
+        GATE[at, :] = (d_gate * r).astype(bf16)
+        UP[at, :] = (d_up * r).astype(bf16)
+        coef = r * r * stat * (1.0 / width)
+        for j in range(0, width, cw):
+            e = dot_nt(GATE[at, :], WG[j : j + cw, :]) + dot_nt(UP[at, :], WU[j : j + cw, :])
+            PH[at, j : j + cw] = (e - M[at, j : j + cw].astype(f32) * coef).astype(bf16)
+        h_plane[b].start()
+
+    back(0)
+    back(1)
+    h_plane[0].middle()
+    back(2)
+    h_plane[1].middle()
+    back(3)
+    h_plane[2].middle()
+
+    stage_copies = {}
+    jobs = []
+    for src, dst in ((GATE, gate_part), (UP, up_part)):
+        for at, size in tiles_of(width, STAGE.shape[1]):
+            jobs.append((src, dst, at, size))
+
+    def weight_tile(i):
+        src, dst, at, size = jobs[i]
+        slot = i % 2
+        if i >= 2:
+            stage_copies[i - 2].wait()
+        STAGE[slot] = dot_tn(M[:, at : at + size], src[...]).astype(bf16)
+        copy = pltpu.make_async_copy(STAGE.at[slot], dst.at[pl.ds(at, size)], stage_sems.at[2 + slot])
+        copy.start()
+        stage_copies[i] = copy
+
+    def finish_block(b):
+        at = pl.ds(b * rows, rows)
+        GM[at, :] = (COT[at, rows_at(p.c, cw)].astype(f32) + h_plane[b].finish()).astype(bf16)
+
+    weight_tile(0)
+    weight_tile(1)
+    h_plane[3].middle()
+    weight_tile(2)
+    finish_block(0)
+    weight_tile(3)
+    finish_block(1)
+    weight_tile(4)
+    weight_tile(5)
+    finish_block(2)
+    weight_tile(6)
+    weight_tile(7)
+    Y[...] = (M[rows_at(p.c, rows), :].astype(f32) + y_plane.finish()).astype(bf16)
+    y_copy = pltpu.make_async_copy(Y, y_out, copy_sems.at[4])
+    y_copy.start()
+    finish_block(3)
+    gm_copy = pltpu.make_async_copy(GM, gm_out, copy_sems.at[5])
+    gm_copy.start()
+    stage_copies[6].wait()
+    stage_copies[7].wait()
+    y_copy.wait()
+    gm_copy.wait()
+    down_line.drain()
+    y_plane.drain()
+    for b in range(n_ctx):
+        h_plane[b].drain()
+
+
+def middle_stage(m, cot_all, wgate, wup, wdown_o):
+    n_fsdp, n_ctx = lax.axis_size("fsdp"), lax.axis_size("ctx")
+    seq, width = m.shape
+    rows = seq // n_ctx
+    cw = width // n_ctx
+    units = wgate.shape[1]
+    outs = [
+        ((rows, width), bf16), ((units, width), bf16), ((width, units), bf16), ((width, units), bf16),
+        ((seq, cw), bf16),
+    ]
+    scratch = [
+        pltpu.VMEM((seq, width), bf16),
+        pltpu.VMEM((seq, width), bf16),
+        pltpu.VMEM((width, units), bf16),
+        pltpu.VMEM((width, units), bf16),
+        pltpu.VMEM((units, width), bf16),
+        pltpu.VMEM((seq, units), bf16),
+        pltpu.VMEM((seq, units), bf16),
+        pltpu.VMEM((seq, units), bf16),
+        pltpu.VMEM((seq, 128), f32),
+        pltpu.VMEM((seq, width), bf16),
+        pltpu.VMEM((seq, width), bf16),
+        pltpu.VMEM((2, rows // 2, width), bf16),
+        pltpu.VMEM((2, rows, width), bf16),
+        pltpu.VMEM((n_ctx, 2, rows // 2, cw), bf16),
+        pltpu.VMEM((n_ctx, 2, rows, cw), bf16),
+        pltpu.VMEM((seq, cw), bf16),
+        pltpu.VMEM((rows, width), bf16),
+        pltpu.VMEM((2, 256, width), bf16),
+        pltpu.VMEM((2, 512, units), bf16),
+        pltpu.SemaphoreType.DMA((1, LineGather.SEMS)),
+        pltpu.SemaphoreType.DMA((5, PlaneScatter.SEMS)),
+        pltpu.SemaphoreType.DMA((6,)),
+        pltpu.SemaphoreType.DMA((4,)),
+    ]
+    flops = 18 * seq * width * units
+    return call(middle_kernel, (m, cot_all, wgate, wup, wdown_o), outs, scratch, 2, flops, "middle_stage")
+
 
 def rotate(field, cosine, sine_table, direction):
     half_width = field.shape[-1] // 2
@@ -610,7 +875,7 @@
     mid_rows = lax.dynamic_slice_in_dim(m, c * rows, rows, axis=0).astype(f32)
     output = (mid_rows + mlp).astype(bf16)
     grad_hidden = dot_nt(cot_all, wdown)
-    down_raw = scatter(dot_tn(hidden, cot_all), "fsdp")
+    down_raw = dot_tn(hidden, cot_all).astype(bf16)
     d_gate = grad_hidden * up * sig * (1.0 + gate * (1.0 - sig))
     d_up = grad_hidden * gate * sig
     stat = jnp.sum(d_gate * gate + d_up * up, axis=-1, keepdims=True)
@@ -624,7 +889,7 @@
     return output, down_raw, gate_raw, up_raw, gm
 
 
-def backward_plain(x, xn, gain, qt, kt, vt, lse, o, gm, wqkv, wout, tabs, gate_raw, up_raw):
+def backward_plain(x, xn, gain, qt, kt, vt, lse, o, gm, wqkv, wout, tabs, gate_raw, up_raw, down_raw):
     n_ctx = lax.axis_size("ctx")
     c = lax.axis_index("ctx")
     seq, width = x.shape
@@ -639,6 +904,7 @@
     begin = tabs[:, 64].reshape(seq).astype(jnp.int32)
     gate_grad = scatter(gate_raw, "fsdp")
     up_grad = scatter(up_raw, "fsdp")
+    down_grad = scatter(down_raw, "fsdp")
     out_grad = scatter(dot_tn(o, gm), "fsdp")
     d_att = scatter(dot_nt(gm, wout), "ctx", axis=1).reshape(seq, kv, heads // kv, HEAD_DIM)
     q = qt.T.reshape(seq, kv, heads // kv, HEAD_DIM)
@@ -671,7 +937,8 @@
     out_all = gather(out_grad, "ctx", axis=1)
     gate_all = gather(gate_grad[None], "ctx")
     up_all = gather(up_grad[None], "ctx")
-    return grad_tokens, qkv_all, out_all, gate_all, up_all
+    down_all = gather(down_grad, "ctx")
+    return grad_tokens, qkv_all, out_all, gate_all, up_all, down_all
 
 
 def per_device(
@@ -733,12 +1000,12 @@
     x, xn, qt, kt, vt, lse, o, m, wqkv, wout, wgate, wup, cot_all, tabs = forward(
         tokens, tab, gains, wqkv_o, wout_o, wgate_o, wup_o, cotangent
     )
-    middle = middle_plain
+    middle = middle_stage if kernels else middle_plain
     output, down_raw, gate_raw, up_raw, gm = middle(m, cot_all, wgate, wup, wdown_o)
     gain_row = gather(gain_attn, "fsdp").astype(f32)[None, :]
     backward = backward_plain
-    grad_tokens, qkv_all, out_all, gate_all, up_all = backward(
-        x, xn, gain_row, qt, kt, vt, lse, o, gm, wqkv, wout, tabs, gate_raw, up_raw
+    grad_tokens, qkv_all, out_all, gate_all, up_all, down_all = backward(
+        x, xn, gain_row, qt, kt, vt, lse, o, gm, wqkv, wout, tabs, gate_raw, up_raw, down_raw
     )
 
     qkv_all = qkv_all.astype(f32)
@@ -759,7 +1026,7 @@
         return full.transpose(1, 2, 0, 3).reshape(own_rows, ff_width).astype(f32)
 
     raw_gate, raw_up = spread(gate_all), spread(up_all)
-    grad_down = gather(down_raw, "ctx").astype(f32) if down_raw.shape[0] == unit else down_raw.astype(f32)
+    grad_down = down_all.astype(f32)
 
     def gain_term(grad, w):
         return jnp.sum(grad * w.astype(f32), axis=1)

time: 993 us -> 984 us (level)
  matrix products: 211 us -> 99.2 us
  Pallas kernels: 181 us -> 269 us
  waiting for transfers between devices: 397 us -> 416 us
  other arithmetic: 74.5 us -> 61.6 us
    pallas_call x1 -> x2, Pallas kernels: 181 us -> 269 us  [call(): pl.pallas_call(kernel, out_shape=[jax.ShapeDtypeStruct(s, d) for s, d in...]
    reduce_scatter x9 -> x7, waiting for transfers between devices: 273 us -> 323 us  [scatter(): lax.psum_scatter(x.astype(bf16), axis_name, scatter_dimension=axis, tiled...]
    dot_general x5 -> x2, matrix products: 50.9 us -> 12.7 us  [dot_nt(): lax.dot_general(a, b, (((1,), (1,)), ((), ())), preferred_element_type=f32)]
    dot_general x3 -> x0, matrix products: 37.3 us -> none  [dot(): return jnp.dot(a, b, preferred_element_type=f32)]
    dot_general x5 -> x2, matrix products: 49 us -> 13.5 us  [dot_tn(): lax.dot_general(a, b, (((0,), (0,)), ((), ())), preferred_element_type=f32)]
    all_gather x6 -> x5, waiting for transfers between devices: 123 us -> 90.2 us  [gather(): return lax.all_gather(x, axis_name, axis=axis, tiled=True)]
    unnamed x79 -> x74, local copies, waits for them, and re-layouts: 38.7 us -> 38.5 us
  transfers between devices with their start and end apart: 15 -> 12, of which waited for: 11 -> 10; matrix products, arithmetic and copies ran while one was open for 32% -> 22% of each run, Pallas kernels for 18% -> 0%
where the time goes in v3:
time: 984 us; the launch traced here: 968 us
  waiting for transfers between devices  416 us (42%)
  Pallas kernels  269 us (27%)
  matrix products  99.2 us (10%)
  local copies, waits for them, and re-layouts  94.5 us (10%)
  other arithmetic  61.6 us (6%)
  between operations  15 us (2%)
  blocking collectives  12.1 us (1%)
    reduce_scatter x7, waiting for transfers between devices, scatter(): lax.psum_scatter(x.astype(bf16), axis_name, scatter_dimension=axis, tiled...  323 us
    pallas_call x2, Pallas kernels, call(): pl.pallas_call(kernel, out_shape=[jax.ShapeDtypeStruct(s, d) for s, d in...  269 us
    all_gather x5, waiting for transfers between devices, gather(): return lax.all_gather(x, axis_name, axis=axis, tiled=True)  90.2 us
    unnamed x74, local copies, waits for them, and re-layouts  38.5 us
    convert_element_type x6, local copies, waits for them, and re-layouts, spread(): return full.transpose(1, 2, 0, 3).reshape(own_rows, ff_width).astype(f32)  36 us
    another operation x3, other arithmetic  29.1 us
    dot_general x1, matrix products, backward_plain(): d_probs = jnp.einsum('qkgd,lkd->kgql', d_att, v, preferred_element_type=f32)  24.5 us
  transfers between devices with their start and end apart: 12, of which 10 were waited for; matrix products, arithmetic and copies ran while one was open for 22% of the time, Pallas kernels for 0%

profile of v3, /device:TPU:8, one launch (start us, length us, event | category | flops | bytes accessed | tf_op | source)
XLA Modules:
  0.0 967.6 jit_solution(3487391364403366513)
XLA Ops:
  35.0 151.3 %forward_stage.1 = (bf16[1024,2048]{1,0:T(8,128)(2,1)}, bf16[1024,2048]{1,0:T(8,128)(2,1)}, bf16[512,1024]{1,0:T(8,128)(2,1)}, bf16[64,1024]{1,0:T(8,128)(2,1)},...) custom-call(bf16[256,2048]{1,0:T(8,128)(2,1)} %tok.1, ...), custom_call_target="tpu_custom_call" | custom-call | flops 9126805504 | bytes 67108864 | tf_op jit(solution)/shard_map/forward_stage/pallas_call | solution.py:254
  186.4 117.6 %middle_stage.1 = (bf16[256,2048]{1,0:T(8,128)(2,1)}, bf16[1408,2048]{1,0:T(8,128)(2,1)}, bf16[2048,1408]{1,0:T(8,128)(2,1)}, bf16[2048,1408]{1,0:T(8,128)(2,1)}, bf16[1024,512]{1,0:T(8,128)(2,1)}) custom-call(bf16[1024,2048]{1,0:T(8,128)(2,1)} %get-tuple-element.30.m_in, bf16[1024,2048]{1,0:T(8,128)(2,1)} %get-tuple-element.31.cot_in, ...), custom_call_target="tpu_custom_call" | custom-call | flops 53150220288 | bytes 67108864 | tf_op jit(solution)/shard_map/middle_stage/pallas_call | solution.py:254
  304.0 5.6 convolution_convert_fusion
  310.8 5.9 convolution_convert_fusion.2
  318.9 13.7 %fusion.30 = f32[1024,1024,8]{1,0,2:T(8,128)} fusion(bf16[1024,8,64]{0,2,1:T(8,128)(2,1)S(1)} %bitcast.185, bf16[64,1024]{1,0:T(8,128)(2,1)S(1)} %copy-done.11), kind=kOutput, calls=%fused_computation.60 | convolution fusion | flops 1073741824 | bytes 34734080 | tf_op jit(solution)/shard_map/qkgd,lkd->kgql/dot_general | solution.py:913
  332.6 43.5 %reduce-scatter.8.cloned.1.call-done = bf16[1024,512]{1,0:T(8,128)(2,1)} async-done(((bf16[1024,2048]{1,0:T(8,128)(2,1)}), bf16[1024,512]{1,0:T(8,128)(2,1)}) %reduce-scatter.8.cloned.1.call-update) | async-done | bytes 1048592 | tf_op jit(solution)/shard_map/reduce_scatter | solution.py:802
  378.4 24.5 %fusion.2 = (f32[8,1024]{1,0:T(8,128)S(1)}, f32[1024,1024,8]{1,0,2:T(8,128)}) fusion(f32[1024,1024,8]{1,0,2:T(8,128)} %fusion.30, f32[8,1024]{1,0:T(8,128)S(1)} %bitcast.196, pred[1024,1024]{0,1:T(8,128)(4,1)S(1)} %fusion.17, bf16[1024,8,64]{0,2,1:T(8,128)(2,1)} %bitcast.192, bf16[64,1024]{1,0:T(8,128)(2,1)S(1)} %copy-done.20), kind=kOutput, calls=%fused_computation.5 | convolution fusion | flops 1115676672 | bytes 69402624 | tf_op jit(solution)/shard_map/qkgd,lkd->kgql/dot_general | solution.py:917
  402.9 28.8 %fusion.7 = bf16[8,1024,1024]{1,2,0:T(8,128)(2,1)} fusion(f32[1024,1024,8]{1,0,2:T(8,128)} %get-tuple-element.97, f32[1024,1024,8]{1,0,2:T(8,128)} %fusion.30, f32[8,1024]{1,0:T(8,128)S(1)} %get-tuple-element.96, f32[8,1024]{1,0:T(8,128)S(1)} %bitcast.197, pred[1024,1024]{0,1:T(8,128)(4,1)S(1)} %fusion.17), kind=kLoop, calls=%fused_computation.10 | loop fusion | flops 50331648 | bytes 85000192 | tf_op jit(solution)/shard_map/reshape.12
  431.6 11.0 %fusion.25 = (f32[1024]{0:T(1024)S(1)}, f32[1024,1,64]{0,2,1:T(8,128)S(1)}) fusion(bf16[64,1024]{1,0:T(8,128)(2,1)S(1)} %copy-done.11, bf16[1024,8,64]{0,2,1:T(8,128)(2,1)S(1)} %bitcast.186, bf16[8,1024,1024]{1,2,0:T(8,128)(2,1)} %fusion.7), kind=kOutput, calls=%fused_computation.52 | convolution fusion | flops 1074002944 | bytes 18223104 | tf_op jit(solution)/shard_map/kgql,qkgd->lkd/dot_general | solution.py:921
  442.7 8.9 fusion.18
  453.2 15.0 %convert_bitcast_fusion = (bf16[1024,64]{0,1:T(8,128)(2,1)S(1)}, f32[1024]{0:T(1024)S(1)}) fusion(bf16[64,1024]{1,0:T(8,128)(2,1)S(1)} %copy-done.20, bf16[1024,8,64]{0,2,1:T(8,128)(2,1)S(1)} %bitcast.193, f32[1024,1024,8]{1,0,2:T(8,128)} %fusion.30, f32[8,1024]{1,0:T(8,128)S(1)} %bitcast.198, pred[1024,1024]{0,1:T(8,128)(4,1)S(1)} %fusion.17), kind=kOutput, calls=%fused_computation.62 | convolution fusion | flops 1107557376 | bytes 35950592 | tf_op jit(solution)/shard_map/kgql,qkgd->lkd/dot_general | solution.py:922
  468.2 7.5 convolution_convert_fusion.1
  478.2 31.2 %reduce-scatter.12.cloned.1.call-done = bf16[256,640]{1,0:T(8,128)(2,1)} async-done(((bf16[2048,640]{1,0:T(8,128)(2,1)}), bf16[256,640]{1,0:T(8,128)(2,1)}) %reduce-scatter.12.cloned.1.call-update) | async-done | bytes 327696 | tf_op jit(solution)/shard_map/reduce_scatter | solution.py:802
  509.5 67.2 %reduce-scatter.14.cloned.1.call-done = bf16[256,1408]{1,0:T(8,128)(2,1)} async-done(((bf16[2048,1408]{1,0:T(8,128)(2,1)}), bf16[256,1408]{1,0:T(8,128)(2,1)}) %reduce-scatter.14.cloned.1.call-update) | async-done | bytes 720912 | tf_op jit(solution)/shard_map/reduce_scatter | solution.py:802
  576.7 65.4 %reduce-scatter.16.cloned.1.call-done = bf16[256,1408]{1,0:T(8,128)(2,1)} async-done(((bf16[2048,1408]{1,0:T(8,128)(2,1)}), bf16[256,1408]{1,0:T(8,128)(2,1)}) %reduce-scatter.16.cloned.1.call-update) | async-done | bytes 720912 | tf_op jit(solution)/shard_map/reduce_scatter | solution.py:802
  642.2 65.4 %reduce-scatter.20.cloned.1.call-done = bf16[176,2048]{1,0:T(8,128)(2,1)} async-done(((bf16[1408,2048]{1,0:T(8,128)(2,1)}), bf16[176,2048]{1,0:T(8,128)(2,1)}) %reduce-scatter.20.cloned.1.call-update) | async-done | bytes 720912 | tf_op jit(solution)/shard_map/reduce_scatter | solution.py:802
  712.2 7.7 copy.98
  719.9 12.1 %all-gather.3 = bf16[8,1,256]{2,1,0:T(2,128)(2,1)S(1)} all-gather(bf16[1,1,256]{2,1,0:T(2,128)(2,1)S(1)} %reshape.284), channel_id=1, replica_groups=mesh['fsdp'=8,'ctx'=4] {'fsdp'}, dimensions={0}, use_global_device_ids=true | all-gather | bytes 4608 | tf_op jit(solution)/shard_map/all_gather | solution.py:798
  733.0 7.1 fusion.14
  744.6 23.6 %all-gather.14.cloned.1.call-done = bf16[1024,640]{1,0:T(8,128)(2,1)} async-done(((bf16[256,640]{1,0:T(8,128)(2,1)}), bf16[1024,640]{1,0:T(8,128)(2,1)}) %all-gather.14.cloned.1.call-update) | async-done | bytes 1310736 | tf_op jit(solution)/shard_map/all_gather | solution.py:798
  776.4 35.7 %all-gather.16.cloned.1.call-done = bf16[1024,1408]{1,0:T(8,128)(2,1)} async-done(((bf16[256,1408]{1,0:T(8,128)(2,1)}), bf16[1024,1408]{1,0:T(8,128)(2,1)}) %all-gather.16.cloned.1.call-update) | async-done | bytes 2883600 | tf_op jit(solution)/shard_map/all_gather | solution.py:798
  812.1 5.1 copy.79
  817.2 7.9 reshape.274
  825.1 6.2 copy.80
  831.3 24.5 %all-gather.18.cloned.1.call-done = bf16[1024,1408]{1,0:T(8,128)(2,1)} async-done(((bf16[256,1408]{1,0:T(8,128)(2,1)}), bf16[1024,1408]{1,0:T(8,128)(2,1)}) %all-gather.18.cloned.1.call-update) | async-done | bytes 2883600 | tf_op jit(solution)/shard_map/all_gather | solution.py:798
  860.9 7.8 reshape.275
  873.1 7.1 bitcast_multiply_fusion.1
  880.2 6.2 copy.87
  886.5 6.2 copy.88
  893.2 6.3 all-gather.12.cloned.1.call-done
  899.6 5.3 convert_element_type.196
  904.9 50.6 %reduce-scatter.10.cloned.1.call-done = bf16[256,2048]{1,0:T(8,128)(2,1)} async-done(((bf16[1024,2048]{1,0:T(8,128)(2,1)}), bf16[256,2048]{1,0:T(8,128)(2,1)}) %reduce-scatter.10.cloned.1.call-update) | async-done | bytes 1048592 | tf_op jit(solution)/shard_map/reduce_scatter | solution.py:802
  (147 shorter events, 70.7 us)
Async XLA Ops:
  7.2 21.4 %copy-start = (bf16[704,2048]{1,0:T(8,128)(2,1)S(1)}, bf16[704,2048]{1,0:T(8,128)(2,1)}, u32[]{:S(2)}) copy-start(bf16[704,2048]{1,0:T(8,128)(2,1)} %param.22) | copy-start | bytes 8650756
  7.2 368.9 %reduce-scatter.8.cloned.1.call-start = ((), (), s32[]{:S(2)}) async-start(), calls=%async_computation.7 | async-start | bytes 5242880 | tf_op jit(solution)/shard_map/reduce_scatter | solution.py:802
  20.1 8.2 copy-start.26
  20.1 8.2 copy-start.25
  23.1 8.4 copy-start.16
  23.1 8.4 copy-start.18
  28.3 6.1 copy-start.23
  28.3 158.0 %copy-start.21 = (f32[256]{0:T(256)}, f32[256]{0:T(256)S(1)}, u32[]{:S(2)}) copy-start(f32[256]{0:T(256)S(1)} %convert_element_type.153) | copy-start | bytes 3076
  28.6 3.8 copy-start.6
  186.3 117.7 %copy-start.27 = (bf16[2048,512]{1,0:T(8,128)(2,1)S(1)}, bf16[2048,512]{1,0:T(8,128)(2,1)}, u32[]{:S(2)}) copy-start(bf16[2048,512]{1,0:T(8,128)(2,1)} %get-tuple-element.41) | copy-start | bytes 6291460
  309.6 167.9 %reduce-scatter.18.cloned.1.call-start = ((), (), s32[]{:S(2)}) async-start(), calls=%async_computation.12 | async-start | bytes 2359296 | tf_op jit(solution)/shard_map/reduce_scatter | solution.py:802
  310.8 6.0 copy-start.15
  316.8 192.6 %reduce-scatter.12.cloned.1.call-start = ((), (), s32[]{:S(2)}) async-start(), calls=%async_computation.9 | async-start | bytes 2949120 | tf_op jit(solution)/shard_map/reduce_scatter | solution.py:802
  318.9 59.5 %copy-start.20 = (bf16[64,1024]{1,0:T(8,128)(2,1)S(1)}, bf16[64,1024]{1,0:T(8,128)(2,1)}, u32[]{:S(2)}) copy-start(bf16[64,1024]{1,0:T(8,128)(2,1)} %get-tuple-element.39) | copy-start | bytes 393220
  475.7 100.9 %reduce-scatter.14.cloned.1.call-start = ((), (), s32[]{:S(2)}) async-start(), calls=%async_computation.10 | async-start | bytes 6488064 | tf_op jit(solution)/shard_map/reduce_scatter | solution.py:802
  476.3 165.9 %reduce-scatter.16.cloned.1.call-start = ((), (), s32[]{:S(2)}) async-start(), calls=%async_computation.11 | async-start | bytes 6488064 | tf_op jit(solution)/shard_map/reduce_scatter | solution.py:802
  476.9 230.8 %reduce-scatter.20.cloned.1.call-start = ((), (), s32[]{:S(2)}) async-start(), calls=%async_computation.14 | async-start | bytes 6488064 | tf_op jit(solution)/shard_map/reduce_scatter | solution.py:802
  476.9 230.8 %copy-start.24 = (bf16[256]{0:T(256)(128)(2,1)S(1)}, bf16[256]{0:T(256)(128)(2,1)}, u32[]{:S(2)}) copy-start(bf16[256]{0:T(256)(128)(2,1)} %param.14) | copy-start | bytes 1540
  476.9 230.8 %copy-start.13 = (bf16[1024,512]{1,0:T(8,128)(2,1)S(1)}, bf16[1024,512]{1,0:T(8,128)(2,1)}, u32[]{:S(2)}) copy-start(bf16[1024,512]{1,0:T(8,128)(2,1)} %get-tuple-element.40) | copy-start | bytes 3145732
  477.5 264.4 %all-gather.10.cloned.1.call-start = ((), (), s32[]{:S(2)}) async-start(), calls=%async_computation.13 | async-start | bytes 1310720 | tf_op jit(solution)/shard_map/all_gather | solution.py:798
  478.2 290.0 %all-gather.14.cloned.1.call-start = ((), (), s32[]{:S(2)}) async-start(), calls=%async_computation.16 | async-start | bytes 1638400 | tf_op jit(solution)/shard_map/all_gather | solution.py:798
  509.4 302.6 %all-gather.16.cloned.1.call-start = ((), (), s32[]{:S(2)}) async-start(), calls=%async_computation.17 | async-start | bytes 3604480 | tf_op jit(solution)/shard_map/all_gather | solution.py:798
  576.7 279.1 %all-gather.18.cloned.1.call-start = ((), (), s32[]{:S(2)}) async-start(), calls=%async_computation.18 | async-start | bytes 3604480 | tf_op jit(solution)/shard_map/all_gather | solution.py:798
  642.2 257.4 %all-gather.12.cloned.1.call-start = ((), (), s32[]{:S(2)}) async-start(), calls=%async_computation.15 | async-start | bytes 3604480 | tf_op jit(solution)/shard_map/all_gather | solution.py:798
  707.7 247.7 %reduce-scatter.10.cloned.1.call-start = ((), (), s32[]{:S(2)}) async-start(), calls=%async_computation.8 | async-start | bytes 5242880 | tf_op jit(solution)/shard_map/reduce_scatter | solution.py:802
  712.2 19.8 %copy-start.10 = (bf16[1024,2048]{1,0:T(8,128)(2,1)S(1)}, bf16[1024,2048]{1,0:T(8,128)(2,1)}, u32[]{:S(2)}) copy-start(bf16[1024,2048]{1,0:T(8,128)(2,1)} %get-tuple-element.43) | copy-start | bytes 12582916
  719.9 13.1 %copy-start.14 = (bf16[1024,8,64]{0,2,1:T(8,128)(2,1)S(1)}, bf16[1024,8,64]{0,2,1:T(8,128)(2,1)}, u32[]{:S(2)}) copy-start(bf16[1024,8,64]{0,2,1:T(8,128)(2,1)} %pad_maximum_fusion.1) | copy-start | bytes 3145732
  719.9 13.1 %copy-start.28 = (bf16[2048,640]{1,0:T(8,128)(2,1)S(1)}, bf16[2048,640]{1,0:T(8,128)(2,1)}, u32[]{:S(2)}) copy-start(bf16[2048,640]{1,0:T(8,128)(2,1)} %get-tuple-element.42) | copy-start | bytes 7864324
  771.0 4.8 copy-start.5
  868.8 4.4 copy-start.3
  868.8 4.4 copy-start.22
  899.6 60.9 %copy-start.1 = (bf16[704,2048]{1,0:T(8,128)(2,1)S(1)}, bf16[704,2048]{1,0:T(8,128)(2,1)}, u32[]{:S(2)}) copy-start(bf16[704,2048]{1,0:T(8,128)(2,1)} %param.22) | copy-start | bytes 8650756
  (9 other events, 18.5 us)
Sparse Core Ops, SparseCore 0:
  309.8 66.2 reduce-scatter.7
  379.1 32.1 reduce-scatter.17
  475.8 33.5 reduce-scatter.11
  511.7 64.9 reduce-scatter.13
  578.9 63.2 reduce-scatter.15
  644.4 63.2 reduce-scatter.19
  709.6 27.7 all-gather.9
  739.4 28.8 all-gather.13
  770.2 41.8 all-gather.15
  813.9 41.7 all-gather.17
  857.8 41.7 all-gather.11
  902.7 52.6 reduce-scatter.9

commit v4 on v3

--- a/solution.py
+++ b/solution.py
@@ -250,7 +250,7 @@
     return [pl.BlockSpec(memory_space=pl.ANY)] * count
 
 
-def call(kernel, ins, outs, scratch, collective_id, flops, name):
+def call(kernel, ins, outs, scratch, collective_id, flops, name, vmem=60.0):
     return pl.pallas_call(
         kernel,
         out_shape=[jax.ShapeDtypeStruct(s, d) for s, d in outs],
@@ -258,7 +258,7 @@
         out_specs=any_spec(len(outs)),
         scratch_shapes=scratch,
         compiler_params=pltpu.CompilerParams(
-            collective_id=collective_id, has_side_effects=True, vmem_limit_bytes=60 * 2**20
+            collective_id=collective_id, has_side_effects=True, vmem_limit_bytes=int(vmem * 2**20)
         ),
         cost_estimate=pl.CostEstimate(flops=flops, bytes_accessed=2**26, transcendentals=2**22),
         name=name,
@@ -310,11 +310,12 @@
         self.add(self.half(p.cy, 1), self.first.at[1])
         self.to_y().start()
 
-    def finish(self):
-        self.got(self.second.at[0], self.sems.at[6])
-        self.got(self.second.at[1], self.sems.at[7])
-        own = self.part(self.p.c)[...].astype(f32)
-        return own + self.second[0].astype(f32) + self.second[1].astype(f32)
+    def finish(self, at=slice(None), first=True):
+        if first:
+            self.got(self.second.at[0], self.sems.at[6])
+            self.got(self.second.at[1], self.sems.at[7])
+        own = self.part(self.p.c)[at].astype(f32)
+        return own + self.second[0, at].astype(f32) + self.second[1, at].astype(f32)
 
     def drain(self):
         self.far_to_y().wait_send()
@@ -323,11 +324,107 @@
         self.to_y().wait_send()
 
 
+class LineScatter:
+    SEMS = 22
+
+    def __init__(self, place, part, acc, slots, sems, stage=None):
+        self.p, self.part, self.acc, self.slots, self.sems = place, part, acc, slots, sems
+        self.stage = stage
+        self.n = place.depth
+
+    def to_sibling(self, level):
+        p = self.p
+        return remote(
+            self.part(level, p.other), self.acc.at[level], self.sems.at[level], self.sems.at[4 + level], p.sibling
+        )
+
+    def start(self):
+        for level in range(self.n):
+            self.to_sibling(level).start()
+
+    def load(self, level):
+        return pltpu.make_async_copy(
+            self.part(level, self.p.core), self.stage[level % 2], self.sems.at[20 + level % 2]
+        )
+
+    def got(self, ref, sem):
+        remote(ref, ref, self.sems.at[0], sem, self.p.sibling).wait_recv()
+
+    def add(self, ref, other):
+        ref[...] = (ref[...].astype(f32) + other[...].astype(f32)).astype(bf16)
+
+    def combine(self):
+        if self.stage is not None:
+            self.load(0).start()
+            self.load(1).start()
+        for level in range(self.n):
+            self.got(self.acc.at[level], self.sems.at[4 + level])
+            if self.stage is None:
+                self.add(self.acc.at[level], self.part(level, self.p.core))
+            else:
+                self.load(level).wait()
+                self.add(self.acc.at[level], self.stage[level % 2])
+                if level + 2 < self.n:
+                    self.load(level + 2).start()
+
+    def slot(self, up, s):
+        return self.slots.at[s - 1] if up else self.slots.at[(0, 3, 4)[s - 1]]
+
+    def along(self, up, s):
+        p = self.p
+        level = p.z if up else self.n - 1 - p.z
+        block = self.n - s + level
+        block = block if up else self.n - 1 - block
+        base = 8 if up else 14
+        copy = remote(
+            self.acc.at[block],
+            self.slot(up, s),
+            self.sems.at[base + s - 1],
+            self.sems.at[base + 3 + s - 1],
+            p.up if up else p.down,
+        )
+        return copy, (level <= s - 1) & (level < self.n - 1)
+
+    def step(self, s):
+        for up in (True, False):
+            level = self.p.z if up else self.n - 1 - self.p.z
+            if s > 1:
+                block = self.n - s + level
+                block = block if up else self.n - 1 - block
+                base = 11 if up else 17
+
+                @pl.when((level >= 1) & (s - 1 >= level))
+                def _():
+                    self.got(self.slot(up, s - 1), self.sems.at[base + s - 2])
+                    self.add(self.acc.at[block], self.slot(up, s - 1))
+
+            if s < self.n:
+                copy, valid = self.along(up, s)
+
+                @pl.when(valid)
+                def _():
+                    copy.start()
+
+    def result(self):
+        return self.acc.at[self.p.z]
+
+    def drain(self):
+        for level in range(self.n):
+            self.to_sibling(level).wait_send()
+        for up in (True, False):
+            for s in range(1, self.n):
+                copy, valid = self.along(up, s)
+
+                @pl.when(valid)
+                def _():
+                    copy.wait_send()
+
+
 def forward_kernel(
     tok, tab, gains, wqkv_o, wout_o, wgate_o, wup_o, cot,
-    x_out, xn_out, qt_out, kt_out, vt_out, lse_out, o_out, m_out,
+    xn_out, r_out, grow_out, qt_out, kt_out, vt_out, lse_out, o_out, m_out,
     wqkv_out, wout_out, wgate, wup, cot_all, tab_out,
-    X, XN, QT, KT, VT, K, LSE, O, M, WQ, WO, TAB, G8, GROW, BIAS, OT,
+    X, XN, QT, KT, VT, K, LSE, O, M, WQ, WO, TAB, G8, GROW, BIAS, OT, R1,
     line_sems, plane_sems, copy_sems,
 ):
     p = Place()
@@ -401,6 +498,7 @@
         at = rows_at(c, rows)
         x = X[at, :].astype(f32)
         r = lax.rsqrt(jnp.mean(x * x, axis=-1, keepdims=True) + eps_norm)
+        R1[at, :] = jnp.broadcast_to(r, (rows, 128))
         XN[at, :] = (x * r * GROW[0:1, :]).astype(bf16)
 
     own_tok.wait()
@@ -418,10 +516,12 @@
     out_line.hop(3)
     up_line.start()
     norm(p.cd)
-    x_copy = pltpu.make_async_copy(X, x_out, copy_sems.at[3])
-    xn_copy = pltpu.make_async_copy(XN, xn_out, copy_sems.at[4])
-    x_copy.start()
+    xn_copy = pltpu.make_async_copy(XN, xn_out, copy_sems.at[3])
+    r_copy = pltpu.make_async_copy(R1, r_out, copy_sems.at[4])
+    grow_copy = pltpu.make_async_copy(GROW, grow_out, copy_sems.at[14])
     xn_copy.start()
+    r_copy.start()
+    grow_copy.start()
     own_tab.wait()
     tab_plane.finish()
     qkv_line.finish()
@@ -504,7 +604,7 @@
     m_plane[2].middle()
     up_line.hop(2)
     m_plane[3].middle()
-    copies = [x_copy, xn_copy, wq_copy]
+    copies = [xn_copy, r_copy, grow_copy, wq_copy]
     for i, (src, dst) in enumerate(
         ((QT, qt_out), (KT, kt_out), (VT, vt_out), (LSE, lse_out), (O, o_out), (WO, wout_out), (TAB, tab_out))
     ):
@@ -540,8 +640,8 @@
     heads = qw // HEAD_DIM
     tab_shape = (n_ctx,) + tab.shape
     outs = [
-        ((seq, width), bf16), ((seq, width), bf16), ((qw, seq), bf16), ((64, seq), bf16), ((64, seq), bf16),
-        ((8 * heads, seq), f32), ((seq, width), bf16), ((seq, width), bf16), ((whole, nq), bf16),
+        ((seq, width), bf16), ((seq, 128), f32), ((8, width), f32), ((qw, seq), bf16), ((64, seq), bf16),
+        ((64, seq), bf16), ((8 * heads, seq), f32), ((seq, width), bf16), ((seq, width), bf16), ((whole, nq), bf16),
         ((whole, nw), bf16), ((whole, nu), bf16), ((whole, nu), bf16), ((seq, width), bf16), (tab_shape, f32),
     ]
     scratch = [
@@ -561,9 +661,10 @@
         pltpu.VMEM((8, width), f32),
         pltpu.VMEM((seq, rows), f32),
         pltpu.VMEM((qw, rows), f32),
+        pltpu.VMEM((seq, 128), f32),
         pltpu.SemaphoreType.DMA((5, LineGather.SEMS)),
         pltpu.SemaphoreType.DMA((11, PlaneGather.SEMS)),
-        pltpu.SemaphoreType.DMA((14,)),
+        pltpu.SemaphoreType.DMA((15,)),
     ]
     ins = (tok, tab, gains, wqkv_o, wout_o, wgate_o, wup_o, cot)
     flops = 2 * seq * width * (nq + nw) + 8 * heads * seq * seq * HEAD_DIM
@@ -779,6 +880,322 @@
     ]
     flops = 18 * seq * width * units
     return call(middle_kernel, (m, cot_all, wgate, wup, wdown_o), outs, scratch, 2, flops, "middle_stage")
+
+
+def backward_kernel(
+    xn_in, r_in, grow_in, qt_in, kt_in, vt_in, lse_in, o_in, gm_in, wqkv_in, wout_in, tab_in,
+    gate_part, up_part, down_part,
+    tok_out, qkv_all, out_all, gate_all, up_all, down_all,
+    XN, R1, GROW, QT, KT, VT, LSE, O, GM, WQ, WO, TAB,
+    K, V, DK, DV, DOT, DQT, DPRE, STAT, BIAS, PT, G1, G2, T1, T2, TOK,
+    DACC, DSLOT, GACC, GSLOT, UACC, USLOT, OACC, OSLOT, QACC, QSLOT,
+    line_sems, plane_sems, scatter_sems, copy_sems,
+):
+    p = Place()
+    n_ctx = 4
+    seq, width = XN.shape
+    rows = seq // n_ctx
+    half = rows // 2
+    cw = width // n_ctx
+    qw = QT.shape[0]
+    heads = qw // HEAD_DIM
+    nq = WQ.shape[1]
+    own_rows = QACC.shape[1]
+    scale = HEAD_DIM ** (-0.5)
+    loads = []
+    for i, (src, dst) in enumerate(
+        (
+            (gm_in, GM), (wout_in, WO), (o_in, O), (kt_in, KT), (vt_in, VT), (qt_in, QT), (lse_in, LSE),
+            (tab_in, TAB), (xn_in, XN), (wqkv_in, WQ), (r_in, R1), (grow_in, GROW),
+        )
+    ):
+        loads.append(pltpu.make_async_copy(src, dst, copy_sems.at[i]))
+        if dst is not XN:
+            loads[-1].start()
+
+    p.barrier()
+
+    def block_rows(ref):
+        count = ref.shape[0] // (2 * p.depth)
+        return lambda level, core: ref.at[pl.ds(pl.multiple_of((2 * level + core) * count, 16), count)]
+
+    unit, nu = DACC.shape[1], GACC.shape[2]
+    rows_stage = [XN.at[pl.ds(i * unit, unit)] for i in range(2)]
+    cols_stage = [XN.at[pl.ds(i * own_rows, own_rows), pl.ds(0, nu)] for i in range(2)]
+    down_line = LineScatter(p, block_rows(down_part), DACC, DSLOT, line_sems.at[0], rows_stage)
+    gate_line = LineScatter(p, block_rows(gate_part), GACC, GSLOT, line_sems.at[1], cols_stage)
+    up_line = LineScatter(p, block_rows(up_part), UACC, USLOT, line_sems.at[2], cols_stage)
+    out_line = LineScatter(p, block_rows(WO), OACC, OSLOT, line_sems.at[3])
+
+    def qkv_block(level, core):
+        f = 2 * level + core
+        at = pl.ds(pl.multiple_of((f % p.depth) * own_rows, own_rows), own_rows)
+        return O.at[at, pl.ds(pl.multiple_of((f // p.depth) * nq, 128), nq)]
+
+    qkv_line = LineScatter(p, qkv_block, QACC, QSLOT, line_sems.at[4])
+    down_line.start()
+    gate_line.start()
+    up_line.start()
+
+    def col_scatter(b):
+        return PlaneScatter(
+            p,
+            lambda c: PT.at[pl.ds(b * rows, rows), rows_at(c, cw)],
+            lambda c, h: PT.at[pl.ds(b * rows + h * half, half), rows_at(c, cw)],
+            G1.at[b],
+            G2.at[b],
+            scatter_sems.at[b],
+        )
+
+    g_plane = [col_scatter(b) for b in range(n_ctx)]
+    t_plane = PlaneScatter(
+        p,
+        lambda c: PT.at[rows_at(c, rows)],
+        lambda c, h: PT.at[pl.ds(pl.multiple_of(c * rows + h * half, half), half)],
+        T1,
+        T2,
+        scatter_sems.at[n_ctx],
+    )
+
+    def whole(ref, line, index, first):
+        count = line.acc.shape[1]
+
+        def halves(c, h):
+            return ref(c).at[pl.ds(h * first, count - first if h else first)]
+
+        plane = PlaneGather(p, ref, halves, plane_sems.at[index], own=line.result())
+        own = pltpu.make_async_copy(line.result(), ref(p.c), plane_sems.at[index, PlaneGather.SEMS])
+        return plane, own
+
+    down_plane, down_own = whole(lambda c: down_all.at[c], down_line, 0, 96)
+    gate_plane, gate_own = whole(lambda c: gate_all.at[c], gate_line, 1, half)
+    up_plane, up_own = whole(lambda c: up_all.at[c], up_line, 2, half)
+    out_plane, out_own = whole(lambda c: out_all.at[c], out_line, 3, half)
+    qkv_plane, qkv_own = whole(lambda c: qkv_all.at[c], qkv_line, 4, half)
+
+    loads[0].wait()
+    loads[1].wait()
+    for b in range(n_ctx):
+        at = pl.ds(b * rows, rows)
+        for j in range(0, width, 512):
+            PT[at, j : j + 512] = dot_nt(GM[at, :], WO[j : j + 512, :]).astype(bf16)
+        g_plane[b].start()
+    down_line.combine()
+    down_line.step(1)
+    g_plane[0].middle()
+    loads[2].wait()
+
+    @pl.loop(0, width // 512)
+    def _(i):
+        at = rows_at(i, 512)
+        WO[at, :] = dot_tn(O[:, at], GM[...]).astype(bf16)
+
+    out_line.start()
+    g_plane[1].middle()
+    gate_line.combine()
+    loads[8].start()
+    gate_line.step(1)
+    g_plane[2].middle()
+    for i in (3, 4, 5, 6, 7, 10):
+        loads[i].wait()
+
+    @pl.loop(0, n_ctx)
+    def _(b):
+        at = rows_at(b, rows)
+        K[at, :] = KT[:, at].astype(f32).T.astype(bf16)
+        V[at, :] = VT[:, at].astype(f32).T.astype(bf16)
+        DK[at, :] = jnp.zeros((rows, HEAD_DIM), f32)
+        DV[at, :] = jnp.zeros((rows, HEAD_DIM), f32)
+
+    g_plane[3].middle()
+
+    def attend_back(b):
+        n = (b + 1) * rows
+        cols = slice(b * rows, (b + 1) * rows)
+        DOT[...] = g_plane[b].finish().T.astype(bf16)
+        at = pl.ds(b * rows, rows)
+        DQT[...] = O[at, rows_at(p.c, cw)].astype(f32).T
+        key = lax.broadcasted_iota(jnp.int32, (n, rows), 0)
+        query = lax.broadcasted_iota(jnp.int32, (n, rows), 1) + b * rows
+        begin = TAB[b, 64:65, :].astype(jnp.int32)
+        BIAS[0:n, :] = jnp.where((key <= query) & (key >= begin), 0.0, neg_large)
+        STAT[...] = jnp.zeros((8, rows), f32)
+
+        @pl.loop(0, heads)
+        def _(h):
+            head = rows_at(h, HEAD_DIM)
+            q = QT[head, cols]
+            d_out = DOT[head, :]
+            delta = jnp.sum(d_out.astype(f32) * DQT[head, :], axis=0, keepdims=True)
+            s = dot(K[0:n, :], q) * scale + BIAS[0:n, :]
+            probs = jnp.exp(s - LSE[rows_at(h, 8), cols][0:1])
+            d_probs = dot(V[0:n, :], d_out)
+            d_s = (probs * (d_probs - delta)).astype(bf16)
+            d_q = dot(KT[:, 0:n], d_s) * scale
+            DK[0:n, :] += dot_nt(d_s, q) * scale
+            DV[0:n, :] += dot_nt(probs.astype(bf16), d_out)
+            STAT[...] += jnp.broadcast_to(jnp.sum(d_q * q.astype(f32), axis=0, keepdims=True), (8, rows))
+            u, w = d_q[0:32], d_q[32:64]
+            cosine, sine = TAB[b, 0:32, :], TAB[b, 32:64, :]
+            DQT[head, :] = jnp.concatenate([u * cosine + w * sine, w * cosine - u * sine], axis=0)
+
+        DPRE[at, 0:qw] = DQT[...].T.astype(bf16)
+        R1[at, 0:8] = STAT[...].T
+
+    attend_back(0)
+    down_line.step(2)
+    attend_back(1)
+    gate_line.step(2)
+    attend_back(2)
+    down_line.step(3)
+    attend_back(3)
+    gate_line.step(3)
+    loads[8].wait()
+    loads[9].wait()
+    loads[11].wait()
+
+    @pl.loop(0, n_ctx)
+    def _(b):
+        at = rows_at(b, rows)
+        d_k = DK[at, :].T
+        d_v = DV[at, :].T
+        stat = jnp.sum(d_k * KT[:, at].astype(f32) + d_v * VT[:, at].astype(f32), axis=0, keepdims=True)
+        R1[at, 0:8] += jnp.broadcast_to(stat, (8, rows)).T
+        u, w = d_k[0:32], d_k[32:64]
+        cosine, sine = TAB[b, 0:32, :], TAB[b, 32:64, :]
+        both = jnp.concatenate([u * cosine + w * sine, w * cosine - u * sine, d_v], axis=0)
+        DPRE[at, qw:] = both.T.astype(bf16)
+
+    def tokens(c):
+        at = rows_at(c, rows)
+        r = R1[at, 127:128]
+        coef = r * R1[at, 0:1] * (1.0 / width)
+        for j in range(0, width, 512):
+            cols = slice(j, j + 512)
+            gain = GROW[0:1, cols]
+            e = dot_nt(DPRE[at, :], WQ[cols, :])
+            PT[at, cols] = (e * (gain * r) - XN[at, cols].astype(f32) * ((1.0 / gain) * coef)).astype(bf16)
+        mine = rows_at(p.c, cw)
+        PT[at, mine] = (PT[at, mine].astype(f32) + GM[at, :].astype(f32)).astype(bf16)
+
+    for b in range(n_ctx):
+        g_plane[b].drain()
+    tokens(p.cd)
+    t_plane.start()
+    tokens(p.cx)
+    tokens(p.cy)
+    t_plane.middle()
+    tokens(p.c)
+
+    @pl.loop(0, p.depth)
+    def _(i):
+        for j in range(2):
+            at = rows_at(i + j * p.depth, own_rows)
+            O[rows_at(i, own_rows), j * nq : (j + 1) * nq] = dot_tn(XN[:, at], DPRE[...]).astype(bf16)
+
+    qkv_line.start()
+    down_line.step(4)
+    down_plane.start()
+    down_own.start()
+    up_line.combine()
+    up_line.step(1)
+    out_line.combine()
+    out_line.step(1)
+    gate_line.step(4)
+    gate_plane.start()
+    gate_own.start()
+    tok_copies = []
+    for i in range(n_ctx):
+        if i >= 2:
+            tok_copies[i - 2].wait()
+        at = pl.ds(i * (rows // n_ctx), rows // n_ctx)
+        TOK[i % 2] = t_plane.finish(at, i == 0)
+        tok_copies.append(pltpu.make_async_copy(TOK.at[i % 2], tok_out.at[at], copy_sems.at[12 + i % 2]))
+        tok_copies[-1].start()
+    down_plane.middle()
+    up_line.step(2)
+    out_line.step(2)
+    gate_plane.middle()
+    qkv_line.combine()
+    qkv_line.step(1)
+    up_line.step(3)
+    out_line.step(3)
+    qkv_line.step(2)
+    up_line.step(4)
+    up_plane.start()
+    up_own.start()
+    out_line.step(4)
+    out_plane.start()
+    out_own.start()
+    qkv_line.step(3)
+    up_plane.middle()
+    out_plane.middle()
+    qkv_line.step(4)
+    qkv_plane.start()
+    qkv_own.start()
+    qkv_plane.middle()
+    for plane, own in (
+        (down_plane, down_own), (gate_plane, gate_own), (up_plane, up_own), (out_plane, out_own), (qkv_plane, qkv_own),
+    ):
+        plane.finish()
+        own.wait()
+        plane.drain()
+    tok_copies[2].wait()
+    tok_copies[3].wait()
+    t_plane.drain()
+    for line in (down_line, gate_line, up_line, out_line, qkv_line):
+        line.drain()
+
+
+def backward_stage(xn, r, grow, qt, kt, vt, lse, o, gm, wqkv, wout, tabs, gate_part, up_part, down_part):
+    n_fsdp, n_ctx = lax.axis_size("fsdp"), lax.axis_size("ctx")
+    seq, width = xn.shape
+    rows = seq // n_ctx
+    half = rows // 2
+    cw = width // n_ctx
+    own = width // n_fsdp
+    depth = n_fsdp // 2
+    nq, nu = wqkv.shape[1], gate_part.shape[1]
+    unit = down_part.shape[0] // n_fsdp
+    qw = qt.shape[0]
+    outs = [
+        ((rows, width), f32), ((n_ctx, own, nq), bf16), ((n_ctx, own, cw), bf16), ((n_ctx, own, nu), bf16),
+        ((n_ctx, own, nu), bf16), ((n_ctx, unit, width), bf16),
+    ]
+    ins = (xn, r, grow, qt, kt, vt, lse, o, gm, wqkv, wout, tabs, gate_part, up_part, down_part)
+    scratch = [pltpu.VMEM(a.shape, a.dtype) for a in ins[:12]] + [
+        pltpu.VMEM((seq, HEAD_DIM), bf16),
+        pltpu.VMEM((seq, HEAD_DIM), bf16),
+        pltpu.VMEM((seq, HEAD_DIM), f32),
+        pltpu.VMEM((seq, HEAD_DIM), f32),
+        pltpu.VMEM((qw, rows), bf16),
+        pltpu.VMEM((qw, rows), f32),
+        pltpu.VMEM((seq, nq), bf16),
+        pltpu.VMEM((8, rows), f32),
+        pltpu.VMEM((seq, rows), f32),
+        pltpu.VMEM((seq, width), bf16),
+        pltpu.VMEM((n_ctx, 2, half, cw), bf16),
+        pltpu.VMEM((n_ctx, 2, rows, cw), bf16),
+        pltpu.VMEM((2, half, width), bf16),
+        pltpu.VMEM((2, rows, width), bf16),
+        pltpu.VMEM((2, rows // n_ctx, width), f32),
+        pltpu.VMEM((depth, unit, width), bf16),
+        pltpu.VMEM((5, unit, width), bf16),
+        pltpu.VMEM((depth, own, nu), bf16),
+        pltpu.VMEM((5, own, nu), bf16),
+        pltpu.VMEM((depth, own, nu), bf16),
+        pltpu.VMEM((5, own, nu), bf16),
+        pltpu.VMEM((depth, own, cw), bf16),
+        pltpu.VMEM((5, own, cw), bf16),
+        pltpu.VMEM((depth, own, nq), bf16),
+        pltpu.VMEM((5, own, nq), bf16),
+        pltpu.SemaphoreType.DMA((5, LineScatter.SEMS)),
+        pltpu.SemaphoreType.DMA((5, PlaneGather.SEMS + 1)),
+        pltpu.SemaphoreType.DMA((n_ctx + 1, PlaneScatter.SEMS)),
+        pltpu.SemaphoreType.DMA((14,)),
+    ]
+    flops = 4 * seq * width * (nq + cw) + 20 * qw * seq * seq
+    return call(backward_kernel, ins, outs, scratch, 3, flops, "backward_stage")
 
 
 def rotate(field, cosine, sine_table, direction):
@@ -855,7 +1272,9 @@
     qt = q.reshape(seq, qw).T
     kt = k.reshape(seq, kvw).T
     vt = v.reshape(seq, kvw).T
-    return x, xn, qt, kt, vt, lse, o, m, wqkv, wout, wgate, wup, cot_all, tabs
+    r = jnp.broadcast_to(r, (seq, 128))
+    grow = jnp.broadcast_to(gain, (8, width))
+    return xn, r, grow, qt, kt, vt, lse, o, m, wqkv, wout, wgate, wup, cot_all, tabs
 
 
 def middle_plain(m, cot_all, wgate, wup, wdown_o):
@@ -889,10 +1308,11 @@
     return output, down_raw, gate_raw, up_raw, gm
 
 
-def backward_plain(x, xn, gain, qt, kt, vt, lse, o, gm, wqkv, wout, tabs, gate_raw, up_raw, down_raw):
+def backward_plain(xn, r, grow, qt, kt, vt, lse, o, gm, wqkv, wout, tabs, gate_raw, up_raw, down_raw):
     n_ctx = lax.axis_size("ctx")
     c = lax.axis_index("ctx")
-    seq, width = x.shape
+    seq, width = xn.shape
+    r, gain = r[:, 0:1], grow[0:1]
     heads = HEADS // n_ctx
     qw = heads * HEAD_DIM
     kvw = kt.shape[0]
@@ -927,17 +1347,16 @@
     d_k = rotate(d_k, cosine, sine, -1.0).reshape(seq, kvw)
     d_pre = jnp.concatenate([d_q, d_k, d_v.reshape(seq, kvw)], axis=1).astype(bf16)
     qkv_grad = scatter(dot_tn(xn, d_pre), "fsdp")
-    xf = x.astype(f32)
-    r = lax.rsqrt(jnp.mean(xf * xf, axis=-1, keepdims=True) + eps_norm)
-    back = dot_nt(d_pre, wqkv) * (gain * r) - xf * (r * r * stat * (1.0 / width))
+    back = dot_nt(d_pre, wqkv) * (gain * r)
+    back = back - xn.astype(f32) * ((1.0 / gain) * (r * stat * (1.0 / width)))
     at = (jnp.arange(width, dtype=jnp.int32) // cw == c)[None, :]
     back = back + jnp.where(at, jnp.tile(gm.astype(f32), (1, n_ctx)), 0.0)
     grad_tokens = scatter(back, "ctx").astype(f32)
     qkv_all = gather(qkv_grad[None], "ctx")
-    out_all = gather(out_grad, "ctx", axis=1)
+    out_all = gather(out_grad[None], "ctx")
     gate_all = gather(gate_grad[None], "ctx")
     up_all = gather(up_grad[None], "ctx")
-    down_all = gather(down_grad, "ctx")
+    down_all = gather(down_grad[None], "ctx")
     return grad_tokens, qkv_all, out_all, gate_all, up_all, down_all
 
 
@@ -997,15 +1416,14 @@
     )
 
     forward = forward_stage if kernels else forward_plain
-    x, xn, qt, kt, vt, lse, o, m, wqkv, wout, wgate, wup, cot_all, tabs = forward(
+    xn, r, grow, qt, kt, vt, lse, o, m, wqkv, wout, wgate, wup, cot_all, tabs = forward(
         tokens, tab, gains, wqkv_o, wout_o, wgate_o, wup_o, cotangent
     )
     middle = middle_stage if kernels else middle_plain
     output, down_raw, gate_raw, up_raw, gm = middle(m, cot_all, wgate, wup, wdown_o)
-    gain_row = gather(gain_attn, "fsdp").astype(f32)[None, :]
-    backward = backward_plain
+    backward = backward_stage if kernels else backward_plain
     grad_tokens, qkv_all, out_all, gate_all, up_all, down_all = backward(
-        x, xn, gain_row, qt, kt, vt, lse, o, gm, wqkv, wout, tabs, gate_raw, up_raw, down_raw
+        xn, r, grow, qt, kt, vt, lse, o, gm, wqkv, wout, tabs, gate_raw, up_raw, down_raw
     )
 
     qkv_all = qkv_all.astype(f32)
@@ -1019,14 +1437,14 @@
     grad_query = joined(qkv_all[:, :, :qw])
     grad_key = kv_part(qkv_all[:, :, qw : qw + kvw])
     grad_value = kv_part(qkv_all[:, :, qw + kvw :])
-    grad_out = out_all.astype(f32)
+    grad_out = joined(out_all.astype(f32))
 
     def spread(full):
         full = full.reshape(n_ctx, own_rows, n_fsdp, unit)
         return full.transpose(1, 2, 0, 3).reshape(own_rows, ff_width).astype(f32)
 
     raw_gate, raw_up = spread(gate_all), spread(up_all)
-    grad_down = down_all.astype(f32)
+    grad_down = down_all.astype(f32).reshape(-1, width)
 
     def gain_term(grad, w):
         return jnp.sum(grad * w.astype(f32), axis=1)

time: 984 us -> 613 us (0.62)
  waiting for transfers between devices: 416 us -> 0 us
  Pallas kernels: 269 us -> 501 us
  matrix products: 99.2 us -> 0 us
  other arithmetic: 61.6 us -> 23.6 us
  local copies, waits for them, and re-layouts: 94.5 us -> 79.9 us
  between operations: 15 us -> 1.06 us
  blocking collectives: 12.1 us -> 0 us
    reduce_scatter x7 -> x0, waiting for transfers between devices: 323 us -> none  [scatter(): lax.psum_scatter(x.astype(bf16), axis_name, scatter_dimension=axis, tiled...]
    pallas_call x2 -> x3, Pallas kernels: 269 us -> 501 us  [call(): pl.pallas_call(kernel, out_shape=[jax.ShapeDtypeStruct(s, d) for s, d in...]
    dot_general x9 -> x0, matrix products: 99.2 us -> none  [the longest x1 24.5 us: backward_plain(): d_probs = jnp.einsum('qkgd,lkd->kgql', d_att, v, preferred_element_type=f32)]
    all_gather x5 -> x0, waiting for transfers between devices: 90.2 us -> none  [gather(): return lax.all_gather(x, axis_name, axis=axis, tiled=True)]
    another operation x3 -> x0, other arithmetic: 29.1 us -> none
    convert_element_type x6 -> x4, local copies, waits for them, and re-layouts: 36 us -> 17.9 us  [spread(): return full.transpose(1, 2, 0, 3).reshape(own_rows, ff_width).astype(f32)]
    all_gather x1 -> x0, blocking collectives: 12.1 us -> none  [gather(): return lax.all_gather(x, axis_name, axis=axis, tiled=True)]
    convert_element_type x5 -> x0, other arithmetic: 10.9 us -> none  [the longest x1 5.27 us: per_device(): grad_down = down_all.astype(f32)]
  transfers between devices with their start and end apart: 12 -> 0, of which waited for: 10 -> 0; matrix products, arithmetic and copies ran while one was open for 22% -> 0% of each run, Pallas kernels for 0% -> 0%
where the time goes in v4:
time: 613 us; the launch traced here: 605 us
  Pallas kernels  501 us (82%)
  local copies, waits for them, and re-layouts  79.9 us (13%)
  other arithmetic  23.6 us (4%)
    pallas_call x3, Pallas kernels, call(): pl.pallas_call(kernel, out_shape=[jax.ShapeDtypeStruct(s, d) for s, d in...  501 us
    unnamed x39, local copies, waits for them, and re-layouts  40.3 us
    convert_element_type x4, local copies, waits for them, and re-layouts, spread(): return full.transpose(1, 2, 0, 3).reshape(own_rows, ff_width).astype(f32)  17.9 us

profile of v4, /device:TPU:8, one launch (start us, length us, event | category | flops | bytes accessed | tf_op | source)
XLA Modules:
  0.0 605.1 jit_solution(10907405264356453627)
XLA Ops:
  0.7 1.9 constant_dynamic-slice_fusion.3
  4.4 4.6 copy.27
  8.9 4.5 copy.29
  13.5 2.3 constant_dynamic-slice_fusion.1
  17.0 2.9 copy.28
  19.9 2.3 bitcast_convert_fusion.1
  22.2 2.9 copy.30
  25.1 3.2 multiply_convert_fusion
  29.8 151.3 %forward_stage.1 = (bf16[1024,2048]{1,0:T(8,128)(2,1)}, f32[1024,128]{1,0:T(8,128)}, f32[8,2048]{1,0:T(8,128)}, bf16[512,1024]{1,0:T(8,128)(2,1)}, bf16[64,1024]...) custom-call(bf16[256,2048]{1,0:T(8,128)(2,1)} %tok.1, ...), custom_call_target="tpu_custom_call" | custom-call | flops 9126805504 | bytes 67108864 | tf_op jit(solution)/shard_map/forward_stage/pallas_call | solution.py:254
  182.1 118.2 %middle_stage.1 = (bf16[256,2048]{1,0:T(8,128)(2,1)}, bf16[1408,2048]{1,0:T(8,128)(2,1)}, bf16[2048,1408]{1,0:T(8,128)(2,1)}, bf16[2048,1408]{1,0:T(8,128)(2,1)}, bf16[1024,512]{1,0:T(8,128)(2,1)}) custom-call(bf16[1024,2048]{1,0:T(8,128)(2,1)} %get-tuple-element.37.m_in, bf16[1024,2048]{1,0:T(8,128)(2,1)} %get-tuple-element.38.cot_in, ...), custom_call_target="tpu_custom_call" | custom-call | flops 53150220288 | bytes 67108864 | tf_op jit(solution)/shard_map/middle_stage/pallas_call | solution.py:254
  300.3 231.1 %backward_stage.1 = (f32[256,2048]{1,0:T(8,128)}, bf16[4,256,640]{2,1,0:T(8,128)(2,1)}, bf16[4,256,512]{2,1,0:T(8,128)(2,1)}, bf16[4,256,1408]{2,1,0:T(8,128)(2,...) custom-call(bf16[1024,2048]{1,0:T(8,128)(2,1)} %get-tuple-element.42.xn_in, ...), custom_call_target="tpu_custom_call" | custom-call | flops 20401094656 | bytes 67108864 | tf_op jit(solution)/shard_map/backward_stage/pallas_call | solution.py:254
  531.3 5.4 copy.37
  536.7 5.8 copy.38
  542.6 3.4 copy.40
  546.0 3.3 copy.41
  552.0 5.8 bitcast_multiply_fusion
  557.8 6.2 %copy.48 = f32[256,5632]{1,0:T(8,128)} copy(f32[256,5632]{0,1:T(8,128)} %get-tuple-element.83) | data formatting | bytes 11534336
  564.0 6.2 %copy.49 = f32[256,5632]{1,0:T(8,128)} copy(f32[256,5632]{0,1:T(8,128)} %get-tuple-element.74) | data formatting | bytes 11534336
  570.8 1.5 convert_element_type.83
  572.3 1.5 copy-done.5
  573.8 1.6 slice_bitcast_fusion
  575.4 1.9 copy.31
  577.3 2.3 copy.32
  579.6 1.6 multiply_reduce_fusion
  581.2 2.4 slice_bitcast_fusion.2
  585.9 1.8 copy.44
  587.7 1.5 convert_bitcast_fusion
  589.2 1.8 copy.43
  591.0 3.0 copy.47
  594.1 3.5 bitcast_convert_fusion
  599.2 2.5 copy.52
  601.7 3.1 copy.53
  (46 shorter events, 12.7 us)
Async XLA Ops:
  0.6 180.5 %copy-start = (bf16[704,2048]{1,0:T(8,128)(2,1)S(1)}, bf16[704,2048]{1,0:T(8,128)(2,1)}, u32[]{:S(2)}) copy-start(bf16[704,2048]{1,0:T(8,128)(2,1)} %param.22) | copy-start | bytes 8650756
  19.9 5.2 copy-start.12
  25.1 3.2 copy-start.11
  25.1 4.1 copy-start.10
  536.7 5.8 copy-start.7
  546.0 4.3 copy-start.2
  546.0 5.2 copy-start.3
  546.0 6.0 copy-start.4
  572.3 1.5 copy-start.5
  579.6 5.2 copy-start.8
  581.2 4.0 copy-start.9
  591.0 3.0 copy-start.6
  599.2 5.6 copy-start.1

commit v5 on v4

--- a/solution.py
+++ b/solution.py
@@ -1,3 +1,5 @@
+import functools
+
 import jax
 import jax.numpy as jnp
 from jax import lax
@@ -90,8 +92,8 @@
 
     def __init__(self, place, own, full, sems):
         self.p, self.own, self.full, self.sems = place, own, full, sems
-        self.rows = own.shape[0]
         self.n = place.depth
+        self.rows = full.shape[0] // (2 * self.n)
 
     def view(self, level, core):
         start = pl.multiple_of((2 * level + core) * self.rows, 16)
@@ -100,7 +102,7 @@
     def to_up(self, hop):
         p = self.p
         level = p.z - (hop - 1)
-        src = self.own if hop == 1 else self.view(level, p.core)
+        src = self.own if hop == 1 and self.own is not None else self.view(level, p.core)
         return remote(
             src, self.view(level, p.core), self.sems.at[hop - 1], self.sems.at[6 + hop - 1], p.up
         )
@@ -108,14 +110,14 @@
     def to_down(self, hop):
         p = self.p
         level = p.z + (hop - 1)
-        src = self.own if hop == 1 else self.view(level, p.core)
+        src = self.own if hop == 1 and self.own is not None else self.view(level, p.core)
         return remote(
             src, self.view(level, p.core), self.sems.at[3 + hop - 1], self.sems.at[9 + hop - 1], p.down
         )
 
     def to_sibling(self, level, own=False):
         p = self.p
-        src = self.own if own else self.view(level, p.core)
+        src = self.own if own and self.own is not None else self.view(level, p.core)
         return remote(
             src, self.view(level, p.core), self.sems.at[12 + level], self.sems.at[16 + level], p.sibling
         )
@@ -136,7 +138,8 @@
             self.to_down(1).start()
 
         self.to_sibling(p.z, True).start()
-        self.local().start()
+        if self.own is not None:
+            self.local().start()
 
     def arrived(self, level, sem):
         view = self.view(level, self.p.core)
@@ -169,7 +172,8 @@
 
     def finish(self):
         p = self.p
-        self.local().wait()
+        if self.own is not None:
+            self.local().wait()
         for level in range(self.n):
             view = self.view(level, p.other)
             remote(view, view, self.sems.at[0], self.sems.at[16 + level], p.sibling).wait_recv()
@@ -421,10 +425,11 @@
 
 
 def forward_kernel(
-    tok, tab, gains, wqkv_o, wout_o, wgate_o, wup_o, cot,
+    tok, tab, gains, gcol, w_query, w_key, w_value, w_out, w_gate, w_up, cot,
     xn_out, r_out, grow_out, qt_out, kt_out, vt_out, lse_out, o_out, m_out,
     wqkv_out, wout_out, wgate, wup, cot_all, tab_out,
     X, XN, QT, KT, VT, K, LSE, O, M, WQ, WO, TAB, G8, GROW, BIAS, OT, R1,
+    WK, WV, GF, UF, GO, UO, GCOL,
     line_sems, plane_sems, copy_sems,
 ):
     p = Place()
@@ -436,13 +441,24 @@
     cw = O.shape[1] // n_ctx
     scale = HEAD_DIM ** (-0.5)
 
+    mine = rows_at(p.f, WK.shape[0])
+    loads = []
+    for i, (src, dst) in enumerate(
+        (
+            (w_query.at[:, rows_at(p.c, qw)], WQ.at[mine, pl.ds(0, qw)]),
+            (w_key, WK), (w_value, WV), (w_gate, GF), (w_up, UF), (gcol, GCOL),
+        )
+    ):
+        loads.append(pltpu.make_async_copy(src, dst, copy_sems.at[15 + i]))
+        loads[-1].start()
+
     p.barrier()
 
     gain_line = LineGather(p, gains, G8, line_sems.at[0])
-    qkv_line = LineGather(p, wqkv_o, WQ, line_sems.at[1])
-    out_line = LineGather(p, wout_o, WO, line_sems.at[2])
-    gate_line = LineGather(p, wgate_o, wgate, line_sems.at[3])
-    up_line = LineGather(p, wup_o, wup, line_sems.at[4])
+    qkv_line = LineGather(p, None, WQ, line_sems.at[1])
+    out_line = LineGather(p, w_out.at[:, rows_at(p.c, cw)], WO, line_sems.at[2])
+    gate_line = LineGather(p, GO, wgate, line_sems.at[3])
+    up_line = LineGather(p, UO, wup, line_sems.at[4])
 
     def row_block(ref):
         return (
@@ -474,16 +490,38 @@
     m_plane = [PlaneGather(p, *col_block(M, b), plane_sems.at[7 + b]) for b in range(n_ctx)]
 
     gain_line.start()
-    qkv_line.start()
     tab_plane.start()
     tok_plane.start()
     out_line.start()
+    for i in range(3):
+        loads[i].wait()
+    for c in range(n_ctx):
+
+        @pl.when(p.c == c)
+        def _():
+            WQ[mine, qw : qw + HEAD_DIM] = WK[:, HEAD_DIM * c : HEAD_DIM * (c + 1)]
+            WQ[mine, qw + HEAD_DIM :] = WV[:, HEAD_DIM * c : HEAD_DIM * (c + 1)]
+
+    qkv_line.start()
     own_tok = pltpu.make_async_copy(tok, X.at[rows_at(p.c, rows)], copy_sems.at[0])
     own_tab = pltpu.make_async_copy(tab, TAB.at[p.c], copy_sems.at[1])
     own_cot = pltpu.make_async_copy(cot, cot_all.at[rows_at(p.c, rows)], copy_sems.at[2])
     own_tok.start()
     own_tab.start()
     own_cot.start()
+
+    for i in range(3, 6):
+        loads[i].wait()
+    unit = GO.shape[1] // (2 * p.depth)
+    for c in range(n_ctx):
+
+        @pl.when(p.c == c)
+        def _():
+            for f in range(2 * p.depth):
+                at = (f * n_ctx + c) * unit
+                for src, dst in ((GF, GO), (UF, UO)):
+                    part = src[:, at : at + unit].astype(f32) * GCOL[:, 0:1]
+                    dst[:, f * unit : (f + 1) * unit] = part.astype(bf16)
 
     gain_line.hop(1)
     tab_plane.middle()
@@ -574,9 +612,9 @@
 
     def middle(b):
         at = pl.ds(b * rows, rows)
-        mine = rows_at(p.c, cw)
-        mid = X[at, mine].astype(f32) + dot(O[at, :], WO[...])
-        M[at, mine] = mid.astype(bf16)
+        cols = rows_at(p.c, cw)
+        mid = X[at, cols].astype(f32) + dot(O[at, :], WO[...])
+        M[at, cols] = mid.astype(bf16)
         m_plane[b].start()
 
     attend(0)
@@ -630,13 +668,14 @@
         plane.drain()
 
 
-def forward_stage(tok, tab, gains, wqkv_o, wout_o, wgate_o, wup_o, cot):
+def forward_stage(tok, tab, gains, gcol, w_query, w_key, w_value, w_out, w_gate, w_up, cot):
     n_fsdp, n_ctx = lax.axis_size("fsdp"), lax.axis_size("ctx")
     rows, width = tok.shape
     seq = rows * n_ctx
-    whole = n_fsdp * wqkv_o.shape[0]
-    nq, nw, nu = wqkv_o.shape[1], wout_o.shape[1], wgate_o.shape[1]
+    own = w_query.shape[0]
+    whole = n_fsdp * own
     qw = HEADS // n_ctx * HEAD_DIM
+    nq, nw, nu = qw + 2 * HEAD_DIM, width // n_ctx, w_gate.shape[1] // n_ctx
     heads = qw // HEAD_DIM
     tab_shape = (n_ctx,) + tab.shape
     outs = [
@@ -662,11 +701,18 @@
         pltpu.VMEM((seq, rows), f32),
         pltpu.VMEM((qw, rows), f32),
         pltpu.VMEM((seq, 128), f32),
+        pltpu.VMEM(w_key.shape, bf16),
+        pltpu.VMEM(w_value.shape, bf16),
+        pltpu.VMEM(w_gate.shape, bf16),
+        pltpu.VMEM(w_up.shape, bf16),
+        pltpu.VMEM((own, nu), bf16),
+        pltpu.VMEM((own, nu), bf16),
+        pltpu.VMEM(gcol.shape, f32),
         pltpu.SemaphoreType.DMA((5, LineGather.SEMS)),
         pltpu.SemaphoreType.DMA((11, PlaneGather.SEMS)),
-        pltpu.SemaphoreType.DMA((15,)),
+        pltpu.SemaphoreType.DMA((21,)),
     ]
-    ins = (tok, tab, gains, wqkv_o, wout_o, wgate_o, wup_o, cot)
+    ins = (tok, tab, gains, gcol, w_query, w_key, w_value, w_out, w_gate, w_up, cot)
     flops = 2 * seq * width * (nq + nw) + 8 * heads * seq * seq * HEAD_DIM
     return call(forward_kernel, ins, outs, scratch, 1, flops, "forward_stage")
 
@@ -680,7 +726,7 @@
 
 
 def middle_kernel(
-    m_in, cot_in, wgate_in, wup_in, wdown_o,
+    m_in, cot_in, wgate_in, wup_in, w_down,
     y_out, down_part, gate_part, up_part, gm_out,
     M, COT, WG, WU, WD, GATE, UP, HID, R2, PD, PH, D1, D2, H1, H2, GM, Y, STAGE_D, STAGE,
     line_sems, plane_sems, copy_sems, stage_sems,
@@ -698,7 +744,9 @@
         loads[-1].start()
 
     p.barrier()
-    down_line = LineGather(p, wdown_o, WD, line_sems.at[0])
+    unit = w_down.shape[0] // n_ctx
+    down_own = w_down.at[pl.ds(pl.multiple_of(p.c * unit, 16), unit)]
+    down_line = LineGather(p, down_own, WD, line_sems.at[0])
     down_line.start()
 
     loads[0].wait()
@@ -843,7 +891,7 @@
         h_plane[b].drain()
 
 
-def middle_stage(m, cot_all, wgate, wup, wdown_o):
+def middle_stage(m, cot_all, wgate, wup, w_down):
     n_fsdp, n_ctx = lax.axis_size("fsdp"), lax.axis_size("ctx")
     seq, width = m.shape
     rows = seq // n_ctx
@@ -879,7 +927,7 @@
         pltpu.SemaphoreType.DMA((4,)),
     ]
     flops = 18 * seq * width * units
-    return call(middle_kernel, (m, cot_all, wgate, wup, wdown_o), outs, scratch, 2, flops, "middle_stage")
+    return call(middle_kernel, (m, cot_all, wgate, wup, w_down), outs, scratch, 2, flops, "middle_stage")
 
 
 def backward_kernel(
@@ -1198,6 +1246,66 @@
     return call(backward_kernel, ins, outs, scratch, 3, flops, "backward_stage")
 
 
+def finish_kernel(
+    unit, qkv, out, gate, up, down, tok, y, w_query, w_key, w_value, w_gate, w_up, g1, g2,
+    o_query, o_key, o_value, o_out, o_gate, o_up, o_down, o_tok, o_y, o_g1, o_g2,
+):
+    n_ctx = qkv.shape[0]
+    qw = o_query.shape[1] // n_ctx
+    cw = out.shape[2]
+    for c in range(n_ctx):
+        o_query[:, c * qw : (c + 1) * qw] = qkv[c, :, 0:qw].astype(f32)
+        o_key[:, c * HEAD_DIM : (c + 1) * HEAD_DIM] = qkv[c, :, qw : qw + HEAD_DIM].astype(f32)
+        o_value[:, c * HEAD_DIM : (c + 1) * HEAD_DIM] = qkv[c, :, qw + HEAD_DIM :].astype(f32)
+        o_out[:, c * cw : (c + 1) * cw] = out[c].astype(f32)
+
+    def total(ref, w):
+        return jnp.sum(ref[...] * w[...].astype(f32), axis=-1, keepdims=True)
+
+    first = total(o_query, w_query) + total(o_key, w_key) + total(o_value, w_value)
+    o_g1[...] = jnp.broadcast_to(first / g1[:, 0:1], o_g1.shape)
+    gain = g2[:, 0:1]
+    for src, dst in ((gate, o_gate), (up, o_up)):
+        for f in range(src.shape[2] // unit):
+            for c in range(n_ctx):
+                at = (f * n_ctx + c) * unit
+                dst[:, at : at + unit] = src[c, :, f * unit : (f + 1) * unit].astype(f32) * gain
+    second = total(o_gate, w_gate) + total(o_up, w_up)
+    o_g2[...] = jnp.broadcast_to(second / gain, o_g2.shape)
+    o_down[...] = down[...].astype(f32)
+    o_tok[...] = tok[...]
+    o_y[...] = y[...]
+
+
+def finish_stage(qkv, out, gate, up, down, tok, y, w_query, w_key, w_value, w_gate, w_up, g1, g2):
+    steps = 4
+    n_fsdp = lax.axis_size("fsdp")
+    own = w_query.shape[0]
+    down = down.reshape(-1, down.shape[-1])
+    unit = gate.shape[2] // n_fsdp
+
+    def spec(shape):
+        if len(shape) == 3:
+            return pl.BlockSpec((shape[0], shape[1] // steps, shape[2]), lambda i: (0, i, 0))
+        return pl.BlockSpec((shape[0] // steps, shape[1]), lambda i: (i, 0))
+
+    ins = (qkv, out, gate, up, down, tok, y, w_query, w_key, w_value, w_gate, w_up, g1, g2)
+    outs = [
+        (w_query.shape, f32), (w_key.shape, f32), (w_value.shape, f32), ((own, out.shape[0] * out.shape[2]), f32),
+        (w_gate.shape, f32), (w_up.shape, f32), (down.shape, f32), (tok.shape, f32), (y.shape, bf16),
+        ((own, 128), f32), ((own, 128), f32),
+    ]
+    return pl.pallas_call(
+        functools.partial(finish_kernel, unit),
+        grid=(steps,),
+        out_shape=[jax.ShapeDtypeStruct(s, d) for s, d in outs],
+        in_specs=[spec(a.shape) for a in ins],
+        out_specs=[spec(s) for s, d in outs],
+        compiler_params=pltpu.CompilerParams(vmem_limit_bytes=56 * 2**20),
+        name="finish_stage",
+    )(*ins)
+
+
 def rotate(field, cosine, sine_table, direction):
     half_width = field.shape[-1] // 2
     first_half = field[..., :half_width]
@@ -1229,9 +1337,31 @@
     return (index[None, :] <= index[:, None]) & (index[None, :] >= begin[:, None])
 
 
-def forward_plain(tok, tab, gains, wqkv_o, wout_o, wgate_o, wup_o, cot):
-    n_ctx = lax.axis_size("ctx")
+def forward_plain(tok, tab, gains, gcol, w_query, w_key, w_value, w_out, w_gate, w_up, cot):
+    n_ctx, n_fsdp = lax.axis_size("ctx"), lax.axis_size("fsdp")
     c = lax.axis_index("ctx")
+    own_rows = w_query.shape[0]
+    qw = HEADS // n_ctx * HEAD_DIM
+    copies = max(1, n_ctx // KV_HEADS)
+    kvw = max(1, KV_HEADS // n_ctx) * HEAD_DIM
+    unit = w_gate.shape[1] // (n_fsdp * n_ctx)
+    cw = tok.shape[1] // n_ctx
+    wqkv_o = jnp.concatenate(
+        [
+            columns(w_query, c * qw, qw),
+            columns(w_key, (c // copies) * kvw, kvw),
+            columns(w_value, (c // copies) * kvw, kvw),
+        ],
+        axis=1,
+    )
+    wout_o = columns(w_out, c * cw, cw)
+
+    def units(w):
+        parts = w.reshape(own_rows, n_fsdp, n_ctx, unit)
+        mine = lax.dynamic_index_in_dim(parts, c, axis=2, keepdims=False)
+        return (gcol[:, 0:1] * mine.reshape(own_rows, n_fsdp * unit)).astype(bf16)
+
+    wgate_o, wup_o = units(w_gate), units(w_up)
     x = gather(tok, "ctx")
     tabs = gather(tab[None], "ctx")
     wqkv = gather(wqkv_o, "fsdp")
@@ -1277,9 +1407,11 @@
     return xn, r, grow, qt, kt, vt, lse, o, m, wqkv, wout, wgate, wup, cot_all, tabs
 
 
-def middle_plain(m, cot_all, wgate, wup, wdown_o):
+def middle_plain(m, cot_all, wgate, wup, w_down):
     n_ctx = lax.axis_size("ctx")
     c = lax.axis_index("ctx")
+    unit = w_down.shape[0] // n_ctx
+    wdown_o = lax.dynamic_slice_in_dim(w_down, c * unit, unit, axis=0)
     seq, width = m.shape
     rows = seq // n_ctx
     cw = width // n_ctx
@@ -1360,6 +1492,45 @@
     return grad_tokens, qkv_all, out_all, gate_all, up_all, down_all
 
 
+def finish_plain(qkv_all, out_all, gate_all, up_all, down_all, tok, y, w_query, w_key, w_value, w_gate, w_up, g1, g2):
+    n_ctx, n_fsdp = lax.axis_size("ctx"), lax.axis_size("fsdp")
+    own_rows = w_query.shape[0]
+    qw = HEADS // n_ctx * HEAD_DIM
+    copies = max(1, n_ctx // KV_HEADS)
+    kvw = max(1, KV_HEADS // n_ctx) * HEAD_DIM
+    ff_width = w_gate.shape[1]
+    unit = ff_width // (n_fsdp * n_ctx)
+    qkv_all = qkv_all.astype(f32)
+
+    def joined(part):
+        return jnp.moveaxis(part, 0, 1).reshape(own_rows, -1)
+
+    def kv_part(part):
+        return joined(part.reshape(n_ctx // copies, copies, own_rows, kvw).sum(axis=1))
+
+    grad_query = joined(qkv_all[:, :, :qw])
+    grad_key = kv_part(qkv_all[:, :, qw : qw + kvw])
+    grad_value = kv_part(qkv_all[:, :, qw + kvw :])
+    grad_out = joined(out_all.astype(f32))
+
+    def spread(full):
+        full = full.reshape(n_ctx, own_rows, n_fsdp, unit)
+        return full.transpose(1, 2, 0, 3).reshape(own_rows, ff_width).astype(f32)
+
+    raw_gate, raw_up = spread(gate_all), spread(up_all)
+    grad_down = down_all.astype(f32).reshape(-1, down_all.shape[-1])
+
+    def gain_term(grad, w):
+        return jnp.sum(grad * w.astype(f32), axis=1, keepdims=True)
+
+    first = gain_term(grad_query, w_query) + gain_term(grad_key, w_key) + gain_term(grad_value, w_value)
+    second = gain_term(raw_gate, w_gate) + gain_term(raw_up, w_up)
+    g1, g2 = g1[:, 0:1], g2[:, 0:1]
+    return (
+        grad_query, grad_key, grad_value, grad_out, g2 * raw_gate, g2 * raw_up, grad_down, tok, y, first / g1, second,
+    )
+
+
 def per_device(
     tokens,
     positions,
@@ -1374,39 +1545,13 @@
     w_down,
     cotangent,
 ):
-    n_ctx = lax.axis_size("ctx")
-    n_fsdp = lax.axis_size("fsdp")
-    kernels = n_ctx == 4 and n_fsdp == 8
+    kernels = lax.axis_size("ctx") == 4 and lax.axis_size("fsdp") == 8
     c = lax.axis_index("ctx")
-    rows, width = tokens.shape
+    rows = tokens.shape[0]
     own_rows = w_query.shape[0]
-    qw = HEADS // n_ctx * HEAD_DIM
-    copies = max(1, n_ctx // KV_HEADS)
-    kvw = max(1, KV_HEADS // n_ctx) * HEAD_DIM
-    cw = width // n_ctx
-    ff_width = w_gate.shape[1]
-    unit = ff_width // (n_fsdp * n_ctx)
-    gain_one = gain_attn.astype(f32)[:, None]
-    gain_two = gain_mlp.astype(f32)[:, None]
-
-    wqkv_o = jnp.concatenate(
-        [
-            columns(w_query, c * qw, qw),
-            columns(w_key, (c // copies) * kvw, kvw),
-            columns(w_value, (c // copies) * kvw, kvw),
-        ],
-        axis=1,
-    )
-    wout_o = columns(w_out, c * cw, cw)
-
-    def units(w):
-        parts = w.reshape(own_rows, n_fsdp, n_ctx, unit)
-        mine = lax.dynamic_index_in_dim(parts, c, axis=2, keepdims=False)
-        return (gain_two * mine.reshape(own_rows, n_fsdp * unit)).astype(bf16)
-
-    wgate_o, wup_o = units(w_gate), units(w_up)
-    wdown_o = lax.dynamic_slice_in_dim(w_down, c * unit, unit, axis=0)
     gains = jnp.broadcast_to(gain_attn[None, :], (16, own_rows))
+    gain_one = jnp.broadcast_to(gain_attn.astype(f32)[:, None], (own_rows, 128))
+    gain_two = jnp.broadcast_to(gain_mlp.astype(f32)[:, None], (own_rows, 128))
     frequency = theta_base ** (-(jnp.arange(HEAD_DIM // 2, dtype=f32) * 2.0) / HEAD_DIM)
     angles = frequency[:, None] * positions.astype(f32)[None, :]
     begin = c * rows + jnp.arange(rows, dtype=jnp.int32) - positions
@@ -1417,55 +1562,20 @@
 
     forward = forward_stage if kernels else forward_plain
     xn, r, grow, qt, kt, vt, lse, o, m, wqkv, wout, wgate, wup, cot_all, tabs = forward(
-        tokens, tab, gains, wqkv_o, wout_o, wgate_o, wup_o, cotangent
+        tokens, tab, gains, gain_two, w_query, w_key, w_value, w_out, w_gate, w_up, cotangent
     )
     middle = middle_stage if kernels else middle_plain
-    output, down_raw, gate_raw, up_raw, gm = middle(m, cot_all, wgate, wup, wdown_o)
+    y, down_raw, gate_raw, up_raw, gm = middle(m, cot_all, wgate, wup, w_down)
     backward = backward_stage if kernels else backward_plain
-    grad_tokens, qkv_all, out_all, gate_all, up_all, down_all = backward(
+    tok, qkv_all, out_all, gate_all, up_all, down_all = backward(
         xn, r, grow, qt, kt, vt, lse, o, gm, wqkv, wout, tabs, gate_raw, up_raw, down_raw
     )
-
-    qkv_all = qkv_all.astype(f32)
-
-    def joined(part):
-        return jnp.moveaxis(part, 0, 1).reshape(own_rows, -1)
-
-    def kv_part(part):
-        return joined(part.reshape(n_ctx // copies, copies, own_rows, kvw).sum(axis=1))
-
-    grad_query = joined(qkv_all[:, :, :qw])
-    grad_key = kv_part(qkv_all[:, :, qw : qw + kvw])
-    grad_value = kv_part(qkv_all[:, :, qw + kvw :])
-    grad_out = joined(out_all.astype(f32))
-
-    def spread(full):
-        full = full.reshape(n_ctx, own_rows, n_fsdp, unit)
-        return full.transpose(1, 2, 0, 3).reshape(own_rows, ff_width).astype(f32)
-
-    raw_gate, raw_up = spread(gate_all), spread(up_all)
-    grad_down = down_all.astype(f32).reshape(-1, width)
-
-    def gain_term(grad, w):
-        return jnp.sum(grad * w.astype(f32), axis=1)
-
-    grad_gain_one = (
-        gain_term(grad_query, w_query) + gain_term(grad_key, w_key) + gain_term(grad_value, w_value)
-    ) / gain_one[:, 0]
-    grad_gain_two = gain_term(raw_gate, w_gate) + gain_term(raw_up, w_up)
-    return (
-        output,
-        grad_tokens,
-        grad_gain_one,
-        grad_gain_two,
-        grad_query,
-        grad_key,
-        grad_value,
-        grad_out,
-        gain_two * raw_gate,
-        gain_two * raw_up,
-        grad_down,
+    finish = finish_stage if kernels else finish_plain
+    g_query, g_key, g_value, g_out, g_gate, g_up, g_down, tok, y, g_one, g_two = finish(
+        qkv_all, out_all, gate_all, up_all, down_all, tok, y,
+        w_query, w_key, w_value, w_gate, w_up, gain_one, gain_two,
     )
+    return (y, tok, g_one[:, 0], g_two[:, 0], g_query, g_key, g_value, g_out, g_gate, g_up, g_down)
 
 
 def solution(mesh):

time: 613 us -> 529 us (0.86)
  local copies, waits for them, and re-layouts: 79.9 us -> 5.12 us
  other arithmetic: 23.6 us -> 1.62 us
  Pallas kernels: 501 us -> 516 us
    unnamed x39 -> x2, local copies, waits for them, and re-layouts: 40.3 us -> 0.01 us
    convert_element_type x6 -> x0, local copies, waits for them, and re-layouts: 23.7 us -> none  [the longest x4 17.9 us: spread(): return full.transpose(1, 2, 0, 3).reshape(own_rows, ff_width).astype(f32)]
    pallas_call x0 -> x1, Pallas kernels: none -> 16.7 us  [finish_stage(): pl.pallas_call(functools.partial(finish_kernel, unit), grid=(steps,), out...]
    convert_element_type x5 -> x0, other arithmetic: 8.24 us -> none  [the longest x3 6.76 us: units(): return (gain_two * mine.reshape(own_rows, n_fsdp * unit)).astype(bf16)]
    transpose x5 -> x0, local copies, waits for them, and re-layouts: 7.32 us -> none  [joined(): return jnp.moveaxis(part, 0, 1).reshape(own_rows, -1)]
where the time goes in v5:
time: 529 us; the launch traced here: 524 us
  Pallas kernels  516 us (98%)
    pallas_call x3, Pallas kernels, call(): pl.pallas_call(kernel, out_shape=[jax.ShapeDtypeStruct(s, d) for s, d in...  500 us
    pallas_call x1, Pallas kernels, finish_stage(): pl.pallas_call(functools.partial(finish_kernel, unit), grid=(steps,), out...  16.7 us

profile of v5, /device:TPU:8, one launch (start us, length us, event | category | flops | bytes accessed | tf_op | source)
XLA Modules:
  0.0 523.9 jit_solution(18358856840521763940)
XLA Ops:
  0.6 0.8 fusion
  1.4 0.2 multiply_cosine_fusion
  1.6 0.6 pad_maximum_fusion.tab
  2.3 1.4 broadcast_in_dim.10.gcol.g2
  3.7 1.3 broadcast_in_dim.9.gains
  5.0 151.3 %forward_stage.1 = (bf16[1024,2048]{1,0:T(8,128)(2,1)}, f32[1024,128]{1,0:T(8,128)}, f32[8,2048]{1,0:T(8,128)}, bf16[512,1024]{1,0:T(8,128)(2,1)}, bf16[64,1024]...) custom-call(bf16[256,2048]{1,0:T(8,128)(2,1)} %tok.1, ...), custom_call_target="tpu_custom_call" | custom-call | flops 9126805504 | bytes 67108864 | tf_op jit(solution)/shard_map/forward_stage/pallas_call | solution.py:258
  156.3 117.8 %middle_stage.1 = (bf16[256,2048]{1,0:T(8,128)(2,1)}, bf16[1408,2048]{1,0:T(8,128)(2,1)}, bf16[2048,1408]{1,0:T(8,128)(2,1)}, bf16[2048,1408]{1,0:T(8,128)(2,1)}, bf16[1024,512]{1,0:T(8,128)(2,1)}) custom-call(bf16[1024,2048]{1,0:T(8,128)(2,1)} %get-tuple-element.56.m_in, bf16[1024,2048]{1,0:T(8,128)(2,1)} %get-tuple-element.57.cot_in, ...), custom_call_target="tpu_custom_call" | custom-call | flops 53150220288 | bytes 67108864 | tf_op jit(solution)/shard_map/middle_stage/pallas_call | solution.py:258
  274.2 0.0 copy-start
  274.2 230.4 %backward_stage.1 = (f32[256,2048]{1,0:T(8,128)}, bf16[4,256,640]{2,1,0:T(8,128)(2,1)}, bf16[4,256,512]{2,1,0:T(8,128)(2,1)}, bf16[4,256,1408]{2,1,0:T(8,128)(2,...) custom-call(bf16[1024,2048]{1,0:T(8,128)(2,1)} %get-tuple-element.48.xn_in, ...), custom_call_target="tpu_custom_call" | custom-call | flops 20401094656 | bytes 67108864 | tf_op jit(solution)/shard_map/backward_stage/pallas_call | solution.py:258
  504.6 0.0 copy-done
  504.6 0.8 broadcast_in_dim.11.g1
  505.4 16.7 %finish_stage.1 = (f32[256,2048]{1,0:T(8,128)}, f32[256,256]{1,0:T(8,128)}, f32[256,256]{1,0:T(8,128)}, f32[256,2048]{1,0:T(8,128)}, f32[256,5632]{1,0:T(8,128)}...) custom-call(bf16[4,256,640]{2,1,0:T(8,128)(2,1)} %get-tuple-element., ...), custom_call_target="tpu_custom_call" | custom-call | tf_op jit(solution)/shard_map/finish_stage/pallas_call | solution.py:1298
  522.0 1.7 slice_reduce_fusion
  (2 shorter events, 0.0 us)
Async XLA Ops:
  274.2 230.4 %copy-start = (bf16[256]{0:T(256)(128)(2,1)S(1)}, bf16[256]{0:T(256)(128)(2,1)}, u32[]{:S(2)}) copy-start(bf16[256]{0:T(256)(128)(2,1)} %param.14) | copy-start | bytes 1540

commit v6 on v5

--- a/solution.py
+++ b/solution.py
@@ -269,6 +269,20 @@
     )(*ins)
 
 
+def tiles_of(total, most):
+    sizes, at = [], 0
+    while at < total:
+        sizes.append((at, min(most, total - at)))
+        at += most
+    return sizes
+
+
+def add_to(ref, other):
+    for start, size in tiles_of(ref.shape[0], 96):
+        at = pl.ds(start, size)
+        ref[at, :] = (ref[at, :].astype(f32) + other[at, :].astype(f32)).astype(bf16)
+
+
 class PlaneScatter:
     SEMS = 8
 
@@ -303,7 +317,7 @@
         remote(ref, ref, self.sems.at[0], sem, self.p.x).wait_recv()
 
     def add(self, ref, other):
-        ref[...] = (ref[...].astype(f32) + other[...].astype(f32)).astype(bf16)
+        add_to(ref, other)
 
     def middle(self):
         p = self.p
@@ -355,7 +369,7 @@
         remote(ref, ref, self.sems.at[0], sem, self.p.sibling).wait_recv()
 
     def add(self, ref, other):
-        ref[...] = (ref[...].astype(f32) + other[...].astype(f32)).astype(bf16)
+        add_to(ref, other)
 
     def combine(self):
         if self.stage is not None:
@@ -717,19 +731,11 @@
     return call(forward_kernel, ins, outs, scratch, 1, flops, "forward_stage")
 
 
-def tiles_of(total, most):
-    sizes, at = [], 0
-    while at < total:
-        sizes.append((at, min(most, total - at)))
-        at += most
-    return sizes
-
-
 def middle_kernel(
     m_in, cot_in, wgate_in, wup_in, w_down,
-    y_out, down_part, gate_part, up_part, gm_out,
-    M, COT, WG, WU, WD, GATE, UP, HID, R2, PD, PH, D1, D2, H1, H2, GM, Y, STAGE_D, STAGE,
-    line_sems, plane_sems, copy_sems, stage_sems,
+    y_out, down_part, down_sum, gate_part, up_part, gm_out,
+    M, COT, WG, WU, WD, GATE, UP, HID, R2, PD, PH, D1, D2, H1, H2, DACC, DSLOT,
+    line_sems, sum_sems, plane_sems, copy_sems, stage_sems,
 ):
     p = Place()
     n_ctx = 4
@@ -758,30 +764,40 @@
         at = rows_at(b, rows)
         mf = M[at, :].astype(f32)
         r = lax.rsqrt(jnp.mean(mf * mf, axis=-1, keepdims=True) + eps_norm)
-        gate = dot(M[at, :], WG[...]) * r
-        up = dot(M[at, :], WU[...]) * r
         R2[at, :] = jnp.broadcast_to(r, (rows, 128))
-        GATE[at, :] = gate.astype(bf16)
-        UP[at, :] = up.astype(bf16)
-        HID[at, :] = (gate * (1.0 / (1.0 + jnp.exp(-gate))) * up).astype(bf16)
+        for start, size in tiles_of(units, 512):
+            cols = slice(start, start + size)
+            gate = dot(M[at, :], WG[:, cols]) * r
+            up = dot(M[at, :], WU[:, cols]) * r
+            GATE[at, cols] = gate.astype(bf16)
+            UP[at, cols] = up.astype(bf16)
+            HID[at, cols] = (gate * (1.0 / (1.0 + jnp.exp(-gate))) * up).astype(bf16)
 
     down_line.hop(1)
     loads[3].wait()
     stage_copies = {}
-    for i, (at, size) in enumerate(tiles_of(units, STAGE_D.shape[1])):
-        slot = i % 2
+    for i, (at, size) in enumerate(tiles_of(units, rows)):
+        slot = pl.ds(i % 2 * rows, size)
         if i >= 2:
             stage_copies[i - 2].wait()
-        STAGE_D[slot, 0:size, :] = dot_tn(HID[:, at : at + size], COT[...]).astype(bf16)
-        copy = pltpu.make_async_copy(
-            STAGE_D.at[slot, pl.ds(0, size)], down_part.at[pl.ds(at, size)], stage_sems.at[slot]
-        )
+        for j in range(0, width, cw):
+            PH[slot, j : j + cw] = dot_tn(HID[:, at : at + size], COT[:, j : j + cw]).astype(bf16)
+        copy = pltpu.make_async_copy(PH.at[slot], down_part.at[pl.ds(at, size)], stage_sems.at[i % 2])
         copy.start()
         stage_copies[i] = copy
     n_down = len(stage_copies)
-    down_line.hop(2)
     stage_copies[n_down - 2].wait()
     stage_copies[n_down - 1].wait()
+
+    def down_block(level, core):
+        return down_part.at[pl.ds(pl.multiple_of((2 * level + core) * unit, 16), unit)]
+
+    down_stage = [PD.at[pl.ds(i * rows, unit)] for i in range(2)]
+    sum_line = LineScatter(p, down_block, DACC, DSLOT, sum_sems.at[0], down_stage)
+    sum_line.start()
+    down_line.hop(2)
+    sum_line.combine()
+    sum_line.step(1)
     down_line.hop(3)
     down_line.finish()
 
@@ -808,7 +824,8 @@
 
     def partial_out(c):
         at = rows_at(c, rows)
-        PD[at, :] = dot(HID[at, :], WD[...]).astype(bf16)
+        for j in range(0, width, cw):
+            PD[at, j : j + cw] = dot(HID[at, :], WD[:, j : j + cw]).astype(bf16)
 
     partial_out(p.cd)
     y_plane.start()
@@ -816,19 +833,23 @@
     partial_out(p.cy)
     y_plane.middle()
     partial_out(p.c)
+    sum_line.step(2)
 
     def back(b):
         at = pl.ds(b * rows, rows)
         r = R2[at, 0:1]
-        grad_hidden = dot_nt(COT[at, :], WD[...])
-        gate = GATE[at, :].astype(f32)
-        up = UP[at, :].astype(f32)
-        sig = 1.0 / (1.0 + jnp.exp(-gate))
-        d_up = grad_hidden * gate * sig
-        d_gate = grad_hidden * up * sig * (1.0 + gate * (1.0 - sig))
-        stat = jnp.sum(d_gate * gate + d_up * up, axis=-1, keepdims=True)
-        GATE[at, :] = (d_gate * r).astype(bf16)
-        UP[at, :] = (d_up * r).astype(bf16)
+        stat = jnp.zeros((rows, 1), f32)
+        for start, size in tiles_of(units, 512):
+            cols = slice(start, start + size)
+            grad_hidden = dot_nt(COT[at, :], WD[cols, :])
+            gate = GATE[at, cols].astype(f32)
+            up = UP[at, cols].astype(f32)
+            sig = 1.0 / (1.0 + jnp.exp(-gate))
+            d_up = grad_hidden * gate * sig
+            d_gate = grad_hidden * up * sig * (1.0 + gate * (1.0 - sig))
+            stat += jnp.sum(d_gate * gate + d_up * up, axis=-1, keepdims=True)
+            GATE[at, cols] = (d_gate * r).astype(bf16)
+            UP[at, cols] = (d_up * r).astype(bf16)
         coef = r * r * stat * (1.0 / width)
         for j in range(0, width, cw):
             e = dot_nt(GATE[at, :], WG[j : j + cw, :]) + dot_nt(UP[at, :], WU[j : j + cw, :])
@@ -838,6 +859,7 @@
     back(0)
     back(1)
     h_plane[0].middle()
+    sum_line.step(3)
     back(2)
     h_plane[1].middle()
     back(3)
@@ -846,26 +868,32 @@
     stage_copies = {}
     jobs = []
     for src, dst in ((GATE, gate_part), (UP, up_part)):
-        for at, size in tiles_of(width, STAGE.shape[1]):
+        for at, size in tiles_of(width, 512):
             jobs.append((src, dst, at, size))
 
     def weight_tile(i):
         src, dst, at, size = jobs[i]
-        slot = i % 2
+        slot = pl.ds(i % 2 * size, size)
         if i >= 2:
             stage_copies[i - 2].wait()
-        STAGE[slot] = dot_tn(M[:, at : at + size], src[...]).astype(bf16)
-        copy = pltpu.make_async_copy(STAGE.at[slot], dst.at[pl.ds(at, size)], stage_sems.at[2 + slot])
+        for start, part in tiles_of(units, 512):
+            cols = slice(start, start + part)
+            HID[slot, cols] = dot_tn(M[:, at : at + size], src[:, cols]).astype(bf16)
+        copy = pltpu.make_async_copy(HID.at[slot], dst.at[pl.ds(at, size)], stage_sems.at[2 + i % 2])
         copy.start()
         stage_copies[i] = copy
 
     def finish_block(b):
         at = pl.ds(b * rows, rows)
-        GM[at, :] = (COT[at, rows_at(p.c, cw)].astype(f32) + h_plane[b].finish()).astype(bf16)
+        mine = rows_at(p.c, cw)
+        COT[at, mine] = (COT[at, mine].astype(f32) + h_plane[b].finish()).astype(bf16)
 
     weight_tile(0)
     weight_tile(1)
     h_plane[3].middle()
+    sum_line.step(4)
+    sum_copy = pltpu.make_async_copy(sum_line.result(), down_sum, copy_sems.at[6])
+    sum_copy.start()
     weight_tile(2)
     finish_block(0)
     weight_tile(3)
@@ -875,16 +903,22 @@
     finish_block(2)
     weight_tile(6)
     weight_tile(7)
-    Y[...] = (M[rows_at(p.c, rows), :].astype(f32) + y_plane.finish()).astype(bf16)
-    y_copy = pltpu.make_async_copy(Y, y_out, copy_sems.at[4])
+    piece = rows // n_ctx
+    for i in range(n_ctx):
+        own = pl.ds(pl.multiple_of(p.c * rows + i * piece, piece), piece)
+        mlp = y_plane.finish(pl.ds(i * piece, piece), i == 0)
+        PD[own, :] = (M[own, :].astype(f32) + mlp).astype(bf16)
+    y_copy = pltpu.make_async_copy(PD.at[rows_at(p.c, rows)], y_out, copy_sems.at[4])
     y_copy.start()
     finish_block(3)
-    gm_copy = pltpu.make_async_copy(GM, gm_out, copy_sems.at[5])
+    gm_copy = pltpu.make_async_copy(COT.at[:, rows_at(p.c, cw)], gm_out, copy_sems.at[5])
     gm_copy.start()
     stage_copies[6].wait()
     stage_copies[7].wait()
     y_copy.wait()
     gm_copy.wait()
+    sum_copy.wait()
+    sum_line.drain()
     down_line.drain()
     y_plane.drain()
     for b in range(n_ctx):
@@ -897,9 +931,10 @@
     rows = seq // n_ctx
     cw = width // n_ctx
     units = wgate.shape[1]
+    unit = units // n_fsdp
     outs = [
-        ((rows, width), bf16), ((units, width), bf16), ((width, units), bf16), ((width, units), bf16),
-        ((seq, cw), bf16),
+        ((rows, width), bf16), ((units, width), bf16), ((unit, width), bf16), ((width, units), bf16),
+        ((width, units), bf16), ((seq, cw), bf16),
     ]
     scratch = [
         pltpu.VMEM((seq, width), bf16),
@@ -917,13 +952,12 @@
         pltpu.VMEM((2, rows, width), bf16),
         pltpu.VMEM((n_ctx, 2, rows // 2, cw), bf16),
         pltpu.VMEM((n_ctx, 2, rows, cw), bf16),
-        pltpu.VMEM((seq, cw), bf16),
-        pltpu.VMEM((rows, width), bf16),
-        pltpu.VMEM((2, 256, width), bf16),
-        pltpu.VMEM((2, 512, units), bf16),
+        pltpu.VMEM((n_fsdp // 2, unit, width), bf16),
+        pltpu.VMEM((5, unit, width), bf16),
         pltpu.SemaphoreType.DMA((1, LineGather.SEMS)),
+        pltpu.SemaphoreType.DMA((1, LineScatter.SEMS)),
         pltpu.SemaphoreType.DMA((5, PlaneScatter.SEMS)),
-        pltpu.SemaphoreType.DMA((6,)),
+        pltpu.SemaphoreType.DMA((7,)),
         pltpu.SemaphoreType.DMA((4,)),
     ]
     flops = 18 * seq * width * units
@@ -932,11 +966,11 @@
 
 def backward_kernel(
     xn_in, r_in, grow_in, qt_in, kt_in, vt_in, lse_in, o_in, gm_in, wqkv_in, wout_in, tab_in,
-    gate_part, up_part, down_part,
+    gate_part, up_part, down_sum,
     tok_out, qkv_all, out_all, gate_all, up_all, down_all,
     XN, R1, GROW, QT, KT, VT, LSE, O, GM, WQ, WO, TAB,
     K, V, DK, DV, DOT, DQT, DPRE, STAT, BIAS, PT, G1, G2, T1, T2, TOK,
-    DACC, DSLOT, GACC, GSLOT, UACC, USLOT, OACC, OSLOT, QACC, QSLOT,
+    GACC, GSLOT, UACC, USLOT, OACC, OSLOT, QACC, QSLOT,
     line_sems, plane_sems, scatter_sems, copy_sems,
 ):
     p = Place()
@@ -967,10 +1001,8 @@
         count = ref.shape[0] // (2 * p.depth)
         return lambda level, core: ref.at[pl.ds(pl.multiple_of((2 * level + core) * count, 16), count)]
 
-    unit, nu = DACC.shape[1], GACC.shape[2]
-    rows_stage = [XN.at[pl.ds(i * unit, unit)] for i in range(2)]
+    nu = GACC.shape[2]
     cols_stage = [XN.at[pl.ds(i * own_rows, own_rows), pl.ds(0, nu)] for i in range(2)]
-    down_line = LineScatter(p, block_rows(down_part), DACC, DSLOT, line_sems.at[0], rows_stage)
     gate_line = LineScatter(p, block_rows(gate_part), GACC, GSLOT, line_sems.at[1], cols_stage)
     up_line = LineScatter(p, block_rows(up_part), UACC, USLOT, line_sems.at[2], cols_stage)
     out_line = LineScatter(p, block_rows(WO), OACC, OSLOT, line_sems.at[3])
@@ -981,7 +1013,6 @@
         return O.at[at, pl.ds(pl.multiple_of((f // p.depth) * nq, 128), nq)]
 
     qkv_line = LineScatter(p, qkv_block, QACC, QSLOT, line_sems.at[4])
-    down_line.start()
     gate_line.start()
     up_line.start()
 
@@ -1005,21 +1036,21 @@
         scatter_sems.at[n_ctx],
     )
 
-    def whole(ref, line, index, first):
-        count = line.acc.shape[1]
+    def whole(ref, own, index, first):
+        count = own.shape[0]
 
         def halves(c, h):
             return ref(c).at[pl.ds(h * first, count - first if h else first)]
 
-        plane = PlaneGather(p, ref, halves, plane_sems.at[index], own=line.result())
-        own = pltpu.make_async_copy(line.result(), ref(p.c), plane_sems.at[index, PlaneGather.SEMS])
-        return plane, own
-
-    down_plane, down_own = whole(lambda c: down_all.at[c], down_line, 0, 96)
-    gate_plane, gate_own = whole(lambda c: gate_all.at[c], gate_line, 1, half)
-    up_plane, up_own = whole(lambda c: up_all.at[c], up_line, 2, half)
-    out_plane, out_own = whole(lambda c: out_all.at[c], out_line, 3, half)
-    qkv_plane, qkv_own = whole(lambda c: qkv_all.at[c], qkv_line, 4, half)
+        plane = PlaneGather(p, ref, halves, plane_sems.at[index], own=own)
+        return plane, pltpu.make_async_copy(own, ref(p.c), plane_sems.at[index, PlaneGather.SEMS])
+
+    unit = down_sum.shape[0]
+    down_plane, down_own = whole(lambda c: down_all.at[c], down_sum, 0, unit // 32 * 16 + unit // 16 % 2 * 16)
+    gate_plane, gate_own = whole(lambda c: gate_all.at[c], gate_line.result(), 1, own_rows // 2)
+    up_plane, up_own = whole(lambda c: up_all.at[c], up_line.result(), 2, own_rows // 2)
+    out_plane, out_own = whole(lambda c: out_all.at[c], out_line.result(), 3, own_rows // 2)
+    qkv_plane, qkv_own = whole(lambda c: qkv_all.at[c], qkv_line.result(), 4, own_rows // 2)
 
     loads[0].wait()
     loads[1].wait()
@@ -1028,8 +1059,8 @@
         for j in range(0, width, 512):
             PT[at, j : j + 512] = dot_nt(GM[at, :], WO[j : j + 512, :]).astype(bf16)
         g_plane[b].start()
-    down_line.combine()
-    down_line.step(1)
+    gate_line.combine()
+    gate_line.step(1)
     g_plane[0].middle()
     loads[2].wait()
 
@@ -1040,9 +1071,9 @@
 
     out_line.start()
     g_plane[1].middle()
-    gate_line.combine()
+    up_line.combine()
     loads[8].start()
-    gate_line.step(1)
+    up_line.step(1)
     g_plane[2].middle()
     for i in (3, 4, 5, 6, 7, 10):
         loads[i].wait()
@@ -1091,13 +1122,13 @@
         R1[at, 0:8] = STAT[...].T
 
     attend_back(0)
-    down_line.step(2)
+    gate_line.step(2)
     attend_back(1)
-    gate_line.step(2)
     attend_back(2)
-    down_line.step(3)
+    down_plane.start()
+    down_own.start()
+    up_line.step(2)
     attend_back(3)
-    gate_line.step(3)
     loads[8].wait()
     loads[9].wait()
     loads[11].wait()
@@ -1142,16 +1173,17 @@
             O[rows_at(i, own_rows), j * nq : (j + 1) * nq] = dot_tn(XN[:, at], DPRE[...]).astype(bf16)
 
     qkv_line.start()
-    down_line.step(4)
-    down_plane.start()
-    down_own.start()
-    up_line.combine()
-    up_line.step(1)
+    gate_line.step(3)
+    down_plane.middle()
     out_line.combine()
     out_line.step(1)
+    up_line.step(3)
+    qkv_line.combine()
+    qkv_line.step(1)
     gate_line.step(4)
     gate_plane.start()
     gate_own.start()
+    out_line.step(2)
     tok_copies = []
     for i in range(n_ctx):
         if i >= 2:
@@ -1160,27 +1192,21 @@
         TOK[i % 2] = t_plane.finish(at, i == 0)
         tok_copies.append(pltpu.make_async_copy(TOK.at[i % 2], tok_out.at[at], copy_sems.at[12 + i % 2]))
         tok_copies[-1].start()
-    down_plane.middle()
-    up_line.step(2)
-    out_line.step(2)
-    gate_plane.middle()
-    qkv_line.combine()
-    qkv_line.step(1)
-    up_line.step(3)
-    out_line.step(3)
     qkv_line.step(2)
     up_line.step(4)
     up_plane.start()
     up_own.start()
+    gate_plane.middle()
+    out_line.step(3)
+    qkv_line.step(3)
     out_line.step(4)
     out_plane.start()
     out_own.start()
-    qkv_line.step(3)
     up_plane.middle()
-    out_plane.middle()
     qkv_line.step(4)
     qkv_plane.start()
     qkv_own.start()
+    out_plane.middle()
     qkv_plane.middle()
     for plane, own in (
         (down_plane, down_own), (gate_plane, gate_own), (up_plane, up_own), (out_plane, out_own), (qkv_plane, qkv_own),
@@ -1191,11 +1217,11 @@
     tok_copies[2].wait()
     tok_copies[3].wait()
     t_plane.drain()
-    for line in (down_line, gate_line, up_line, out_line, qkv_line):
+    for line in (gate_line, up_line, out_line, qkv_line):
         line.drain()
 
 
-def backward_stage(xn, r, grow, qt, kt, vt, lse, o, gm, wqkv, wout, tabs, gate_part, up_part, down_part):
+def backward_stage(xn, r, grow, qt, kt, vt, lse, o, gm, wqkv, wout, tabs, gate_part, up_part, down_sum):
     n_fsdp, n_ctx = lax.axis_size("fsdp"), lax.axis_size("ctx")
     seq, width = xn.shape
     rows = seq // n_ctx
@@ -1204,13 +1230,13 @@
     own = width // n_fsdp
     depth = n_fsdp // 2
     nq, nu = wqkv.shape[1], gate_part.shape[1]
-    unit = down_part.shape[0] // n_fsdp
+    unit = down_sum.shape[0]
     qw = qt.shape[0]
     outs = [
         ((rows, width), f32), ((n_ctx, own, nq), bf16), ((n_ctx, own, cw), bf16), ((n_ctx, own, nu), bf16),
         ((n_ctx, own, nu), bf16), ((n_ctx, unit, width), bf16),
     ]
-    ins = (xn, r, grow, qt, kt, vt, lse, o, gm, wqkv, wout, tabs, gate_part, up_part, down_part)
+    ins = (xn, r, grow, qt, kt, vt, lse, o, gm, wqkv, wout, tabs, gate_part, up_part, down_sum)
     scratch = [pltpu.VMEM(a.shape, a.dtype) for a in ins[:12]] + [
         pltpu.VMEM((seq, HEAD_DIM), bf16),
         pltpu.VMEM((seq, HEAD_DIM), bf16),
@@ -1227,8 +1253,6 @@
         pltpu.VMEM((2, half, width), bf16),
         pltpu.VMEM((2, rows, width), bf16),
         pltpu.VMEM((2, rows // n_ctx, width), f32),
-        pltpu.VMEM((depth, unit, width), bf16),
-        pltpu.VMEM((5, unit, width), bf16),
         pltpu.VMEM((depth, own, nu), bf16),
         pltpu.VMEM((5, own, nu), bf16),
         pltpu.VMEM((depth, own, nu), bf16),
@@ -1426,7 +1450,7 @@
     mid_rows = lax.dynamic_slice_in_dim(m, c * rows, rows, axis=0).astype(f32)
     output = (mid_rows + mlp).astype(bf16)
     grad_hidden = dot_nt(cot_all, wdown)
-    down_raw = dot_tn(hidden, cot_all).astype(bf16)
+    down_sum = scatter(dot_tn(hidden, cot_all), "fsdp")
     d_gate = grad_hidden * up * sig * (1.0 + gate * (1.0 - sig))
     d_up = grad_hidden * gate * sig
     stat = jnp.sum(d_gate * gate + d_up * up, axis=-1, keepdims=True)
@@ -1437,10 +1461,10 @@
     back = dot_nt(d_gate, wgate) + dot_nt(d_up, wup) - mf * (r * r * stat * (1.0 / width))
     back_own = scatter(back, "ctx", axis=1).astype(f32)
     gm = (columns(cot_all, c * cw, cw).astype(f32) + back_own).astype(bf16)
-    return output, down_raw, gate_raw, up_raw, gm
-
-
-def backward_plain(xn, r, grow, qt, kt, vt, lse, o, gm, wqkv, wout, tabs, gate_raw, up_raw, down_raw):
+    return output, None, down_sum, gate_raw, up_raw, gm
+
+
+def backward_plain(xn, r, grow, qt, kt, vt, lse, o, gm, wqkv, wout, tabs, gate_raw, up_raw, down_sum):
     n_ctx = lax.axis_size("ctx")
     c = lax.axis_index("ctx")
     seq, width = xn.shape
@@ -1456,7 +1480,6 @@
     begin = tabs[:, 64].reshape(seq).astype(jnp.int32)
     gate_grad = scatter(gate_raw, "fsdp")
     up_grad = scatter(up_raw, "fsdp")
-    down_grad = scatter(down_raw, "fsdp")
     out_grad = scatter(dot_tn(o, gm), "fsdp")
     d_att = scatter(dot_nt(gm, wout), "ctx", axis=1).reshape(seq, kv, heads // kv, HEAD_DIM)
     q = qt.T.reshape(seq, kv, heads // kv, HEAD_DIM)
@@ -1488,7 +1511,7 @@
     out_all = gather(out_grad[None], "ctx")
     gate_all = gather(gate_grad[None], "ctx")
     up_all = gather(up_grad[None], "ctx")
-    down_all = gather(down_grad[None], "ctx")
+    down_all = gather(down_sum[None], "ctx")
     return grad_tokens, qkv_all, out_all, gate_all, up_all, down_all
 
 
@@ -1565,10 +1588,10 @@
         tokens, tab, gains, gain_two, w_query, w_key, w_value, w_out, w_gate, w_up, cotangent
     )
     middle = middle_stage if kernels else middle_plain
-    y, down_raw, gate_raw, up_raw, gm = middle(m, cot_all, wgate, wup, w_down)
+    y, _, down_sum, gate_raw, up_raw, gm = middle(m, cot_all, wgate, wup, w_down)
     backward = backward_stage if kernels else backward_plain
     tok, qkv_all, out_all, gate_all, up_all, down_all = backward(
-        xn, r, grow, qt, kt, vt, lse, o, gm, wqkv, wout, tabs, gate_raw, up_raw, down_raw
+        xn, r, grow, qt, kt, vt, lse, o, gm, wqkv, wout, tabs, gate_raw, up_raw, down_sum
     )
     finish = finish_stage if kernels else finish_plain
     g_query, g_key, g_value, g_out, g_gate, g_up, g_down, tok, y, g_one, g_two = finish(

time: 529 us -> 488 us (0.922)
  Pallas kernels: 516 us -> 475 us
    pallas_call x3, Pallas kernels: 500 us -> 458 us  [call(): pl.pallas_call(kernel, out_shape=[jax.ShapeDtypeStruct(s, d) for s, d in...]
where the time goes in v6:
time: 488 us; the launch traced here: 483 us
  Pallas kernels  475 us (97%)
  local copies, waits for them, and re-layouts  5.13 us (1%)
    pallas_call x3, Pallas kernels, call(): pl.pallas_call(kernel, out_shape=[jax.ShapeDtypeStruct(s, d) for s, d in...  458 us
    pallas_call x1, Pallas kernels, finish_stage(): pl.pallas_call(functools.partial(finish_kernel, unit), grid=(steps,), out...  16.7 us

profile of v6, /device:TPU:8, one launch (start us, length us, event | category | flops | bytes accessed | tf_op | source)
XLA Modules:
  0.0 482.9 jit_solution(3758977397486994766)
XLA Ops:
  0.6 0.8 fusion
  1.4 0.2 multiply_cosine_fusion
  1.6 0.6 pad_maximum_fusion.tab
  2.3 1.4 broadcast_in_dim.10.gcol.g2
  3.7 1.3 broadcast_in_dim.9.gains
  5.0 151.3 %forward_stage.1 = (bf16[1024,2048]{1,0:T(8,128)(2,1)}, f32[1024,128]{1,0:T(8,128)}, f32[8,2048]{1,0:T(8,128)}, bf16[512,1024]{1,0:T(8,128)(2,1)}, bf16[64,1024]...) custom-call(bf16[256,2048]{1,0:T(8,128)(2,1)} %tok.1, ...), custom_call_target="tpu_custom_call" | custom-call | flops 9126805504 | bytes 67108864 | tf_op jit(solution)/shard_map/forward_stage/pallas_call | solution.py:258
  156.3 130.4 %middle_stage.1 = (bf16[256,2048]{1,0:T(8,128)(2,1)}, bf16[1408,2048]{1,0:T(8,128)(2,1)}, bf16[176,2048]{1,0:T(8,128)(2,1)}, bf16[2048,1408]{1,0:T(8,128)(2,1)},...) custom-call(bf16[1024,2048]{1,0:T(8,128)(2,1)} %get-tuple-element.56.m_in, ...), custom_call_target="tpu_custom_call" | custom-call | flops 53150220288 | bytes 67108864 | tf_op jit(solution)/shard_map/middle_stage/pallas_call | solution.py:258
  286.7 0.0 copy-start
  286.7 176.5 %backward_stage.1 = (f32[256,2048]{1,0:T(8,128)}, bf16[4,256,640]{2,1,0:T(8,128)(2,1)}, bf16[4,256,512]{2,1,0:T(8,128)(2,1)}, bf16[4,256,1408]{2,1,0:T(8,128)(2,...) custom-call(bf16[1024,2048]{1,0:T(8,128)(2,1)} %get-tuple-element.48.xn_in, ...), custom_call_target="tpu_custom_call" | custom-call | flops 20401094656 | bytes 67108864 | tf_op jit(solution)/shard_map/backward_stage/pallas_call | solution.py:258
  463.2 0.0 copy-done
  463.3 0.8 broadcast_in_dim.11.g1
  464.0 16.7 %finish_stage.1 = (f32[256,2048]{1,0:T(8,128)}, f32[256,256]{1,0:T(8,128)}, f32[256,256]{1,0:T(8,128)}, f32[256,2048]{1,0:T(8,128)}, f32[256,5632]{1,0:T(8,128)}...) custom-call(bf16[4,256,640]{2,1,0:T(8,128)(2,1)} %get-tuple-element., ...), custom_call_target="tpu_custom_call" | custom-call | tf_op jit(solution)/shard_map/finish_stage/pallas_call | solution.py:1322
  480.7 1.7 slice_reduce_fusion
  (2 shorter events, 0.0 us)
Async XLA Ops:
  286.7 176.5 %copy-start = (bf16[256]{0:T(256)(128)(2,1)S(1)}, bf16[256]{0:T(256)(128)(2,1)}, u32[]{:S(2)}) copy-start(bf16[256]{0:T(256)(128)(2,1)} %param.14) | copy-start | bytes 1540

commit v7 on v6

--- a/solution.py
+++ b/solution.py
@@ -439,9 +439,9 @@
 
 
 def forward_kernel(
-    tok, tab, gains, gcol, w_query, w_key, w_value, w_out, w_gate, w_up, cot,
+    tok, tab, gains, gcol, w_query, w_key, w_value, w_out, w_gate, w_up,
     xn_out, r_out, grow_out, qt_out, kt_out, vt_out, lse_out, o_out, m_out,
-    wqkv_out, wout_out, wgate, wup, cot_all, tab_out,
+    wqkv_out, wout_out, wgate, wup, tab_out,
     X, XN, QT, KT, VT, K, LSE, O, M, WQ, WO, TAB, G8, GROW, BIAS, OT, R1,
     WK, WV, GF, UF, GO, UO, GCOL,
     line_sems, plane_sems, copy_sems,
@@ -481,7 +481,6 @@
         )
 
     tok_plane = PlaneGather(p, *row_block(X), plane_sems.at[0], own=tok)
-    cot_plane = PlaneGather(p, *row_block(cot_all), plane_sems.at[1], own=cot)
     tab_rows = tab.shape[0]
     tab_plane = PlaneGather(
         p,
@@ -519,10 +518,8 @@
     qkv_line.start()
     own_tok = pltpu.make_async_copy(tok, X.at[rows_at(p.c, rows)], copy_sems.at[0])
     own_tab = pltpu.make_async_copy(tab, TAB.at[p.c], copy_sems.at[1])
-    own_cot = pltpu.make_async_copy(cot, cot_all.at[rows_at(p.c, rows)], copy_sems.at[2])
     own_tok.start()
     own_tab.start()
-    own_cot.start()
 
     for i in range(3, 6):
         loads[i].wait()
@@ -564,7 +561,6 @@
     norm(p.cy)
     qkv_line.hop(3)
     tok_plane.finish()
-    cot_plane.start()
     out_line.hop(3)
     up_line.start()
     norm(p.cd)
@@ -600,7 +596,6 @@
 
     wq_copy = pltpu.make_async_copy(WQ, wqkv_out, copy_sems.at[5])
     wq_copy.start()
-    gate_line.hop(1)
 
     def attend(b):
         n = (b + 1) * rows
@@ -635,27 +630,27 @@
     attend(1)
     o_plane[0].middle()
     attend(2)
+    gate_line.hop(1)
     o_plane[1].middle()
     attend(3)
     o_plane[2].middle()
-    cot_plane.middle()
     out_line.finish()
     o_plane[0].finish()
     middle(0)
+    o_plane[1].finish()
+    middle(1)
     o_plane[3].middle()
     up_line.hop(1)
-    o_plane[1].finish()
-    middle(1)
     m_plane[0].middle()
     o_plane[2].finish()
     middle(2)
     m_plane[1].middle()
-    gate_line.hop(2)
     o_plane[3].finish()
     middle(3)
     m_plane[2].middle()
+    gate_line.hop(2)
+    m_plane[3].middle()
     up_line.hop(2)
-    m_plane[3].middle()
     copies = [xn_copy, r_copy, grow_copy, wq_copy]
     for i, (src, dst) in enumerate(
         ((QT, qt_out), (KT, kt_out), (VT, vt_out), (LSE, lse_out), (O, o_out), (WO, wout_out), (TAB, tab_out))
@@ -670,19 +665,17 @@
     copies.append(m_copy)
     gate_line.hop(3)
     up_line.hop(3)
-    cot_plane.finish()
     gate_line.finish()
     up_line.finish()
-    own_cot.wait()
     for copy in copies:
         copy.wait()
     for line in (gain_line, qkv_line, out_line, gate_line, up_line):
         line.drain()
-    for plane in [tok_plane, cot_plane, tab_plane] + o_plane + m_plane:
+    for plane in [tok_plane, tab_plane] + o_plane + m_plane:
         plane.drain()
 
 
-def forward_stage(tok, tab, gains, gcol, w_query, w_key, w_value, w_out, w_gate, w_up, cot):
+def forward_stage(tok, tab, gains, gcol, w_query, w_key, w_value, w_out, w_gate, w_up):
     n_fsdp, n_ctx = lax.axis_size("fsdp"), lax.axis_size("ctx")
     rows, width = tok.shape
     seq = rows * n_ctx
@@ -695,7 +688,7 @@
     outs = [
         ((seq, width), bf16), ((seq, 128), f32), ((8, width), f32), ((qw, seq), bf16), ((64, seq), bf16),
         ((64, seq), bf16), ((8 * heads, seq), f32), ((seq, width), bf16), ((seq, width), bf16), ((whole, nq), bf16),
-        ((whole, nw), bf16), ((whole, nu), bf16), ((whole, nu), bf16), ((seq, width), bf16), (tab_shape, f32),
+        ((whole, nw), bf16), ((whole, nu), bf16), ((whole, nu), bf16), (tab_shape, f32),
     ]
     scratch = [
         pltpu.VMEM((seq, width), bf16),
@@ -726,13 +719,13 @@
         pltpu.SemaphoreType.DMA((11, PlaneGather.SEMS)),
         pltpu.SemaphoreType.DMA((21,)),
     ]
-    ins = (tok, tab, gains, gcol, w_query, w_key, w_value, w_out, w_gate, w_up, cot)
+    ins = (tok, tab, gains, gcol, w_query, w_key, w_value, w_out, w_gate, w_up)
     flops = 2 * seq * width * (nq + nw) + 8 * heads * seq * seq * HEAD_DIM
     return call(forward_kernel, ins, outs, scratch, 1, flops, "forward_stage")
 
 
 def middle_kernel(
-    m_in, cot_in, wgate_in, wup_in, w_down,
+    m_in, cot, wgate_in, wup_in, w_down,
     y_out, down_part, down_sum, gate_part, up_part, gm_out,
     M, COT, WG, WU, WD, GATE, UP, HID, R2, PD, PH, D1, D2, H1, H2, DACC, DSLOT,
     line_sems, sum_sems, plane_sems, copy_sems, stage_sems,
@@ -745,7 +738,7 @@
     cw = width // n_ctx
     units = GATE.shape[1]
     loads = []
-    for i, (src, dst) in enumerate(((m_in, M), (wgate_in, WG), (wup_in, WU), (cot_in, COT))):
+    for i, (src, dst) in enumerate(((m_in, M), (wgate_in, WG), (wup_in, WU), (cot, COT.at[rows_at(p.c, rows)]))):
         loads.append(pltpu.make_async_copy(src, dst, copy_sems.at[i]))
         loads[-1].start()
 
@@ -754,13 +747,20 @@
     down_own = w_down.at[pl.ds(pl.multiple_of(p.c * unit, 16), unit)]
     down_line = LineGather(p, down_own, WD, line_sems.at[0])
     down_line.start()
+    cot_plane = PlaneGather(
+        p,
+        lambda c: COT.at[rows_at(c, rows)],
+        lambda c, h: COT.at[pl.ds(pl.multiple_of(c * rows + h * half, half), half)],
+        plane_sems.at[5],
+        own=cot,
+    )
+    cot_plane.start()
 
     loads[0].wait()
     loads[1].wait()
     loads[2].wait()
 
-    @pl.loop(0, n_ctx)
-    def _(b):
+    def activate(b):
         at = rows_at(b, rows)
         mf = M[at, :].astype(f32)
         r = lax.rsqrt(jnp.mean(mf * mf, axis=-1, keepdims=True) + eps_norm)
@@ -773,8 +773,13 @@
             UP[at, cols] = up.astype(bf16)
             HID[at, cols] = (gate * (1.0 / (1.0 + jnp.exp(-gate))) * up).astype(bf16)
 
+    pl.loop(0, 2)(activate)
     down_line.hop(1)
+    pl.loop(2, 4)(activate)
+    cot_plane.middle()
+    down_line.hop(2)
     loads[3].wait()
+    cot_plane.finish()
     stage_copies = {}
     for i, (at, size) in enumerate(tiles_of(units, rows)):
         slot = pl.ds(i % 2 * rows, size)
@@ -792,12 +797,9 @@
     def down_block(level, core):
         return down_part.at[pl.ds(pl.multiple_of((2 * level + core) * unit, 16), unit)]
 
-    down_stage = [PD.at[pl.ds(i * rows, unit)] for i in range(2)]
+    down_stage = [PH.at[pl.ds(i * rows, unit)] for i in range(2)]
     sum_line = LineScatter(p, down_block, DACC, DSLOT, sum_sems.at[0], down_stage)
     sum_line.start()
-    down_line.hop(2)
-    sum_line.combine()
-    sum_line.step(1)
     down_line.hop(3)
     down_line.finish()
 
@@ -831,9 +833,9 @@
     y_plane.start()
     partial_out(p.cx)
     partial_out(p.cy)
-    y_plane.middle()
+    sum_line.combine()
+    sum_line.step(1)
     partial_out(p.c)
-    sum_line.step(2)
 
     def back(b):
         at = pl.ds(b * rows, rows)
@@ -857,9 +859,10 @@
         h_plane[b].start()
 
     back(0)
+    y_plane.middle()
     back(1)
     h_plane[0].middle()
-    sum_line.step(3)
+    sum_line.step(2)
     back(2)
     h_plane[1].middle()
     back(3)
@@ -889,20 +892,22 @@
         COT[at, mine] = (COT[at, mine].astype(f32) + h_plane[b].finish()).astype(bf16)
 
     weight_tile(0)
+    cot_plane.drain()
+    sum_line.step(3)
+    h_plane[3].middle()
     weight_tile(1)
-    h_plane[3].middle()
+    weight_tile(2)
+    finish_block(0)
+    weight_tile(3)
+    weight_tile(4)
+    finish_block(1)
+    weight_tile(5)
+    weight_tile(6)
+    finish_block(2)
+    weight_tile(7)
     sum_line.step(4)
     sum_copy = pltpu.make_async_copy(sum_line.result(), down_sum, copy_sems.at[6])
     sum_copy.start()
-    weight_tile(2)
-    finish_block(0)
-    weight_tile(3)
-    finish_block(1)
-    weight_tile(4)
-    weight_tile(5)
-    finish_block(2)
-    weight_tile(6)
-    weight_tile(7)
     piece = rows // n_ctx
     for i in range(n_ctx):
         own = pl.ds(pl.multiple_of(p.c * rows + i * piece, piece), piece)
@@ -925,7 +930,7 @@
         h_plane[b].drain()
 
 
-def middle_stage(m, cot_all, wgate, wup, w_down):
+def middle_stage(m, cot, wgate, wup, w_down):
     n_fsdp, n_ctx = lax.axis_size("fsdp"), lax.axis_size("ctx")
     seq, width = m.shape
     rows = seq // n_ctx
@@ -956,12 +961,12 @@
         pltpu.VMEM((5, unit, width), bf16),
         pltpu.SemaphoreType.DMA((1, LineGather.SEMS)),
         pltpu.SemaphoreType.DMA((1, LineScatter.SEMS)),
-        pltpu.SemaphoreType.DMA((5, PlaneScatter.SEMS)),
+        pltpu.SemaphoreType.DMA((6, PlaneScatter.SEMS)),
         pltpu.SemaphoreType.DMA((7,)),
         pltpu.SemaphoreType.DMA((4,)),
     ]
     flops = 18 * seq * width * units
-    return call(middle_kernel, (m, cot_all, wgate, wup, w_down), outs, scratch, 2, flops, "middle_stage")
+    return call(middle_kernel, (m, cot, wgate, wup, w_down), outs, scratch, 2, flops, "middle_stage")
 
 
 def backward_kernel(
@@ -992,8 +997,8 @@
         )
     ):
         loads.append(pltpu.make_async_copy(src, dst, copy_sems.at[i]))
-        if dst is not XN:
-            loads[-1].start()
+    loads[0].start()
+    loads[1].start()
 
     p.barrier()
 
@@ -1015,6 +1020,8 @@
     qkv_line = LineScatter(p, qkv_block, QACC, QSLOT, line_sems.at[4])
     gate_line.start()
     up_line.start()
+    for i in (2, 3, 4, 5, 6, 7, 9, 10, 11):
+        loads[i].start()
 
     def col_scatter(b):
         return PlaneScatter(
@@ -1361,7 +1368,7 @@
     return (index[None, :] <= index[:, None]) & (index[None, :] >= begin[:, None])
 
 
-def forward_plain(tok, tab, gains, gcol, w_query, w_key, w_value, w_out, w_gate, w_up, cot):
+def forward_plain(tok, tab, gains, gcol, w_query, w_key, w_value, w_out, w_gate, w_up):
     n_ctx, n_fsdp = lax.axis_size("ctx"), lax.axis_size("fsdp")
     c = lax.axis_index("ctx")
     own_rows = w_query.shape[0]
@@ -1392,7 +1399,6 @@
     wout = gather(wout_o, "fsdp")
     wgate = gather(wgate_o, "fsdp")
     wup = gather(wup_o, "fsdp")
-    cot_all = gather(cot, "ctx")
     gain = gather(gains[0:1], "fsdp", axis=1).astype(f32)
     xf = x.astype(f32)
     r = lax.rsqrt(jnp.mean(xf * xf, axis=-1, keepdims=True) + eps_norm)
@@ -1428,10 +1434,10 @@
     vt = v.reshape(seq, kvw).T
     r = jnp.broadcast_to(r, (seq, 128))
     grow = jnp.broadcast_to(gain, (8, width))
-    return xn, r, grow, qt, kt, vt, lse, o, m, wqkv, wout, wgate, wup, cot_all, tabs
-
-
-def middle_plain(m, cot_all, wgate, wup, w_down):
+    return xn, r, grow, qt, kt, vt, lse, o, m, wqkv, wout, wgate, wup, tabs
+
+
+def middle_plain(m, cot, wgate, wup, w_down):
     n_ctx = lax.axis_size("ctx")
     c = lax.axis_index("ctx")
     unit = w_down.shape[0] // n_ctx
@@ -1440,6 +1446,7 @@
     rows = seq // n_ctx
     cw = width // n_ctx
     wdown = gather(wdown_o, "fsdp")
+    cot_all = gather(cot, "ctx")
     mf = m.astype(f32)
     r = lax.rsqrt(jnp.mean(mf * mf, axis=-1, keepdims=True) + eps_norm)
     gate = dot(m, wgate) * r
@@ -1584,11 +1591,11 @@
     )
 
     forward = forward_stage if kernels else forward_plain
-    xn, r, grow, qt, kt, vt, lse, o, m, wqkv, wout, wgate, wup, cot_all, tabs = forward(
-        tokens, tab, gains, gain_two, w_query, w_key, w_value, w_out, w_gate, w_up, cotangent
+    xn, r, grow, qt, kt, vt, lse, o, m, wqkv, wout, wgate, wup, tabs = forward(
+        tokens, tab, gains, gain_two, w_query, w_key, w_value, w_out, w_gate, w_up
     )
     middle = middle_stage if kernels else middle_plain
-    y, _, down_sum, gate_raw, up_raw, gm = middle(m, cot_all, wgate, wup, w_down)
+    y, _, down_sum, gate_raw, up_raw, gm = middle(m, cotangent, wgate, wup, w_down)
     backward = backward_stage if kernels else backward_plain
     tok, qkv_all, out_all, gate_all, up_all, down_all = backward(
         xn, r, grow, qt, kt, vt, lse, o, gm, wqkv, wout, tabs, gate_raw, up_raw, down_sum

time: 488 us -> 474 us (0.971)
  Pallas kernels: 475 us -> 459 us
    pallas_call x3, Pallas kernels: 458 us -> 442 us  [call(): pl.pallas_call(kernel, out_shape=[jax.ShapeDtypeStruct(s, d) for s, d in...]
where the time goes in v7:
time: 474 us; the launch traced here: 467 us
  Pallas kernels  459 us (97%)
  local copies, waits for them, and re-layouts  5.13 us (1%)
    pallas_call x3, Pallas kernels, call(): pl.pallas_call(kernel, out_shape=[jax.ShapeDtypeStruct(s, d) for s, d in...  442 us
    pallas_call x1, Pallas kernels, finish_stage(): pl.pallas_call(functools.partial(finish_kernel, unit), grid=(steps,), out...  16.7 us

profile of v7, /device:TPU:8, one launch (start us, length us, event | category | flops | bytes accessed | tf_op | source)
XLA Modules:
  0.0 466.9 jit_solution(6374773154954733444)
XLA Ops:
  0.6 0.8 fusion
  1.4 0.2 multiply_cosine_fusion
  1.6 0.6 pad_maximum_fusion.tab
  2.3 1.4 broadcast_in_dim.10.gcol.g2
  3.7 1.3 broadcast_in_dim.9.gains
  5.0 136.4 %forward_stage.1 = (bf16[1024,2048]{1,0:T(8,128)(2,1)}, f32[1024,128]{1,0:T(8,128)}, f32[8,2048]{1,0:T(8,128)}, bf16[512,1024]{1,0:T(8,128)(2,1)}, bf16[64,1024]...) custom-call(bf16[256,2048]{1,0:T(8,128)(2,1)} %tok.1, ...), custom_call_target="tpu_custom_call" | custom-call | flops 9126805504 | bytes 67108864 | tf_op jit(solution)/shard_map/forward_stage/pallas_call | solution.py:258
  141.4 130.5 %middle_stage.1 = (bf16[256,2048]{1,0:T(8,128)(2,1)}, bf16[1408,2048]{1,0:T(8,128)(2,1)}, bf16[176,2048]{1,0:T(8,128)(2,1)}, bf16[2048,1408]{1,0:T(8,128)(2,1)},...) custom-call(bf16[1024,2048]{1,0:T(8,128)(2,1)} %get-tuple-element.55.m_in, bf16[256,2048]{1,0:T(8,128)(2,1)} %cot.1, ...), custom_call_target="tpu_custom_call" | custom-call | flops 53150220288 | bytes 67108864 | tf_op jit(solution)/shard_map/middle_stage/pallas_call | solution.py:258
  271.8 0.0 copy-start
  271.8 175.4 %backward_stage.1 = (f32[256,2048]{1,0:T(8,128)}, bf16[4,256,640]{2,1,0:T(8,128)(2,1)}, bf16[4,256,512]{2,1,0:T(8,128)(2,1)}, bf16[4,256,1408]{2,1,0:T(8,128)(2,...) custom-call(bf16[1024,2048]{1,0:T(8,128)(2,1)} %get-tuple-element.47.xn_in, ...), custom_call_target="tpu_custom_call" | custom-call | flops 20401094656 | bytes 67108864 | tf_op jit(solution)/shard_map/backward_stage/pallas_call | solution.py:258
  447.3 0.0 copy-done
  447.3 0.8 broadcast_in_dim.11.g1
  448.0 16.7 %finish_stage.1 = (f32[256,2048]{1,0:T(8,128)}, f32[256,256]{1,0:T(8,128)}, f32[256,256]{1,0:T(8,128)}, f32[256,2048]{1,0:T(8,128)}, f32[256,5632]{1,0:T(8,128)}...) custom-call(bf16[4,256,640]{2,1,0:T(8,128)(2,1)} %get-tuple-element., ...), custom_call_target="tpu_custom_call" | custom-call | tf_op jit(solution)/shard_map/finish_stage/pallas_call | solution.py:1329
  464.7 1.7 slice_reduce_fusion
  (2 shorter events, 0.0 us)
Async XLA Ops:
  271.8 175.4 %copy-start = (bf16[256]{0:T(256)(128)(2,1)S(1)}, bf16[256]{0:T(256)(128)(2,1)}, u32[]{:S(2)}) copy-start(bf16[256]{0:T(256)(128)(2,1)} %param.14) | copy-start | bytes 1540

commit v8 on v7

--- a/solution.py
+++ b/solution.py
@@ -439,11 +439,11 @@
 
 
 def forward_kernel(
-    tok, tab, gains, gcol, w_query, w_key, w_value, w_out, w_gate, w_up,
-    xn_out, r_out, grow_out, qt_out, kt_out, vt_out, lse_out, o_out, m_out,
+    tok, tab, w_query, w_key, w_value, w_out, w_gate, w_up,
+    xn_out, r_out, grow_out, gcol_out, qt_out, kt_out, vt_out, lse_out, o_out, m_out,
     wqkv_out, wout_out, wgate, wup, tab_out,
     X, XN, QT, KT, VT, K, LSE, O, M, WQ, WO, TAB, G8, GROW, BIAS, OT, R1,
-    WK, WV, GF, UF, GO, UO, GCOL,
+    WK, WV, GF, UF, GO, UO, GCOL, GOWN,
     line_sems, plane_sems, copy_sems,
 ):
     p = Place()
@@ -460,7 +460,7 @@
     for i, (src, dst) in enumerate(
         (
             (w_query.at[:, rows_at(p.c, qw)], WQ.at[mine, pl.ds(0, qw)]),
-            (w_key, WK), (w_value, WV), (w_gate, GF), (w_up, UF), (gcol, GCOL),
+            (w_key, WK), (w_value, WV), (w_gate, GF), (w_up, UF), (tab, TAB.at[p.c]),
         )
     ):
         loads.append(pltpu.make_async_copy(src, dst, copy_sems.at[15 + i]))
@@ -468,7 +468,7 @@
 
     p.barrier()
 
-    gain_line = LineGather(p, gains, G8, line_sems.at[0])
+    gain_line = LineGather(p, GOWN, G8, line_sems.at[0])
     qkv_line = LineGather(p, None, WQ, line_sems.at[1])
     out_line = LineGather(p, w_out.at[:, rows_at(p.c, cw)], WO, line_sems.at[2])
     gate_line = LineGather(p, GO, wgate, line_sems.at[3])
@@ -502,10 +502,13 @@
     o_plane = [PlaneGather(p, *col_block(O, b), plane_sems.at[3 + b]) for b in range(n_ctx)]
     m_plane = [PlaneGather(p, *col_block(M, b), plane_sems.at[7 + b]) for b in range(n_ctx)]
 
-    gain_line.start()
     tab_plane.start()
     tok_plane.start()
     out_line.start()
+    loads[5].wait()
+    GOWN[...] = jnp.broadcast_to(TAB[p.c, 72:73, :], GOWN.shape).astype(bf16)
+    gain_line.start()
+    GCOL[:, 0:8] = TAB[p.c, 72:80, :].T
     for i in range(3):
         loads[i].wait()
     for c in range(n_ctx):
@@ -517,11 +520,9 @@
 
     qkv_line.start()
     own_tok = pltpu.make_async_copy(tok, X.at[rows_at(p.c, rows)], copy_sems.at[0])
-    own_tab = pltpu.make_async_copy(tab, TAB.at[p.c], copy_sems.at[1])
     own_tok.start()
-    own_tab.start()
-
-    for i in range(3, 6):
+
+    for i in range(3, 5):
         loads[i].wait()
     unit = GO.shape[1] // (2 * p.depth)
     for c in range(n_ctx):
@@ -531,7 +532,7 @@
             for f in range(2 * p.depth):
                 at = (f * n_ctx + c) * unit
                 for src, dst in ((GF, GO), (UF, UO)):
-                    part = src[:, at : at + unit].astype(f32) * GCOL[:, 0:1]
+                    part = src[:, at : at + unit].astype(f32) * GCOL[:, 4:5]
                     dst[:, f * unit : (f + 1) * unit] = part.astype(bf16)
 
     gain_line.hop(1)
@@ -541,7 +542,7 @@
     gain_line.hop(3)
     gain_line.finish()
     for f in range(2 * p.depth):
-        GROW[:, f * gains.shape[1] : (f + 1) * gains.shape[1]] = G8[16 * f : 16 * f + 8, :].astype(f32)
+        GROW[:, f * GOWN.shape[1] : (f + 1) * GOWN.shape[1]] = G8[16 * f : 16 * f + 8, :].astype(f32)
 
     def norm(c):
         at = rows_at(c, rows)
@@ -570,7 +571,6 @@
     xn_copy.start()
     r_copy.start()
     grow_copy.start()
-    own_tab.wait()
     tab_plane.finish()
     qkv_line.finish()
 
@@ -651,7 +651,9 @@
     gate_line.hop(2)
     m_plane[3].middle()
     up_line.hop(2)
-    copies = [xn_copy, r_copy, grow_copy, wq_copy]
+    gcol_copy = pltpu.make_async_copy(GCOL, gcol_out, copy_sems.at[1])
+    gcol_copy.start()
+    copies = [xn_copy, r_copy, grow_copy, gcol_copy, wq_copy]
     for i, (src, dst) in enumerate(
         ((QT, qt_out), (KT, kt_out), (VT, vt_out), (LSE, lse_out), (O, o_out), (WO, wout_out), (TAB, tab_out))
     ):
@@ -675,7 +677,7 @@
         plane.drain()
 
 
-def forward_stage(tok, tab, gains, gcol, w_query, w_key, w_value, w_out, w_gate, w_up):
+def forward_stage(tok, tab, w_query, w_key, w_value, w_out, w_gate, w_up):
     n_fsdp, n_ctx = lax.axis_size("fsdp"), lax.axis_size("ctx")
     rows, width = tok.shape
     seq = rows * n_ctx
@@ -686,7 +688,7 @@
     heads = qw // HEAD_DIM
     tab_shape = (n_ctx,) + tab.shape
     outs = [
-        ((seq, width), bf16), ((seq, 128), f32), ((8, width), f32), ((qw, seq), bf16), ((64, seq), bf16),
+        ((seq, width), bf16), ((seq, 128), f32), ((8, width), f32), ((own, 128), f32), ((qw, seq), bf16), ((64, seq), bf16),
         ((64, seq), bf16), ((8 * heads, seq), f32), ((seq, width), bf16), ((seq, width), bf16), ((whole, nq), bf16),
         ((whole, nw), bf16), ((whole, nu), bf16), ((whole, nu), bf16), (tab_shape, f32),
     ]
@@ -703,7 +705,7 @@
         pltpu.VMEM((whole, nq), bf16),
         pltpu.VMEM((whole, nw), bf16),
         pltpu.VMEM(tab_shape, f32),
-        pltpu.VMEM((16 * n_fsdp, gains.shape[1]), bf16),
+        pltpu.VMEM((16 * n_fsdp, own), bf16),
         pltpu.VMEM((8, width), f32),
         pltpu.VMEM((seq, rows), f32),
         pltpu.VMEM((qw, rows), f32),
@@ -714,12 +716,13 @@
         pltpu.VMEM(w_up.shape, bf16),
         pltpu.VMEM((own, nu), bf16),
         pltpu.VMEM((own, nu), bf16),
-        pltpu.VMEM(gcol.shape, f32),
+        pltpu.VMEM((own, 128), f32),
+        pltpu.VMEM((16, own), bf16),
         pltpu.SemaphoreType.DMA((5, LineGather.SEMS)),
         pltpu.SemaphoreType.DMA((11, PlaneGather.SEMS)),
         pltpu.SemaphoreType.DMA((21,)),
     ]
-    ins = (tok, tab, gains, gcol, w_query, w_key, w_value, w_out, w_gate, w_up)
+    ins = (tok, tab, w_query, w_key, w_value, w_out, w_gate, w_up)
     flops = 2 * seq * width * (nq + nw) + 8 * heads * seq * seq * HEAD_DIM
     return call(forward_kernel, ins, outs, scratch, 1, flops, "forward_stage")
 
@@ -837,7 +840,7 @@
     sum_line.step(1)
     partial_out(p.c)
 
-    def back(b):
+    def grads(b):
         at = pl.ds(b * rows, rows)
         r = R2[at, 0:1]
         stat = jnp.zeros((rows, 1), f32)
@@ -852,20 +855,28 @@
             stat += jnp.sum(d_gate * gate + d_up * up, axis=-1, keepdims=True)
             GATE[at, cols] = (d_gate * r).astype(bf16)
             UP[at, cols] = (d_up * r).astype(bf16)
-        coef = r * r * stat * (1.0 / width)
+        R2[at, :] = jnp.broadcast_to(r * r * stat * (1.0 / width), (rows, 128))
+
+    def push(b):
+        at = pl.ds(b * rows, rows)
+        coef = R2[at, 0:1]
         for j in range(0, width, cw):
             e = dot_nt(GATE[at, :], WG[j : j + cw, :]) + dot_nt(UP[at, :], WU[j : j + cw, :])
             PH[at, j : j + cw] = (e - M[at, j : j + cw].astype(f32) * coef).astype(bf16)
         h_plane[b].start()
 
-    back(0)
+    grads(0)
     y_plane.middle()
-    back(1)
+    push(0)
+    grads(1)
+    push(1)
     h_plane[0].middle()
+    grads(2)
     sum_line.step(2)
-    back(2)
+    push(2)
     h_plane[1].middle()
-    back(3)
+    grads(3)
+    push(3)
     h_plane[2].middle()
 
     stage_copies = {}
@@ -1278,7 +1289,7 @@
 
 
 def finish_kernel(
-    unit, qkv, out, gate, up, down, tok, y, w_query, w_key, w_value, w_gate, w_up, g1, g2,
+    unit, qkv, out, gate, up, down, tok, y, w_query, w_key, w_value, w_gate, w_up, gcol,
     o_query, o_key, o_value, o_out, o_gate, o_up, o_down, o_tok, o_y, o_g1, o_g2,
 ):
     n_ctx = qkv.shape[0]
@@ -1294,8 +1305,8 @@
         return jnp.sum(ref[...] * w[...].astype(f32), axis=-1, keepdims=True)
 
     first = total(o_query, w_query) + total(o_key, w_key) + total(o_value, w_value)
-    o_g1[...] = jnp.broadcast_to(first / g1[:, 0:1], o_g1.shape)
-    gain = g2[:, 0:1]
+    o_g1[...] = jnp.broadcast_to(first / gcol[:, 0:1], o_g1.shape)
+    gain = gcol[:, 4:5]
     for src, dst in ((gate, o_gate), (up, o_up)):
         for f in range(src.shape[2] // unit):
             for c in range(n_ctx):
@@ -1308,8 +1319,8 @@
     o_y[...] = y[...]
 
 
-def finish_stage(qkv, out, gate, up, down, tok, y, w_query, w_key, w_value, w_gate, w_up, g1, g2):
-    steps = 4
+def finish_stage(qkv, out, gate, up, down, tok, y, w_query, w_key, w_value, w_gate, w_up, gcol):
+    steps = 8
     n_fsdp = lax.axis_size("fsdp")
     own = w_query.shape[0]
     down = down.reshape(-1, down.shape[-1])
@@ -1318,9 +1329,11 @@
     def spec(shape):
         if len(shape) == 3:
             return pl.BlockSpec((shape[0], shape[1] // steps, shape[2]), lambda i: (0, i, 0))
+        if shape == down.shape:
+            return pl.BlockSpec((shape[0] // 2, shape[1] // (steps // 2)), lambda i: (i // (steps // 2), i % (steps // 2)))
         return pl.BlockSpec((shape[0] // steps, shape[1]), lambda i: (i, 0))
 
-    ins = (qkv, out, gate, up, down, tok, y, w_query, w_key, w_value, w_gate, w_up, g1, g2)
+    ins = (qkv, out, gate, up, down, tok, y, w_query, w_key, w_value, w_gate, w_up, gcol)
     outs = [
         (w_query.shape, f32), (w_key.shape, f32), (w_value.shape, f32), ((own, out.shape[0] * out.shape[2]), f32),
         (w_gate.shape, f32), (w_up.shape, f32), (down.shape, f32), (tok.shape, f32), (y.shape, bf16),
@@ -1368,7 +1381,7 @@
     return (index[None, :] <= index[:, None]) & (index[None, :] >= begin[:, None])
 
 
-def forward_plain(tok, tab, gains, gcol, w_query, w_key, w_value, w_out, w_gate, w_up):
+def forward_plain(tok, tab, w_query, w_key, w_value, w_out, w_gate, w_up):
     n_ctx, n_fsdp = lax.axis_size("ctx"), lax.axis_size("fsdp")
     c = lax.axis_index("ctx")
     own_rows = w_query.shape[0]
@@ -1386,11 +1399,12 @@
         axis=1,
     )
     wout_o = columns(w_out, c * cw, cw)
+    gcol = jnp.concatenate([tab[72:80, :own_rows].T, jnp.zeros((own_rows, 120), f32)], axis=1)
 
     def units(w):
         parts = w.reshape(own_rows, n_fsdp, n_ctx, unit)
         mine = lax.dynamic_index_in_dim(parts, c, axis=2, keepdims=False)
-        return (gcol[:, 0:1] * mine.reshape(own_rows, n_fsdp * unit)).astype(bf16)
+        return (gcol[:, 4:5] * mine.reshape(own_rows, n_fsdp * unit)).astype(bf16)
 
     wgate_o, wup_o = units(w_gate), units(w_up)
     x = gather(tok, "ctx")
@@ -1399,7 +1413,7 @@
     wout = gather(wout_o, "fsdp")
     wgate = gather(wgate_o, "fsdp")
     wup = gather(wup_o, "fsdp")
-    gain = gather(gains[0:1], "fsdp", axis=1).astype(f32)
+    gain = gather(tab[72:73, :own_rows].astype(bf16), "fsdp", axis=1).astype(f32)
     xf = x.astype(f32)
     r = lax.rsqrt(jnp.mean(xf * xf, axis=-1, keepdims=True) + eps_norm)
     xn = (xf * r * gain).astype(bf16)
@@ -1434,7 +1448,7 @@
     vt = v.reshape(seq, kvw).T
     r = jnp.broadcast_to(r, (seq, 128))
     grow = jnp.broadcast_to(gain, (8, width))
-    return xn, r, grow, qt, kt, vt, lse, o, m, wqkv, wout, wgate, wup, tabs
+    return xn, r, grow, gcol, qt, kt, vt, lse, o, m, wqkv, wout, wgate, wup, tabs
 
 
 def middle_plain(m, cot, wgate, wup, w_down):
@@ -1522,7 +1536,7 @@
     return grad_tokens, qkv_all, out_all, gate_all, up_all, down_all
 
 
-def finish_plain(qkv_all, out_all, gate_all, up_all, down_all, tok, y, w_query, w_key, w_value, w_gate, w_up, g1, g2):
+def finish_plain(qkv_all, out_all, gate_all, up_all, down_all, tok, y, w_query, w_key, w_value, w_gate, w_up, gcol):
     n_ctx, n_fsdp = lax.axis_size("ctx"), lax.axis_size("fsdp")
     own_rows = w_query.shape[0]
     qw = HEADS // n_ctx * HEAD_DIM
@@ -1555,7 +1569,7 @@
 
     first = gain_term(grad_query, w_query) + gain_term(grad_key, w_key) + gain_term(grad_value, w_value)
     second = gain_term(raw_gate, w_gate) + gain_term(raw_up, w_up)
-    g1, g2 = g1[:, 0:1], g2[:, 0:1]
+    g1, g2 = gcol[:, 0:1], gcol[:, 4:5]
     return (
         grad_query, grad_key, grad_value, grad_out, g2 * raw_gate, g2 * raw_up, grad_down, tok, y, first / g1, second,
     )
@@ -1578,21 +1592,28 @@
     kernels = lax.axis_size("ctx") == 4 and lax.axis_size("fsdp") == 8
     c = lax.axis_index("ctx")
     rows = tokens.shape[0]
-    own_rows = w_query.shape[0]
-    gains = jnp.broadcast_to(gain_attn[None, :], (16, own_rows))
-    gain_one = jnp.broadcast_to(gain_attn.astype(f32)[:, None], (own_rows, 128))
-    gain_two = jnp.broadcast_to(gain_mlp.astype(f32)[:, None], (own_rows, 128))
     frequency = theta_base ** (-(jnp.arange(HEAD_DIM // 2, dtype=f32) * 2.0) / HEAD_DIM)
     angles = frequency[:, None] * positions.astype(f32)[None, :]
     begin = c * rows + jnp.arange(rows, dtype=jnp.int32) - positions
+
+    def gain_rows(gain):
+        row = jnp.pad(gain.astype(f32), (0, rows - gain.shape[0]))
+        return jnp.broadcast_to(row[None, :], (4, rows))
+
     tab = jnp.concatenate(
-        [jnp.cos(angles), jnp.sin(angles), jnp.broadcast_to(begin.astype(f32)[None, :], (16, rows))],
+        [
+            jnp.cos(angles),
+            jnp.sin(angles),
+            jnp.broadcast_to(begin.astype(f32)[None, :], (8, rows)),
+            gain_rows(gain_attn),
+            gain_rows(gain_mlp),
+        ],
         axis=0,
     )
 
     forward = forward_stage if kernels else forward_plain
-    xn, r, grow, qt, kt, vt, lse, o, m, wqkv, wout, wgate, wup, tabs = forward(
-        tokens, tab, gains, gain_two, w_query, w_key, w_value, w_out, w_gate, w_up
+    xn, r, grow, gcol, qt, kt, vt, lse, o, m, wqkv, wout, wgate, wup, tabs = forward(
+        tokens, tab, w_query, w_key, w_value, w_out, w_gate, w_up
     )
     middle = middle_stage if kernels else middle_plain
     y, _, down_sum, gate_raw, up_raw, gm = middle(m, cotangent, wgate, wup, w_down)
@@ -1603,7 +1624,7 @@
     finish = finish_stage if kernels else finish_plain
     g_query, g_key, g_value, g_out, g_gate, g_up, g_down, tok, y, g_one, g_two = finish(
         qkv_all, out_all, gate_all, up_all, down_all, tok, y,
-        w_query, w_key, w_value, w_gate, w_up, gain_one, gain_two,
+        w_query, w_key, w_value, w_gate, w_up, gcol,
     )
     return (y, tok, g_one[:, 0], g_two[:, 0], g_query, g_key, g_value, g_out, g_gate, g_up, g_down)
 

time: 474 us -> 480 us (1.013)
  Pallas kernels: 459 us -> 466 us
where the time goes in v8:
time: 480 us; the launch traced here: 473 us
  Pallas kernels  466 us (97%)
  local copies, waits for them, and re-layouts  5.45 us (1%)
    pallas_call x3, Pallas kernels, call(): pl.pallas_call(kernel, out_shape=[jax.ShapeDtypeStruct(s, d) for s, d in...  446 us
    pallas_call x1, Pallas kernels, finish_stage(): pl.pallas_call(functools.partial(finish_kernel, unit), grid=(steps,), out...  20.2 us

profile of v8, /device:TPU:8, one launch (start us, length us, event | category | flops | bytes accessed | tf_op | source)
XLA Modules:
  0.0 473.3 jit_solution(9132474859955493142)
XLA Ops:
  0.7 0.8 subtract_convert_fusion
  1.4 0.7 broadcast_in_dim.7
  2.1 0.7 broadcast_in_dim.8
  2.7 0.2 multiply_sine_fusion
  2.9 2.4 concatenate.3.tab
  5.4 136.4 %forward_stage.1 = (bf16[1024,2048]{1,0:T(8,128)(2,1)}, f32[1024,128]{1,0:T(8,128)}, f32[8,2048]{1,0:T(8,128)}, f32[256,128]{1,0:T(8,128)}, bf16[512,1024]{1,0:T...) custom-call(bf16[256,2048]{1,0:T(8,128)(2,1)} %tok.1, ...), custom_call_target="tpu_custom_call" | custom-call | flops 9126805504 | bytes 67108864 | tf_op jit(solution)/shard_map/forward_stage/pallas_call | solution.py:258
  141.8 142.1 %middle_stage.1 = (bf16[256,2048]{1,0:T(8,128)(2,1)}, bf16[1408,2048]{1,0:T(8,128)(2,1)}, bf16[176,2048]{1,0:T(8,128)(2,1)}, bf16[2048,1408]{1,0:T(8,128)(2,1)},...) custom-call(bf16[1024,2048]{1,0:T(8,128)(2,1)} %get-tuple-element.56.m_in, bf16[256,2048]{1,0:T(8,128)(2,1)} %cot.1, ...), custom_call_target="tpu_custom_call" | custom-call | flops 53150220288 | bytes 67108864 | tf_op jit(solution)/shard_map/middle_stage/pallas_call | solution.py:258
  283.9 167.2 %backward_stage.1 = (f32[256,2048]{1,0:T(8,128)}, bf16[4,256,640]{2,1,0:T(8,128)(2,1)}, bf16[4,256,512]{2,1,0:T(8,128)(2,1)}, bf16[4,256,1408]{2,1,0:T(8,128)(2,...) custom-call(bf16[1024,2048]{1,0:T(8,128)(2,1)} %get-tuple-element.48.xn_in, ...), custom_call_target="tpu_custom_call" | custom-call | flops 20401094656 | bytes 67108864 | tf_op jit(solution)/shard_map/backward_stage/pallas_call | solution.py:258
  451.1 20.2 %finish_stage.1 = (f32[256,2048]{1,0:T(8,128)}, f32[256,256]{1,0:T(8,128)}, f32[256,256]{1,0:T(8,128)}, f32[256,2048]{1,0:T(8,128)}, f32[256,5632]{1,0:T(8,128)}...) custom-call(bf16[4,256,640]{2,1,0:T(8,128)(2,1)} %get-tuple-element., ...), custom_call_target="tpu_custom_call" | custom-call | tf_op jit(solution)/shard_map/finish_stage/pallas_call | solution.py:1342
  471.2 1.7 slice_reduce_fusion
  (2 shorter events, 0.0 us)

commit v9 on v7

--- a/solution.py
+++ b/solution.py
@@ -284,62 +284,57 @@
 
 
 class PlaneScatter:
-    SEMS = 8
+    SEMS = 12
 
     def __init__(self, place, part, half, first, second, sems):
         self.p, self.part, self.half = place, part, half
         self.first, self.second, self.sems = first, second, sems
 
-    def ref(self):
-        return self.part(self.p.c)
-
-    def far_to_y(self):
+    def far(self, h):
         p = self.p
-        return remote(self.half(p.cd, 0), self.first.at[0], self.sems.at[0], self.sems.at[2], p.y)
-
-    def far_to_x(self):
+        return remote(
+            self.half(p.cd, h), self.first.at[h], self.sems.at[h], self.sems.at[2 + h], p.x if h else p.y
+        )
+
+    def direct(self, to_y, h, base):
         p = self.p
-        return remote(self.half(p.cd, 1), self.first.at[1], self.sems.at[1], self.sems.at[3], p.x)
-
-    def to_x(self):
-        p = self.p
-        return remote(self.part(p.cx), self.second.at[0], self.sems.at[4], self.sems.at[6], p.x)
-
-    def to_y(self):
-        p = self.p
-        return remote(self.part(p.cy), self.second.at[1], self.sems.at[5], self.sems.at[7], p.y)
+        count = self.first.shape[1]
+        return remote(
+            self.half(p.cy if to_y else p.cx, h),
+            self.second.at[to_y, pl.ds(h * count, count)],
+            self.sems.at[base + to_y],
+            self.sems.at[base + 2 + to_y],
+            p.y if to_y else p.x,
+        )
 
     def start(self):
-        self.far_to_y().start()
-        self.far_to_x().start()
-
-    def got(self, ref, sem):
-        remote(ref, ref, self.sems.at[0], sem, self.p.x).wait_recv()
-
-    def add(self, ref, other):
-        add_to(ref, other)
+        self.far(0).start()
+        self.far(1).start()
+
+    def near(self):
+        self.direct(0, 1, 8).start()
+        self.direct(1, 0, 8).start()
 
     def middle(self):
         p = self.p
-        self.got(self.first.at[0], self.sems.at[2])
-        self.add(self.half(p.cx, 0), self.first.at[0])
-        self.to_x().start()
-        self.got(self.first.at[1], self.sems.at[3])
-        self.add(self.half(p.cy, 1), self.first.at[1])
-        self.to_y().start()
+        for to_y in (0, 1):
+            self.far(to_y).wait_recv()
+            add_to(self.half(p.cy if to_y else p.cx, to_y), self.first.at[to_y])
+            self.direct(to_y, to_y, 4).start()
 
     def finish(self, at=slice(None), first=True):
         if first:
-            self.got(self.second.at[0], self.sems.at[6])
-            self.got(self.second.at[1], self.sems.at[7])
+            for to_y in (0, 1):
+                self.direct(to_y, 1 - to_y, 8).wait_recv()
+                self.direct(to_y, to_y, 4).wait_recv()
         own = self.part(self.p.c)[at].astype(f32)
         return own + self.second[0, at].astype(f32) + self.second[1, at].astype(f32)
 
     def drain(self):
-        self.far_to_y().wait_send()
-        self.far_to_x().wait_send()
-        self.to_x().wait_send()
-        self.to_y().wait_send()
+        for to_y in (0, 1):
+            self.far(to_y).wait_send()
+            self.direct(to_y, 1 - to_y, 8).wait_send()
+            self.direct(to_y, to_y, 4).wait_send()
 
 
 class LineScatter:
@@ -833,6 +828,7 @@
     y_plane.start()
     partial_out(p.cx)
     partial_out(p.cy)
+    y_plane.near()
     sum_line.combine()
     sum_line.step(1)
     partial_out(p.c)
@@ -857,6 +853,7 @@
             e = dot_nt(GATE[at, :], WG[j : j + cw, :]) + dot_nt(UP[at, :], WU[j : j + cw, :])
             PH[at, j : j + cw] = (e - M[at, j : j + cw].astype(f32) * coef).astype(bf16)
         h_plane[b].start()
+        h_plane[b].near()
 
     back(0)
     y_plane.middle()
@@ -1066,6 +1063,7 @@
         for j in range(0, width, 512):
             PT[at, j : j + 512] = dot_nt(GM[at, :], WO[j : j + 512, :]).astype(bf16)
         g_plane[b].start()
+        g_plane[b].near()
     gate_line.combine()
     gate_line.step(1)
     g_plane[0].middle()
@@ -1170,7 +1168,7 @@
     t_plane.start()
     tokens(p.cx)
     tokens(p.cy)
-    t_plane.middle()
+    t_plane.near()
     tokens(p.c)
 
     @pl.loop(0, p.depth)
@@ -1180,6 +1178,7 @@
             O[rows_at(i, own_rows), j * nq : (j + 1) * nq] = dot_tn(XN[:, at], DPRE[...]).astype(bf16)
 
     qkv_line.start()
+    t_plane.middle()
     gate_line.step(3)
     down_plane.middle()
     out_line.combine()

time: 474 us -> 476 us (level)
  the two profiles are of different devices: /device:TPU:8 before, /device:TPU:1 now
where the time goes in v9:
time: 476 us; the launch traced here: 471 us
  Pallas kernels  464 us (97%)
  local copies, waits for them, and re-layouts  5.13 us (1%)
    pallas_call x3, Pallas kernels, call(): pl.pallas_call(kernel, out_shape=[jax.ShapeDtypeStruct(s, d) for s, d in...  447 us
    pallas_call x1, Pallas kernels, finish_stage(): pl.pallas_call(functools.partial(finish_kernel, unit), grid=(steps,), out...  16.7 us

profile of v9, /device:TPU:1, one launch (start us, length us, event | category | flops | bytes accessed | tf_op | source)
XLA Modules:
  0.0 471.5 jit_solution(705808483885070341)
XLA Ops:
  0.6 0.8 fusion
  1.4 0.2 multiply_cosine_fusion
  1.6 0.6 pad_maximum_fusion.tab
  2.3 1.4 broadcast_in_dim.10.gcol.g2
  3.7 1.3 broadcast_in_dim.9.gains
  5.0 142.0 %forward_stage.1 = (bf16[1024,2048]{1,0:T(8,128)(2,1)}, f32[1024,128]{1,0:T(8,128)}, f32[8,2048]{1,0:T(8,128)}, bf16[512,1024]{1,0:T(8,128)(2,1)}, bf16[64,1024]...) custom-call(bf16[256,2048]{1,0:T(8,128)(2,1)} %tok.1, ...), custom_call_target="tpu_custom_call" | custom-call | flops 9126805504 | bytes 67108864 | tf_op jit(solution)/shard_map/forward_stage/pallas_call | solution.py:258
  147.0 134.4 %middle_stage.1 = (bf16[256,2048]{1,0:T(8,128)(2,1)}, bf16[1408,2048]{1,0:T(8,128)(2,1)}, bf16[176,2048]{1,0:T(8,128)(2,1)}, bf16[2048,1408]{1,0:T(8,128)(2,1)},...) custom-call(bf16[1024,2048]{1,0:T(8,128)(2,1)} %get-tuple-element.55.m_in, bf16[256,2048]{1,0:T(8,128)(2,1)} %cot.1, ...), custom_call_target="tpu_custom_call" | custom-call | flops 53150220288 | bytes 67108864 | tf_op jit(solution)/shard_map/middle_stage/pallas_call | solution.py:258
  281.4 0.0 copy-start
  281.4 170.5 %backward_stage.1 = (f32[256,2048]{1,0:T(8,128)}, bf16[4,256,640]{2,1,0:T(8,128)(2,1)}, bf16[4,256,512]{2,1,0:T(8,128)(2,1)}, bf16[4,256,1408]{2,1,0:T(8,128)(2,...) custom-call(bf16[1024,2048]{1,0:T(8,128)(2,1)} %get-tuple-element.47.xn_in, ...), custom_call_target="tpu_custom_call" | custom-call | flops 20401094656 | bytes 67108864 | tf_op jit(solution)/shard_map/backward_stage/pallas_call | solution.py:258
  451.9 0.0 copy-done
  451.9 0.8 broadcast_in_dim.11.g1
  452.6 16.7 %finish_stage.1 = (f32[256,2048]{1,0:T(8,128)}, f32[256,256]{1,0:T(8,128)}, f32[256,256]{1,0:T(8,128)}, f32[256,2048]{1,0:T(8,128)}, f32[256,5632]{1,0:T(8,128)}...) custom-call(bf16[4,256,640]{2,1,0:T(8,128)(2,1)} %get-tuple-element., ...), custom_call_target="tpu_custom_call" | custom-call | tf_op jit(solution)/shard_map/finish_stage/pallas_call | solution.py:1328
  469.3 1.7 slice_reduce_fusion
  (2 shorter events, 0.0 us)
Async XLA Ops:
  281.4 170.5 %copy-start = (bf16[256]{0:T(256)(128)(2,1)S(1)}, bf16[256]{0:T(256)(128)(2,1)}, u32[]{:S(2)}) copy-start(bf16[256]{0:T(256)(128)(2,1)} %param.14) | copy-start | bytes 1540

commit v10 on v9

--- a/solution.py
+++ b/solution.py
@@ -795,6 +795,8 @@
     down_stage = [PH.at[pl.ds(i * rows, unit)] for i in range(2)]
     sum_line = LineScatter(p, down_block, DACC, DSLOT, sum_sems.at[0], down_stage)
     sum_line.start()
+    sum_line.combine()
+    sum_line.step(1)
     down_line.hop(3)
     down_line.finish()
 
@@ -829,8 +831,6 @@
     partial_out(p.cx)
     partial_out(p.cy)
     y_plane.near()
-    sum_line.combine()
-    sum_line.step(1)
     partial_out(p.c)
 
     def back(b):
@@ -858,10 +858,11 @@
     back(0)
     y_plane.middle()
     back(1)
+    sum_line.step(2)
     h_plane[0].middle()
-    sum_line.step(2)
     back(2)
     h_plane[1].middle()
+    sum_line.step(3)
     back(3)
     h_plane[2].middle()
 
@@ -890,7 +891,6 @@
 
     weight_tile(0)
     cot_plane.drain()
-    sum_line.step(3)
     h_plane[3].middle()
     weight_tile(1)
     weight_tile(2)
@@ -898,13 +898,13 @@
     weight_tile(3)
     weight_tile(4)
     finish_block(1)
+    sum_line.step(4)
+    sum_copy = pltpu.make_async_copy(sum_line.result(), down_sum, copy_sems.at[6])
+    sum_copy.start()
     weight_tile(5)
     weight_tile(6)
     finish_block(2)
     weight_tile(7)
-    sum_line.step(4)
-    sum_copy = pltpu.make_async_copy(sum_line.result(), down_sum, copy_sems.at[6])
-    sum_copy.start()
     piece = rows // n_ctx
     for i in range(n_ctx):
         own = pl.ds(pl.multiple_of(p.c * rows + i * piece, piece), piece)
@@ -1080,6 +1080,8 @@
     loads[8].start()
     up_line.step(1)
     g_plane[2].middle()
+    out_line.combine()
+    out_line.step(1)
     for i in (3, 4, 5, 6, 7, 10):
         loads[i].wait()
 
@@ -1170,6 +1172,7 @@
     tokens(p.cy)
     t_plane.near()
     tokens(p.c)
+    gate_line.step(3)
 
     @pl.loop(0, p.depth)
     def _(i):
@@ -1179,17 +1182,15 @@
 
     qkv_line.start()
     t_plane.middle()
-    gate_line.step(3)
     down_plane.middle()
-    out_line.combine()
-    out_line.step(1)
-    up_line.step(3)
+    out_line.step(2)
     qkv_line.combine()
     qkv_line.step(1)
+    up_line.step(3)
     gate_line.step(4)
     gate_plane.start()
     gate_own.start()
-    out_line.step(2)
+    out_line.step(3)
     tok_copies = []
     for i in range(n_ctx):
         if i >= 2:
@@ -1203,11 +1204,10 @@
     up_plane.start()
     up_own.start()
     gate_plane.middle()
-    out_line.step(3)
-    qkv_line.step(3)
     out_line.step(4)
     out_plane.start()
     out_own.start()
+    qkv_line.step(3)
     up_plane.middle()
     qkv_line.step(4)
     qkv_plane.start()

time: 476 us -> 479 us (level)
  the two profiles are of different devices: /device:TPU:1 before, /device:TPU:8 now
where the time goes in v10:
time: 479 us; the launch traced here: 474 us
  Pallas kernels  466 us (97%)
  local copies, waits for them, and re-layouts  5.13 us (1%)
    pallas_call x3, Pallas kernels, call(): pl.pallas_call(kernel, out_shape=[jax.ShapeDtypeStruct(s, d) for s, d in...  449 us
    pallas_call x1, Pallas kernels, finish_stage(): pl.pallas_call(functools.partial(finish_kernel, unit), grid=(steps,), out...  16.7 us

profile of v10, /device:TPU:8, one launch (start us, length us, event | category | flops | bytes accessed | tf_op | source)
XLA Modules:
  0.0 473.8 jit_solution(13282708533744365653)
XLA Ops:
  0.6 0.8 fusion
  1.4 0.2 multiply_cosine_fusion
  1.6 0.6 pad_maximum_fusion.tab
  2.3 1.4 broadcast_in_dim.10.gcol.g2
  3.7 1.3 broadcast_in_dim.9.gains
  5.0 136.4 %forward_stage.1 = (bf16[1024,2048]{1,0:T(8,128)(2,1)}, f32[1024,128]{1,0:T(8,128)}, f32[8,2048]{1,0:T(8,128)}, bf16[512,1024]{1,0:T(8,128)(2,1)}, bf16[64,1024]...) custom-call(bf16[256,2048]{1,0:T(8,128)(2,1)} %tok.1, ...), custom_call_target="tpu_custom_call" | custom-call | flops 9126805504 | bytes 67108864 | tf_op jit(solution)/shard_map/forward_stage/pallas_call | solution.py:258
  141.4 135.1 %middle_stage.1 = (bf16[256,2048]{1,0:T(8,128)(2,1)}, bf16[1408,2048]{1,0:T(8,128)(2,1)}, bf16[176,2048]{1,0:T(8,128)(2,1)}, bf16[2048,1408]{1,0:T(8,128)(2,1)},...) custom-call(bf16[1024,2048]{1,0:T(8,128)(2,1)} %get-tuple-element.55.m_in, bf16[256,2048]{1,0:T(8,128)(2,1)} %cot.1, ...), custom_call_target="tpu_custom_call" | custom-call | flops 53150220288 | bytes 67108864 | tf_op jit(solution)/shard_map/middle_stage/pallas_call | solution.py:258
  276.5 0.0 copy-start
  276.5 178.0 %backward_stage.1 = (f32[256,2048]{1,0:T(8,128)}, bf16[4,256,640]{2,1,0:T(8,128)(2,1)}, bf16[4,256,512]{2,1,0:T(8,128)(2,1)}, bf16[4,256,1408]{2,1,0:T(8,128)(2,...) custom-call(bf16[1024,2048]{1,0:T(8,128)(2,1)} %get-tuple-element.47.xn_in, ...), custom_call_target="tpu_custom_call" | custom-call | flops 20401094656 | bytes 67108864 | tf_op jit(solution)/shard_map/backward_stage/pallas_call | solution.py:258
  454.5 0.0 copy-done
  454.5 0.8 broadcast_in_dim.11.g1
  455.2 16.7 %finish_stage.1 = (f32[256,2048]{1,0:T(8,128)}, f32[256,256]{1,0:T(8,128)}, f32[256,256]{1,0:T(8,128)}, f32[256,2048]{1,0:T(8,128)}, f32[256,5632]{1,0:T(8,128)}...) custom-call(bf16[4,256,640]{2,1,0:T(8,128)(2,1)} %get-tuple-element., ...), custom_call_target="tpu_custom_call" | custom-call | tf_op jit(solution)/shard_map/finish_stage/pallas_call | solution.py:1328
  471.9 1.7 slice_reduce_fusion
  (2 shorter events, 0.0 us)
Async XLA Ops:
  276.5 178.0 %copy-start = (bf16[256]{0:T(256)(128)(2,1)S(1)}, bf16[256]{0:T(256)(128)(2,1)}, u32[]{:S(2)}) copy-start(bf16[256]{0:T(256)(128)(2,1)} %param.14) | copy-start | bytes 1540

commit v11 on v7

--- a/solution.py
+++ b/solution.py
@@ -771,7 +771,7 @@
             up = dot(M[at, :], WU[:, cols]) * r
             GATE[at, cols] = gate.astype(bf16)
             UP[at, cols] = up.astype(bf16)
-            HID[at, cols] = (gate * (1.0 / (1.0 + jnp.exp(-gate))) * up).astype(bf16)
+            HID[at, cols] = (gate * (0.5 + 0.5 * jnp.tanh(0.5 * gate)) * up).astype(bf16)
 
     pl.loop(0, 2)(activate)
     down_line.hop(1)
@@ -846,7 +846,7 @@
             grad_hidden = dot_nt(COT[at, :], WD[cols, :])
             gate = GATE[at, cols].astype(f32)
             up = UP[at, cols].astype(f32)
-            sig = 1.0 / (1.0 + jnp.exp(-gate))
+            sig = 0.5 + 0.5 * jnp.tanh(0.5 * gate)
             d_up = grad_hidden * gate * sig
             d_gate = grad_hidden * up * sig * (1.0 + gate * (1.0 - sig))
             stat += jnp.sum(d_gate * gate + d_up * up, axis=-1, keepdims=True)

time: 474 us -> 474 us (level)
  no operation moved by 1% of the time
where the time goes in v11:
time: 474 us; the launch traced here: 467 us
  Pallas kernels  459 us (97%)
  local copies, waits for them, and re-layouts  5.13 us (1%)
    pallas_call x3, Pallas kernels, call(): pl.pallas_call(kernel, out_shape=[jax.ShapeDtypeStruct(s, d) for s, d in...  442 us
    pallas_call x1, Pallas kernels, finish_stage(): pl.pallas_call(functools.partial(finish_kernel, unit), grid=(steps,), out...  16.7 us

profile of v11, /device:TPU:8, one launch (start us, length us, event | category | flops | bytes accessed | tf_op | source)
XLA Modules:
  0.0 467.0 jit_solution(1483671808978670789)
XLA Ops:
  0.6 0.8 fusion
  1.4 0.2 multiply_cosine_fusion
  1.6 0.6 pad_maximum_fusion.tab
  2.3 1.4 broadcast_in_dim.10.gcol.g2
  3.7 1.3 broadcast_in_dim.9.gains
  5.0 136.4 %forward_stage.1 = (bf16[1024,2048]{1,0:T(8,128)(2,1)}, f32[1024,128]{1,0:T(8,128)}, f32[8,2048]{1,0:T(8,128)}, bf16[512,1024]{1,0:T(8,128)(2,1)}, bf16[64,1024]...) custom-call(bf16[256,2048]{1,0:T(8,128)(2,1)} %tok.1, ...), custom_call_target="tpu_custom_call" | custom-call | flops 9126805504 | bytes 67108864 | tf_op jit(solution)/shard_map/forward_stage/pallas_call | solution.py:258
  141.4 130.4 %middle_stage.1 = (bf16[256,2048]{1,0:T(8,128)(2,1)}, bf16[1408,2048]{1,0:T(8,128)(2,1)}, bf16[176,2048]{1,0:T(8,128)(2,1)}, bf16[2048,1408]{1,0:T(8,128)(2,1)},...) custom-call(bf16[1024,2048]{1,0:T(8,128)(2,1)} %get-tuple-element.55.m_in, bf16[256,2048]{1,0:T(8,128)(2,1)} %cot.1, ...), custom_call_target="tpu_custom_call" | custom-call | flops 53150220288 | bytes 67108864 | tf_op jit(solution)/shard_map/middle_stage/pallas_call | solution.py:258
  271.7 0.0 copy-start
  271.7 175.6 %backward_stage.1 = (f32[256,2048]{1,0:T(8,128)}, bf16[4,256,640]{2,1,0:T(8,128)(2,1)}, bf16[4,256,512]{2,1,0:T(8,128)(2,1)}, bf16[4,256,1408]{2,1,0:T(8,128)(2,...) custom-call(bf16[1024,2048]{1,0:T(8,128)(2,1)} %get-tuple-element.47.xn_in, ...), custom_call_target="tpu_custom_call" | custom-call | flops 20401094656 | bytes 67108864 | tf_op jit(solution)/shard_map/backward_stage/pallas_call | solution.py:258
  447.3 0.0 copy-done
  447.4 0.8 broadcast_in_dim.11.g1
  448.1 16.7 %finish_stage.1 = (f32[256,2048]{1,0:T(8,128)}, f32[256,256]{1,0:T(8,128)}, f32[256,256]{1,0:T(8,128)}, f32[256,2048]{1,0:T(8,128)}, f32[256,5632]{1,0:T(8,128)}...) custom-call(bf16[4,256,640]{2,1,0:T(8,128)(2,1)} %get-tuple-element., ...), custom_call_target="tpu_custom_call" | custom-call | tf_op jit(solution)/shard_map/finish_stage/pallas_call | solution.py:1329
  464.8 1.7 slice_reduce_fusion
  (2 shorter events, 0.0 us)
Async XLA Ops:
  271.7 175.6 %copy-start = (bf16[256]{0:T(256)(128)(2,1)S(1)}, bf16[256]{0:T(256)(128)(2,1)}, u32[]{:S(2)}) copy-start(bf16[256]{0:T(256)(128)(2,1)} %param.14) | copy-start | bytes 1540
